TPU v7x, 128 devices: a whole 4x4x4 slice. The times are simulated.
128 devices in a mesh: dp: 64 (over x_lo, z, y, core), tensor: 2 (over x_hi).
Axes of the slice: x: 4 (x_hi: 2, x_lo: 2; x = x_hi * 2 + x_lo), y: 4, z: 4, core: 2. Of those that a mesh axis runs over, the one named last changes fastest.
Arguments:
- tokens: bfloat16 [65536, 1024], P('dp'), may hold values from -6 to 6
- norm_gain: float32 [1024], replicated, may hold values from 0.5 to 1.5
- norm_shift: float32 [1024], replicated, may hold values from -4 to 4
- qkv_weight: bfloat16 [1024, 3, 1024], P(None, None, 'tensor'), may hold values from -0.25 to 0.25
- merge_weight: bfloat16 [1024, 1024], P('tensor'), may hold values from -0.5 to 0.5
- up_weight: bfloat16 [1024, 4096], P(None, 'tensor'), may hold values from -0.1875 to 0.1875
- inner_shift: float32 [4096], P('tensor'), may hold values from -6 to 6
- down_weight: bfloat16 [4096, 1024], P('tensor'), may hold values from -0.09375 to 0.09375
- outer_shift: float32 [1024], replicated, may hold values from -6 to 6
- cotangent: bfloat16 [65536, 1024], P('dp'), may hold values from -6 to 6
Outputs:
- block_out: bfloat16 [65536, 1024], P('dp')
- token_grad: bfloat16 [65536, 1024], P('dp')
- gain_grad: float32 [1024], replicated
- shift_grad: float32 [1024], replicated
- qkv_grad: float32 [1024, 3, 1024], P(None, None, 'tensor')
- merge_grad: float32 [1024, 1024], P('tensor')
- up_grad: float32 [1024, 4096], P(None, 'tensor')
- inner_grad: float32 [4096], P('tensor')
- down_grad: float32 [4096, 1024], P('tensor')
- outer_grad: float32 [1024], replicated
All inputs are finite; a program needn't handle non-finite values.
Results may differ from a plain program's by a relative error of at most 0.0065.
The roundings to bfloat16 on the way count: a program that leaves them out, or rounds other values in their place, can miss the bound.
Values sent between devices are 32-bit elements; how exact they have to be, the bound alone decides.
No kernel may reach another device: no remote copies, remote signals or barrier semaphores. Data moves between devices by JAX's collectives and lax.ppermute only.
A program may use at most 256 MiB of HBM per device.

v0:
```python
import functools

import jax
import jax.numpy as jnp
import numpy as np
from jax import lax
from jax.experimental import pallas as pl
from jax.experimental.pallas import tpu as pltpu
from jax.sharding import Mesh
from jax.sharding import PartitionSpec as P

F32 = jnp.float32
BF16 = jnp.bfloat16
HEAD = 64
ROT = 32
PAIR = 2 * HEAD
epsilon = 1e-05


def nn(a, b):
    return jnp.dot(a, b, preferred_element_type=F32)


def nt(a, b):
    return lax.dot_general(a, b, (((1,), (1,)), ((), ())), preferred_element_type=F32)


def tn(a, b):
    return lax.dot_general(a, b, (((0,), (0,)), ((), ())), preferred_element_type=F32)


def rotary_tables(length):
    half = ROT // 2
    rates = np.float32(10000.0) ** (-np.arange(half, dtype=np.float32) / np.float32(half))
    angles = np.arange(length, dtype=np.float32)[:, None] * rates[None, :].astype(np.float32)
    angles = np.repeat(angles, 2, axis=1)
    sign = np.where(np.arange(ROT) % 2 == 0, -1.0, 1.0)
    rest = np.ones((length, HEAD - ROT))
    cosine = np.concatenate([np.cos(angles), rest], axis=1)
    sine = np.concatenate([np.sin(angles) * sign, 0 * rest], axis=1)
    return tuple(jnp.asarray(np.tile(x, (1, 2)).astype(np.float32)) for x in (cosine, sine))


def swap_pairs(x):
    lane = lax.broadcasted_iota(jnp.int32, x.shape, 1)
    return jnp.where(lane % 2 == 0, pltpu.roll(x, PAIR - 1, 1), pltpu.roll(x, 1, 1))


def launch(kernel, name, grid, scalars, after, ins, outs, scratch=(), vmem=16, flops=0, into=None):
    if into is not None:
        after = (*after, into)
    first, skipped = len(scalars), len(after)

    def without(*refs):
        kernel(*refs[:first], *refs[first + skipped :])

    got = pl.pallas_call(
        without,
        grid_spec=pltpu.PrefetchScalarGridSpec(
            num_scalar_prefetch=first,
            grid=grid,
            in_specs=[pl.BlockSpec(memory_space=pltpu.HBM)] * skipped + [spec for _, spec in ins],
            out_specs=[spec for _, _, spec in outs],
            scratch_shapes=list(scratch),
        ),
        out_shape=[jax.ShapeDtypeStruct(shape, dtype) for shape, dtype, _ in outs],
        compiler_params=pltpu.CompilerParams(vmem_limit_bytes=vmem << 20),
        input_output_aliases={} if into is None else {first + skipped - 1: 0},
        cost_estimate=pl.CostEstimate(
            flops=flops,
            bytes_accessed=sum(x.size * x.dtype.itemsize for x, _ in ins)
            + sum(int(np.prod(shape)) * jnp.dtype(dtype).itemsize for shape, dtype, _ in outs),
            transcendentals=0,
        ),
        name=name,
    )(*scalars, *after, *[array for array, _ in ins])
    return got


def whole(*shape):
    return pl.BlockSpec(shape, lambda *_: (0,) * len(shape))


def once(*shape):
    return pl.BlockSpec(shape, lambda *_: (0,) * len(shape), pipeline_mode=pl.Buffered(1))


gelu_rate = float(np.sqrt(2 / np.pi))
ROOM = 64


def norm_rows(x):
    centred = x - jnp.mean(x, axis=1, keepdims=True)
    inverse = lax.rsqrt(jnp.mean(centred * centred, axis=1, keepdims=True) + epsilon)
    return centred * inverse, inverse


def project_kernel(
    tok, gain, shift, w_in, mw_in, cot, cos, sin, normed, normed_t, q, k, v, dh, outer, w, mw, sems
):
    first = pl.program_id(0) == 0
    copies = [pltpu.make_async_copy(mw_in, mw, sems.at[0])] + [
        pltpu.make_async_copy(w_in.at[which], w.at[which], sems.at[1 + which]) for which in range(3)
    ]

    @pl.when(first)
    def _():
        for copy in copies:
            copy.start()

    def body(arriving):
        unit, _ = norm_rows(tok[...].astype(F32))
        n = (unit * gain[...] + shift[...]).astype(BF16)
        normed[...] = n
        normed_t[...] = n.T
        total = jnp.sum(cot[...].astype(F32), axis=0, keepdims=True)
        outer[...] = total if arriving else outer[...] + total
        if arriving:
            copies[0].wait()
        dh[...] = nt(cot[...], mw[...]).astype(BF16)
        c = cos[...]
        s = sin[...]
        for which, ref in enumerate((q, k, v)):
            if arriving:
                copies[1 + which].wait()
            joined = nn(n, w[which])
            if which == 2:
                ref[...] = joined.astype(BF16)
                continue
            for p in range(joined.shape[1] // PAIR):
                block = joined[:, p * PAIR : (p + 1) * PAIR]
                turned = (block * c + swap_pairs(block) * s).astype(BF16)
                if which == 0:
                    turned = turned * jnp.asarray(HEAD**-0.5, BF16)
                ref[:, p * PAIR : (p + 1) * PAIR] = turned

    @pl.when(first)
    def _():
        body(True)

    @pl.when(jnp.logical_not(first))
    def _():
        body(False)


def project(tok, gain, shift, w3, mw, cot, cos, sin, rows=256):
    length, width = tok.shape
    local = mw.shape[0]

    def row_block(n):
        return pl.BlockSpec((rows, n), lambda i: (i, 0))

    def out(n):
        return ((length, n), BF16, row_block(n))

    return launch(
        project_kernel,
        "project",
        (length // rows,),
        (),
        (),
        [
            (tok, row_block(width)),
            (gain, whole(1, width)),
            (shift, whole(1, width)),
            (w3, pl.BlockSpec(memory_space=pltpu.HBM)),
            (mw, pl.BlockSpec(memory_space=pltpu.HBM)),
            (cot, row_block(width)),
            (cos, row_block(PAIR)),
            (sin, row_block(PAIR)),
        ],
        [out(width), ((width, length), BF16, pl.BlockSpec((width, rows), lambda i: (0, i)))]
        + [out(local)] * 4
        + [((1, width), F32, whole(1, width))],
        [
            pltpu.VMEM((3, width, local), BF16),
            pltpu.VMEM((local, width), BF16),
            pltpu.SemaphoreType.DMA((4,)),
        ],
        vmem=60,
        flops=8 * length * width * local,
    )


def hidden_kernel(normed, cot, up_in, shift, down_in, out, dn, act, dpre, ig, up, down, sems, *, cols):
    first = pl.program_id(0) == 0
    cuts = [slice(j, j + cols) for j in range(0, up.shape[1], cols)]
    copies = []
    for j, s in enumerate(cuts):
        copies.append(
            (
                pltpu.make_async_copy(up_in.at[:, s], up.at[:, s], sems.at[2 * j]),
                pltpu.make_async_copy(down_in.at[s, :], down.at[s, :], sems.at[2 * j + 1]),
            )
        )

    @pl.when(first)
    def _():
        for pair in copies:
            for copy in pair:
                copy.start()

    def body(arriving):
        n = normed[...]
        c = cot[...]
        sums = []
        for j, s in enumerate(cuts):
            if arriving:
                for copy in copies[j]:
                    copy.wait()
            v = nn(n, up[:, s]) + shift[:, s]
            da = nt(c, down[s, :])
            square = v * v
            t = jnp.tanh(gelu_rate * v * (1.0 + 0.044715 * square))
            h = 0.5 * (1.0 + t)
            act[:, s] = (v * h).astype(BF16)
            slope = h + (0.5 * gelu_rate) * v * (1.0 - t * t) * (1.0 + (3 * 0.044715) * square)
            d_pre = (da * slope).astype(BF16)
            dpre[:, s] = d_pre
            sums.append(jnp.sum(d_pre.astype(F32), axis=0, keepdims=True))
        sums = jnp.concatenate(sums, axis=1)
        ig[...] = sums if arriving else ig[...] + sums
        out[...] = nn(act[...], down[...])
        dn[...] = nt(dpre[...], up[...])

    @pl.when(first)
    def _():
        body(True)

    @pl.when(jnp.logical_not(first))
    def _():
        body(False)


def hidden_pass(after, normed, cot, up, shift, down, rows=256, cols=512):
    length, width = normed.shape
    hidden = up.shape[1]

    def here(n):
        return pl.BlockSpec((rows, n), lambda i: (i, 0))

    return launch(
        functools.partial(hidden_kernel, cols=cols),
        "hidden",
        (length // rows,),
        (),
        after,
        [
            (normed, here(width)),
            (cot, here(width)),
            (up, pl.BlockSpec(memory_space=pltpu.HBM)),
            (shift, whole(1, hidden)),
            (down, pl.BlockSpec(memory_space=pltpu.HBM)),
        ],
        [((length, width), F32, here(width))] * 2
        + [((length, hidden), BF16, here(hidden))] * 2
        + [((1, hidden), F32, whole(1, hidden))],
        [
            pltpu.VMEM((width, hidden), BF16),
            pltpu.VMEM((hidden, width), BF16),
            pltpu.SemaphoreType.DMA((2 * hidden // cols,)),
        ],
        vmem=60,
        flops=9 * length * width * hidden,
    )


def grad_kernel(place, lhs, rhs, *rest, base, product, own):
    if own:
        got, keep, send, buf, sems, land, land_sems = rest
    else:
        out, buf, sems = rest
    j = pl.program_id(0)
    size = buf.shape[1] // 8

    def arriving(n):
        return pltpu.make_async_copy(
            got.at[place[base + n]], land.at[pl.ds(n * size, size)], land_sems.at[n]
        )

    if own:

        @pl.when(j == 0)
        def _():
            for n in range(16):
                arriving(n).start()

    buf[j] = product(lhs[...], rhs[...])
    if own:

        @pl.when(j == 0)
        def _():
            for n in range(8):
                arriving(n).wait()

        @pl.when(j == 1)
        def _():
            for n in range(8, 16):
                arriving(n).wait()

        buf[j] += land[pl.ds(pl.multiple_of(j * 8 * size, size), 8 * size), :]

    for i in range(8):
        spot = place[base + j * 8 + i]
        block = buf.at[j, pl.ds(i * size, size)]
        sem = sems.at[j * 8 + i]
        if own:

            @pl.when(spot < 8)
            def _():
                pltpu.make_async_copy(block, keep.at[spot], sem).start()

            @pl.when(spot >= 8)
            def _():
                pltpu.make_async_copy(block, send.at[spot - 8], sem).start()

        else:
            pltpu.make_async_copy(block, out.at[spot], sem).start()

    @pl.when(j == 1)
    def _():
        for n in range(16):
            block = buf.at[n // 8, pl.ds((n % 8) * size, size)]
            pltpu.make_async_copy(block, (keep if own else out).at[0], sems.at[n]).wait()


def grad(place, base, spots, after, lhs, rhs, specs, product, got=None):
    width = 1024
    rows = 1024
    own = got is not None
    piece = rows // 16
    anywhere = pl.BlockSpec(memory_space=pltpu.HBM)
    scratch = [pltpu.VMEM((2, rows // 2, width), F32), pltpu.SemaphoreType.DMA((16,))]
    if own:
        scratch += [pltpu.VMEM((rows, width), F32), pltpu.SemaphoreType.DMA((16,))]
    outs = [((8 if own else 16, piece, width), F32, anywhere)] * (2 if own else 1)
    return launch(
        functools.partial(grad_kernel, base=spots, product=product, own=own),
        "grad",
        (2,),
        (place,),
        after,
        [(lhs, specs[0]), (rhs, specs[1])] + ([(got, anywhere)] if own else []),
        outs,
        scratch,
        vmem=24,
        flops=2 * rows * width * lhs.shape[0],
    )


def down_grad(place, base, after, active, cot, got=None):
    length, width = cot.shape
    block = pl.BlockSpec((length, 512), lambda j, place: (0, place[base] * 2 + j))
    return grad(
        place, base, base + 1, after, active, cot, (block, once(length, width)), tn, got
    )


def up_grad(place, base, after, normed_t, d_pre, got=None):
    width, length = normed_t.shape
    rows = pl.BlockSpec((512, length), lambda j, _: (j, 0))
    half = pl.BlockSpec(
        (length, 1024), lambda j, place: (0, place[base]), pipeline_mode=pl.Buffered(1)
    )
    return grad(place, base, base + 17, after, normed_t, d_pre, (rows, half), nn, got)


def attend_kernel(*refs, last, sub):
    if last:
        q, do, k, v, dk_in, dv_in, cos, sin, ho, dq, dk, dv, dk_sum, dv_sum = refs
    else:
        q, do, k, v, cos, sin, ho, dq, dk_sum, dv_sum = refs
    block = q.shape[0]
    seen = k.shape[0]
    low = lax.broadcasted_iota(jnp.int32, (sub, PAIR), 1) < HEAD
    zero = jnp.zeros((sub, PAIR), BF16)
    causal = lax.broadcasted_iota(jnp.int32, (sub, sub), 1) <= lax.broadcasted_iota(
        jnp.int32, (sub, sub), 0
    )
    for i in range(block // sub):
        before = seen - block + i * sub
        upto = before + sub
        rows = slice(i * sub, (i + 1) * sub)
        keys = k[0:upto, :]
        values = v[0:upto, :]
        heads = [
            [jnp.where(low, x[rows, :], zero), jnp.where(low, zero, x[rows, :])] for x in (q, do)
        ]
        scores = [nt(x, keys) for x in heads[0]]
        d_probs = [nt(x, values) for x in heads[1]]
        probs_low, d_scores = [], []
        for h in range(2):
            edge = jnp.where(causal, scores[h][:, before:], -1e30)
            if before:
                edge = jnp.concatenate([scores[h][:, :before], edge], axis=1)
            expo = jnp.exp(edge - jnp.max(edge, axis=1, keepdims=True))
            probs = expo * (1.0 / jnp.sum(expo, axis=1, keepdims=True))
            inner = jnp.sum(probs * d_probs[h], axis=1, keepdims=True)
            probs_low.append(probs.astype(BF16))
            d_scores.append((probs * (d_probs[h] - inner)).astype(BF16))
        mixed = [nn(x, values) for x in probs_low]
        ho[rows, :] = jnp.where(low, mixed[0], mixed[1]).astype(BF16)
        d_query = [nn(x, keys) for x in d_scores]
        d_query = jnp.where(low, d_query[0], d_query[1]) * HEAD**-0.5
        turn = slice(before, upto)
        dq[rows, :] = (
            d_query * cos[turn, :] - swap_pairs(d_query) * sin[turn, :]
        ).astype(BF16)
        for left, right, total in ((probs_low, heads[1], dv_sum), (d_scores, heads[0], dk_sum)):
            add = tn(left[0], right[0]) + tn(left[1], right[1])
            if i == 0:
                total[0:upto, :] = add
            else:
                total[0:before, :] += add[:before]
                total[before:upto, :] = add[before:]
    if last:
        before = seen - block
        dk_sum[0:before, :] += dk_in[...]
        dv_sum[0:before, :] += dv_in[...]
        for i in range(seen // block):
            rows = slice(i * block, (i + 1) * block)
            d_keys = dk_sum[rows, :]
            dk[rows, :] = (d_keys * cos[rows, :] - swap_pairs(d_keys) * sin[rows, :]).astype(BF16)
            dv[rows, :] = dv_sum[rows, :].astype(BF16)


def attend(part, after, q, k, v, do, cos, sin, carried=(), sub=256):
    length, local = q.shape
    half = length // 2
    seen = half * (part + 1)
    rows = pl.BlockSpec((half, PAIR), lambda p: (part, p))
    keys = pl.BlockSpec((seen, PAIR), lambda p: (0, p))
    table = pl.BlockSpec((seen, PAIR), lambda p: (0, 0))
    here = pl.BlockSpec((half, PAIR), lambda p: (0, p))
    outs = [((half, local), BF16, here)] * 2
    scratch = ()
    if part == 0:
        outs += [((half, local), F32, here)] * 2
    else:
        outs += [((length, local), BF16, keys)] * 2
        scratch = [pltpu.VMEM((length, PAIR), F32)] * 2
    return launch(
        functools.partial(attend_kernel, last=part == 1, sub=sub),
        "attend",
        (local // PAIR,),
        (),
        after,
        [(q, rows), (do, rows), (k, keys), (v, keys)]
        + [(x, here) for x in carried]
        + [(cos, table), (sin, table)],
        outs,
        scratch,
        flops=30 * half * seen * PAIR * local // PAIR,
    )


def forward_kernel(ho, mw, a, *pieces, cuts):
    i = pl.program_id(0)
    total = nn(ho[...], mw[...]) + a[...]
    for n, piece in enumerate(pieces):

        @pl.when(jnp.logical_and(i >= cuts[n], i < cuts[n + 1]))
        def _():
            piece[...] = total


def within(first, last):
    return lambda i, *_: (jnp.clip(i, first, last - 1) - first, 0)


def cut_specs(sizes, rows, width):
    cuts = [int(n) // rows for n in np.cumsum((0,) + tuple(sizes))]
    return cuts, [
        pl.BlockSpec((rows, width), within(cuts[k], cuts[k + 1])) for k in range(len(sizes))
    ]


def forward_part(part, after, ho, mw, a, sizes, rows=128):
    half, local = ho.shape
    width = mw.shape[1]
    steps = half // rows
    cuts, specs = cut_specs(sizes, rows, width)
    there = pl.BlockSpec((rows, width), lambda i: (part * steps + i, 0))
    return launch(
        functools.partial(forward_kernel, cuts=cuts),
        "forward",
        (steps,),
        (),
        after,
        [
            (ho, pl.BlockSpec((rows, local), lambda i: (i, 0))),
            (mw, once(local, width)),
            (a, there),
        ],
        [((n, width), F32, spec) for n, spec in zip(sizes, specs)],
        flops=2 * half * width * local,
    )


def backward_kernel(dq0, dq1, dk, dv, w, a, tok, out, sums):
    i = pl.program_id(0)

    def one(dq):
        total = nt(dq[...], w[0]) + nt(dk[...], w[1]) + nt(dv[...], w[2]) + a[...]
        out[...] = total
        unit, _ = norm_rows(tok[...].astype(F32))
        both = jnp.concatenate(
            [jnp.sum(total * unit, axis=0, keepdims=True), jnp.sum(total, axis=0, keepdims=True)],
            axis=0,
        )

        @pl.when(i == 0)
        def _():
            sums[...] = both

        @pl.when(i > 0)
        def _():
            sums[...] += both

    half = pl.num_programs(0) // 2

    @pl.when(i < half)
    def _():
        one(dq0)

    @pl.when(i >= half)
    def _():
        one(dq1)


def backward_pass(after, dq0, dq1, dk, dv, w3, a, tok, rows=256):
    length, local = dk.shape
    width = w3.shape[1]
    steps = length // rows
    here = pl.BlockSpec((rows, width), lambda i: (i, 0))
    narrow = pl.BlockSpec((rows, local), lambda i: (i, 0))
    return launch(
        backward_kernel,
        "backward",
        (steps,),
        (),
        after,
        [
            (dq0, pl.BlockSpec((rows, local), within(0, steps // 2))),
            (dq1, pl.BlockSpec((rows, local), within(steps // 2, steps))),
            (dk, narrow),
            (dv, narrow),
            (w3, once(3, width, local)),
            (a, here),
            (tok, here),
        ],
        [((length, width), F32, here), ((2, width), F32, whole(2, width))],
        vmem=60,
        flops=6 * length * width * local,
    )


def hand_kernel(x, *pieces, cuts):
    i = pl.program_id(0)
    for n, piece in enumerate(pieces):

        @pl.when(jnp.logical_and(i >= cuts[n], i < cuts[n + 1]))
        def _():
            piece[...] = x[...]


def hand(after, x, start, sizes, rows=128):
    width = x.shape[1]
    first = start // rows
    cuts, specs = cut_specs(sizes, rows, width)
    return launch(
        functools.partial(hand_kernel, cuts=cuts),
        "hand",
        (cuts[-1],),
        (),
        after,
        [(x, pl.BlockSpec((rows, width), lambda i: (first + i, 0)))],
        [((size, width), F32, spec) for size, spec in zip(sizes, specs)],
    )


def hand_all_kernel(*refs):
    half = len(refs) // 2
    for x, out in zip(refs[:half], refs[half:]):
        out[...] = x[...]


def hand_all(after, *arrays):
    return launch(
        hand_all_kernel,
        "hand_all",
        (1,),
        (),
        after,
        [(x, once(*x.shape)) for x in arrays],
        [(x.shape, F32, once(*x.shape)) for x in arrays],
    )


def tail_kernel(place, normed_t, ho0, ho1, cot, dq0, dq1, dk, dv, own0, own1, other0, other1):
    n = normed_t[...]
    width = n.shape[0]
    half = dq0.shape[0]
    first = place[0] == 0

    def put(mine, x, roomy):
        def store(ref):
            if not roomy:
                ref[...] = x
                return
            rows = width // 2
            blank = jnp.zeros((ROOM, x.shape[1]), F32)
            for k in range(2):
                start = k * (rows + ROOM)
                ref[start : start + rows, :] = x[k * rows : (k + 1) * rows]
                ref[start + rows : start + rows + ROOM, :] = blank

        @pl.when(mine)
        def _():
            store(own1 if roomy else own0)

        @pl.when(jnp.logical_not(mine))
        def _():
            store(other1 if roomy else other0)

    put(first, nn(n[:, :half], dq0[...]) + nn(n[:, half:], dq1[...]), False)
    put(first, nn(n, dk[...]), True)
    put(jnp.logical_not(first), nn(n, dv[...]), False)
    g = tn(ho0[...], cot[:half, :]) + tn(ho1[...], cot[half:, :])
    columns = g.shape[1] // 2
    put(jnp.logical_not(first), jnp.concatenate([g[:, :columns], g[:, columns:]], axis=0), True)


def tail(place, after, normed_t, ho0, ho1, cot, dq0, dq1, dk, dv):
    width, length = normed_t.shape
    local = dk.shape[1]
    half = length // 2
    assert 2 * local == width
    shapes = [(width, local), (width + 2 * ROOM, local)] * 2
    return launch(
        tail_kernel,
        "tail",
        (1,),
        (place,),
        after,
        [(normed_t, once(width, length))]
        + [(x, once(half, local)) for x in (ho0, ho1)]
        + [(cot, once(length, width))]
        + [(x, once(half, local)) for x in (dq0, dq1)]
        + [(x, once(length, local)) for x in (dk, dv)],
        [(shape, F32, once(*shape)) for shape in shapes],
        vmem=36,
        flops=8 * length * width * local,
    )


def halve_small_kernel(place, own, got, sums, outer, inner, keep, send, *, slot):
    h, width = keep.shape
    bit = place[slot]
    stay = pl.ds(pl.multiple_of(bit * h, ROOM), h)
    go = pl.ds(pl.multiple_of((1 - bit) * h, ROOM), h)
    keep[...] = own[stay, :] + got[stay, :]
    send[...] = own[go, :] + got[go, :]
    rows = [x[i : i + 1, j : j + width] for x in (sums, outer, inner) for i in range(x.shape[0]) for j in range(0, x.shape[1], width)]

    def put(ref):
        for i, row in enumerate(rows):
            ref[h - ROOM + i : h - ROOM + i + 1, :] += row

    @pl.when(bit == 0)
    def _():
        put(keep)

    @pl.when(bit == 1)
    def _():
        put(send)


def halve_small(place, slot, after, own, got, *small):
    n, width = own.shape
    return launch(
        functools.partial(halve_small_kernel, slot=slot),
        "halve_small",
        (1,),
        (place,),
        after,
        [(x, once(*x.shape)) for x in (own, got, *small)],
        [((n // 2, width), F32, once(n // 2, width))] * 2,
    )


def finish_kernel(*refs, cuts, last):
    n = len(cuts) - 1
    wide, (mine, got), (row, out) = refs[: -2 * n - 2], (refs[-2 * n - 2 : -n - 2], refs[-n - 2 : -2]), refs[-2:]
    i = pl.program_id(0)
    x = wide[0][...].astype(F32)

    def one(total):
        if not last:
            out[...] = (x + total + row[...]).astype(BF16)
            return
        unit, inverse = norm_rows(x)
        d_unit = total * row[...]
        centre = jnp.mean(d_unit, axis=1, keepdims=True)
        slope = jnp.mean(d_unit * unit, axis=1, keepdims=True)
        out[...] = (
            wide[1][...].astype(F32) + inverse * (d_unit - centre - unit * slope)
        ).astype(BF16)

    for k in range(n):

        @pl.when(jnp.logical_and(i >= cuts[k], i < cuts[k + 1]))
        def _():
            one(mine[k][...] + got[k][...])


def finish(name, after, wide, mine, got, row, start=0, into=None, rows=128, vmem=16):
    length, width = wide[0].shape
    cuts, pieces = cut_specs([x.shape[0] for x in mine], rows, width)
    first = start // rows
    here = pl.BlockSpec((rows, width), lambda i: (first + i, 0))
    return launch(
        functools.partial(finish_kernel, cuts=cuts, last=len(wide) > 1),
        name,
        (cuts[-1],),
        (),
        after,
        [(x, here) for x in wide]
        + list(zip(mine, pieces))
        + list(zip(got, pieces))
        + [(row, whole(1, width))],
        [((length, width), BF16, here)],
        vmem=vmem,
        into=into,
    )[0]


def halve_kernel(place, a, b, c, d, keep, send):
    keep[...] = a[...] + b[...]
    send[...] = c[...] + d[...]


def halve(place, slot, after, mine, got):
    n, width = mine.shape
    h = n // 2
    rows = h // 2 if h * width > (256 << 10) else h
    steps = h // rows

    def bit(place):
        return 0 if slot is None else place[slot]

    keep = pl.BlockSpec((rows, width), lambda i, place: (bit(place) * steps + i, 0))
    send = pl.BlockSpec((rows, width), lambda i, place: ((1 - bit(place)) * steps + i, 0))
    here = pl.BlockSpec((rows, width), lambda i, _: (i, 0))
    return launch(
        halve_kernel,
        "halve",
        (steps,),
        (place,),
        after,
        [(mine, keep), (got, keep), (mine, send), (got, send)],
        [((h, width), F32, here)] * 2,
    )


def pack_kernel(a, b, c, d, out):
    n = a.shape[0]
    out[:n, :] = a[...] + b[...]
    out[n:, :] = c[...] + d[...]


def pack(after, a, b, c, d):
    shape = (a.shape[0] + c.shape[0], a.shape[1])
    return launch(
        pack_kernel,
        "pack",
        (1,),
        (),
        after,
        [(x, whole(*x.shape)) for x in (a, b, c, d)],
        [(shape, F32, whole(*shape))],
    )[0]


def plus_kernel(a, b, out):
    out[...] = a[...] + b[...]


def plus(after, a, b):
    return launch(
        plus_kernel,
        "plus",
        (1,),
        (),
        after,
        [(x, whole(*x.shape)) for x in (a, b)],
        [(a.shape, F32, whole(*a.shape))],
    )[0]


def part_kernel(a, b, first, second):
    n = first.shape[0]
    first[...] = a[:n, :] + b[:n, :]
    second[...] = a[n:, :] + b[n:, :]


def part(after, n, a, b):
    shapes = [(n, a.shape[1]), (a.shape[0] - n, a.shape[1])]
    return launch(
        part_kernel,
        "part",
        (1,),
        (),
        after,
        [(x, whole(*x.shape)) for x in (a, b)],
        [(shape, F32, whole(*shape)) for shape in shapes],
    )


def join_kernel(place, *refs, slots):
    parts, out, sems = refs[:-2], refs[-2], refs[-1]
    copies = []
    start = 0
    for i, slot in enumerate(slots):
        mine, got = parts[2 * i : 2 * i + 2]
        h = mine.shape[0]
        bit = 0 if slot is None else place[slot]
        copies += [
            pltpu.make_async_copy(mine, out.at[pl.ds(start + bit * h, h)], sems.at[2 * i]),
            pltpu.make_async_copy(got, out.at[pl.ds(start + (1 - bit) * h, h)], sems.at[2 * i + 1]),
        ]
        start += 2 * h
    for copy in copies:
        copy.start()
    for copy in copies:
        copy.wait()


def join(place, after, *parts):
    width = parts[0][0].shape[1]
    rows = sum(2 * mine.shape[0] for mine, _, _ in parts)
    anywhere = pl.BlockSpec(memory_space=pltpu.HBM)
    return launch(
        functools.partial(join_kernel, slots=[slot for _, _, slot in parts]),
        "join",
        (1,),
        (place,),
        after,
        [(x, anywhere) for mine, got, _ in parts for x in (mine, got)],
        [((rows, width), F32, once(rows, width))],
        [pltpu.SemaphoreType.DMA((2 * len(parts),))],
    )[0]


def assemble_kernel(place, *refs):
    arrays, (qkv, merge) = refs[:8], refs[8:]
    count = qkv.shape[1]
    j, t = pl.program_id(0), pl.program_id(1)
    core = place[0]
    for other in range(2):
        for p in range(2):
            bit = place[bit_slot(p, 0)] if other == 0 else place[NEAR + p]
            for half in range(2):
                x = arrays[4 * other + 2 * p + half]
                mine = (j == 2 * (core if other == 0 else 1 - core) + p) & (
                    t == (bit if half == 0 else 1 - bit)
                )

                @pl.when(mine & (j < 3))
                def _():
                    qkv[0] = x[:count, :]

                @pl.when(mine & (j == 3))
                def _():
                    merge[...] = x[:count, :]


def small_kernel(place, own0, own1, near0, near1, out):
    one = jnp.where(place[bit_slot(1, 0)] == 0, own0[...], own1[...])
    two = jnp.where(place[NEAR + 1] == 0, near0[...], near1[...])
    out[...] = one + two


def small_sums(place, after, arrays, rows=16):
    n, width = arrays[0].shape
    room = pl.BlockSpec((rows, width), lambda i, _: ((n - ROOM) // rows, 0))
    return launch(
        small_kernel,
        "small_sums",
        (1,),
        (place,),
        after,
        [(x, room) for x in arrays],
        [((rows, width), F32, whole(rows, width))],
    )[0]


def assemble(place, after, arrays, width):
    local = arrays[0].shape[1]
    half = width // 2
    return launch(
        assemble_kernel,
        "assemble",
        (4, 2),
        (place,),
        after,
        [(x, once(*x.shape)) for x in arrays],
        [
            (
                (3, width, local),
                F32,
                pl.BlockSpec(
                    (1, half, local),
                    lambda j, t, _: (jnp.minimum(j, 2), jnp.where(j < 3, t, 1), 0),
                ),
            ),
            (
                (local, width),
                F32,
                pl.BlockSpec((local, half), lambda j, t, _: (0, jnp.where(j < 3, 0, t))),
            ),
        ],
        vmem=40,
    )


def spread_kernel(low, high, up, down):
    piece, width = low.shape[1] // 2, low.shape[2]
    down[0] = low[0, :piece, :]
    down[1] = high[0, :piece, :]
    up[:, :width] = low[0, piece:, :]
    up[:, width:] = high[0, piece:, :]


def spread(after, gathered):
    count, rows, width = gathered.shape
    piece = rows // 2
    half = count // 2
    return launch(
        spread_kernel,
        "spread",
        (half,),
        (),
        after,
        [
            (gathered, pl.BlockSpec((1, rows, width), lambda n: (n, 0, 0))),
            (gathered, pl.BlockSpec((1, rows, width), lambda n: (half + n, 0, 0))),
        ],
        [
            ((half * piece, 2 * width), F32, pl.BlockSpec((piece, 2 * width), lambda n: (n, 0))),
            (
                (2, half * piece, width),
                F32,
                pl.BlockSpec((2, piece, width), lambda n: (0, n, 0)),
            ),
        ],
        vmem=60,
    )


AXES = ("xlo", "z", "y", "core", "tensor")
RINGS = ("z", "y", "core")
DIRECTIONS = (("y", 0), ("z", 0), ("y", 1), ("z", 1))
SWAP = ((0, 1), (1, 0))


def partner(place, bit):
    return place ^ 1 if bit == 0 else 3 - place


def bit_at(place, bit):
    return int(place in (1, 2)) if bit == 0 else int(place >= 2)


def order_of(core, part):
    return [(core + 2 * part + step) % 4 for step in range(4)]


def spot_of(z, y, core, part):
    spot = 0
    for direction in order_of(core, part):
        axis, bit = DIRECTIONS[direction]
        spot = 2 * spot + bit_at(y if axis == "y" else z, bit)
    return spot


def step_pairs(part, step):
    pairs = []
    for z in range(4):
        for y in range(4):
            for core in range(2):
                axis, bit = DIRECTIONS[order_of(core, part)[step]]
                z2, y2 = (z, partner(y, bit)) if axis == "y" else (partner(z, bit), y)
                pairs.append(((z * 4 + y) * 2 + core, (z2 * 4 + y2) * 2 + core))
    return pairs


def place_table():
    rows = []
    for z in range(4):
        for y in range(4):
            for core in range(2):
                row = [core]
                for part in range(2):
                    for direction in order_of(core, part):
                        axis, bit = DIRECTIONS[direction]
                        row.append(bit_at(y if axis == "y" else z, bit))
                for half in (core, 1 - core):
                    row.append(half)
                    for part in range(2):
                        here = spot_of(z, y, half, part)
                        row += [
                            here ^ spot_of(z2, y2, half, part) for z2 in range(4) for y2 in range(4)
                        ]
                for part in range(2):
                    axis, bit = DIRECTIONS[order_of(1 - core, part)[0]]
                    row.append(bit_at(y if axis == "y" else z, bit))
                rows.append(row)
    return np.array(rows, np.int32)


OWN = 9
OTHER = OWN + 33
NEAR = OTHER + 33


def bit_slot(part, step):
    return 1 + 4 * part + step


def send_step(x, part, step):
    return lax.ppermute(x, RINGS, step_pairs(part, step))


def exchange(x, axis):
    return lax.ppermute(x, axis, SWAP)


def body(
    tokens,
    norm_gain,
    norm_shift,
    qkv_weight,
    merge_weight,
    up_weight,
    inner_shift,
    down_weight,
    outer_shift,
    cotangent,
):
    length, width = tokens.shape
    local = merge_weight.shape[0]
    hidden = up_weight.shape[1]
    place = lax.dynamic_index_in_dim(
        jnp.asarray(place_table()), lax.axis_index(RINGS), 0, keepdims=False
    )
    cos, sin = rotary_tables(length)
    w3 = qkv_weight.transpose(1, 0, 2)
    gain, shift, inner_row = norm_gain[None], norm_shift[None], inner_shift[None]

    normed, normed_t, q, k, v, dh, outer_g = project(
        tokens, gain, shift, w3, merge_weight, cotangent, cos, sin
    )
    out_f, dn_f, active, d_pre, inner_g = hidden_pass(
        (outer_g,), normed, cotangent, up_weight, inner_row, down_weight
    )

    (down_s,) = down_grad(place, OTHER, (inner_g,), active, cotangent)
    down_got = exchange(down_s, "core")
    (up_s,) = up_grad(place, OTHER, (down_s,), normed_t, d_pre)
    up_got = exchange(up_s, "core")

    ho0, dq0, dk_part, dv_part = attend(0, (up_s,), q, k, v, dh, cos, sin)
    mine = list(forward_part(0, (dq0,), ho0, merge_weight, out_f, (512,)))
    theirs = [exchange(mine[0], "tensor")]

    def flat(x):
        return x.reshape(-1, x.shape[-1])

    down_k, down_s = map(flat, down_grad(place, OWN, (mine[0],), active, cotangent, down_got))
    down_got = send_step(down_s, 0, 0)
    up_k, up_s = map(flat, up_grad(place, OWN, (down_s,), normed_t, d_pre, up_got))
    up_got = send_step(up_s, 1, 0)

    ho1, dq1, dk, dv = attend(1, (up_s,), q, k, v, dh, cos, sin, (dk_part, dv_part))
    mine += forward_part(1, (dq1,), ho1, merge_weight, out_f, (512,))
    theirs += [exchange(x, "tensor") for x in mine[1:]]

    own0, own1, tail_s0, tail_s1 = tail(
        place, (mine[1],), normed_t, ho0, ho1, cotangent, dq0, dq1, dk, dv
    )
    tail_got0 = exchange(tail_s0, "core")
    tail_got1 = exchange(tail_s1, "core")
    down_k, down_s = halve(place, None, (tail_s0, theirs[0]), down_k, down_got)
    down_got = send_step(down_s, 0, 1)
    up_k, up_s = halve(place, None, (down_s,), up_k, up_got)
    up_got = send_step(up_s, 1, 1)
    back, sums = backward_pass((up_s,), dq0, dq1, dk, dv, w3, dn_f, tokens)

    tail_k0, tail_s0 = halve(place, bit_slot(0, 0), (sums,), own0, tail_got0)
    tail_got0 = send_step(tail_s0, 0, 0)
    tail_k1, tail_s1 = halve_small(
        place, bit_slot(1, 0), (tail_s0,), own1, tail_got1, sums, outer_g, inner_g
    )
    tail_got1 = send_step(tail_s1, 1, 0)

    down_k, down_s = halve(place, None, (tail_s1,), down_k, down_got)
    down_got = send_step(down_s, 0, 2)
    up_k, up_s = halve(place, None, (down_s,), up_k, up_got)
    up_got = send_step(up_s, 1, 2)

    tail_k0, tail_s0 = halve(place, bit_slot(0, 1), (up_s,), tail_k0, tail_got0)
    tail_got0 = send_step(tail_s0, 0, 1)
    tail_k1, tail_s1 = halve(place, bit_slot(1, 1), (tail_s0,), tail_k1, tail_got1)
    tail_got1 = send_step(tail_s1, 1, 1)

    down_k, down_s = halve(place, None, (tail_s1,), down_k, down_got)
    down_got = send_step(down_s, 0, 3)
    up_k, up_s = halve(place, None, (down_s,), up_k, up_got)
    up_got = send_step(up_s, 1, 3)

    tail_k0, tail_s0 = halve(place, bit_slot(0, 2), (up_s, theirs[1]), tail_k0, tail_got0)
    tail_got0 = send_step(tail_s0, 0, 2)
    tail_k1, tail_s1 = halve(place, bit_slot(1, 2), (tail_s0,), tail_k1, tail_got1)
    tail_got1 = send_step(tail_s1, 1, 2)

    feed_x = pack((tail_s1,), down_k, down_got, up_k, up_got)
    feed_got = exchange(feed_x, "xlo")
    (back0,) = hand((feed_x,), back, 0, (128,))
    back_got0 = exchange(back0, "tensor")

    tail_k0, tail_s0 = halve(place, bit_slot(0, 3), (back0,), tail_k0, tail_got0)
    tail_got0 = send_step(tail_s0, 0, 3)
    tail_k1, tail_s1 = halve(place, bit_slot(1, 3), (tail_s0,), tail_k1, tail_got1)
    tail_got1 = send_step(tail_s1, 1, 3)

    feed_x = plus((tail_s1,), feed_x, feed_got)
    gathered = lax.all_gather(feed_x, ("core", "z", "y"))

    tail_x = pack((feed_x,), tail_k0, tail_got0, tail_k1, tail_got1)
    tail_got = exchange(tail_x, "xlo")

    tail0, tail1 = part((tail_x, back_got0), tail_k0.shape[0], tail_x, tail_got)
    tail_got0 = send_step(tail0, 0, 3)
    tail_got1 = send_step(tail1, 1, 3)

    backs = list(hand((tail1,), back, 128, (256,)))
    backs += hand((backs[0],), back, 384, (384, 256))
    back_gots = [exchange(x, "tensor") for x in backs]

    turn = backs[1]
    for step in (3, 2, 1):
        sink = (back_gots[0],) if step == 2 else ()
        other = (back_gots[1],) if step == 1 else ()
        tail0 = join(place, (turn, tail1, *sink), (tail0, tail_got0, bit_slot(0, step)))
        tail_got0 = send_step(tail0, 0, step - 1)
        tail1 = join(place, (tail0, *other), (tail1, tail_got1, bit_slot(1, step)))
        tail_got1 = send_step(tail1, 1, step - 1)
        if step == 3:
            block_out = finish(
                "finish_out", (tail1,), (tokens,), mine, theirs, outer_shift[None]
            )
            turn = block_out
        if step == 2:
            token_grad = finish(
                "finish_grad", (tail1,), (tokens, cotangent), (back0, backs[0]),
                (back_got0, back_gots[0]), gain, vmem=60,
            )
            turn = token_grad

    up_out, down_out = spread((tail1,), gathered)
    down_out = down_out.reshape(hidden, width)

    near0, near1 = exchange(tail0, "core"), exchange(tail1, "core")
    tail_got0, tail_got1 = hand_all((up_out,), tail_got0, tail_got1)
    near_got0, near_got1 = exchange(tail_got0, "core"), exchange(tail_got1, "core")
    token_grad = finish(
        "finish_grad", (tail_got0,), (tokens, cotangent), (backs[1],), (back_gots[1],), gain,
        start=384, into=token_grad, vmem=60,
    )
    own = (tail0, tail_got0, tail1, tail_got1)
    near = (near0, near_got0, near1, near_got1)
    small = small_sums(place, (token_grad,), (*own[2:], *near[2:]))
    pair = small[:4].reshape(2, width)
    pair = pair + exchange(pair, "tensor")
    qkv_out, merge_out = assemble(place, (small,), (*own, *near), width)
    token_grad = finish(
        "finish_grad", (merge_out,), (tokens, cotangent), (backs[2],), (back_gots[2],), gain,
        start=768, into=token_grad, vmem=60,
    )
    return (
        block_out,
        token_grad,
        pair[0],
        pair[1],
        qkv_out.transpose(1, 0, 2),
        merge_out,
        up_out,
        small[6 : 6 + hidden // local].reshape(hidden),
        down_out,
        small[4:6].reshape(width),
    )


def solution(mesh):
    dp = AXES[:4]
    finer = Mesh(mesh.devices.reshape(2, 4, 4, 2, 2), AXES)
    return jax.shard_map(
        body,
        mesh=finer,
        in_specs=(
            P(dp, None),
            P(),
            P(),
            P(None, None, "tensor"),
            P("tensor", None),
            P(None, "tensor"),
            P("tensor"),
            P("tensor", None),
            P(),
            P(dp, None),
        ),
        out_specs=(
            P(dp, None),
            P(dp, None),
            P(),
            P(),
            P(None, None, "tensor"),
            P("tensor", None),
            P(None, "tensor"),
            P("tensor"),
            P("tensor", None),
            P(),
        ),
        check_vma=False,
    )
```

profile of v0, /device:TPU:1, one launch (start us, length us, event | category | flops | bytes accessed | tf_op | source)
XLA Modules:
  0.0 337.9 jit_solution(7769766816472002166)
XLA Ops:
  7.9 11.5 %project.1 = (bf16[1024,1024]{1,0:T(8,128)(2,1)}, bf16[1024,1024]{1,0:T(8,128)(2,1)}, bf16[1024,512]{1,0:T(8,128)(2,1)}, bf16[1024,512]{1,0:T(8,128)(2,1)}, bf16...) custom-call(bf16[1024,1024]{1,0:T(8,128)(2,1)} %refs_2_.11, f32[1,1024]{1,0:T(1,128)} %bitcast.31, ...), custom_call_target="tpu_custom_call" | custom-call | flops 4294967296 | bytes 17838080 | tf_op jit(solution)/shard_map/project/pallas_call | solution.py:57
  19.4 26.9 %hidden.1 = (f32[1024,1024]{1,0:T(8,128)}, f32[1024,1024]{1,0:T(8,128)}, bf16[1024,2048]{1,0:T(8,128)(2,1)}, bf16[1024,2048]{1,0:T(8,128)(2,1)}, f32[1,2048]{1,0:T(1,128)}) custom-call(f32[1,1024]{1,0:T(1,128)} %get-tuple-element.78.refs_0_.refs_5_, bf16[1024,1024]{1,0:T(8,128)(2,1)} %get-tuple-element.79.refs_1_, bf16[1024,1024]{1,0:T(8,128)(2,1)} %refs_3_.9, ...), custom_call_target="tpu_custom_call" | custom-call | flops 19327352832 | bytes 29376512 | tf_op jit(solution)/shard_map/hidden/pallas_call | solution.py:57
  49.2 3.9 %grad.4.refs_1_ = f32[16,64,1024]{2,1,0:T(8,128)S(1)} custom-call(s32[77]{0:T(128)S(1)} %dynamic-slice_bitcast_fusion.refs_0_, f32[1,2048]{1,0:T(1,128)S(1)} %copy-done.40, bf16[1024,2048]{1,0:T(8,128)(2,1)S(1)} %copy-done.10, bf16[1024,1024]{1,0:T(8,128)(2,1)S(1)} %copy-done), custom_call_target="tpu_custom_call" | custom-call | flops 2147483648 | bytes 10485760 | tf_op jit(solution)/shard_map/grad/pallas_call | solution.py:57
  54.7 3.8 %grad.5.refs_0_ = f32[16,64,1024]{2,1,0:T(8,128)S(1)} custom-call(s32[77]{0:T(128)S(1)} %dynamic-slice_bitcast_fusion.refs_0_, f32[16,64,1024]{2,1,0:T(8,128)S(1)} %grad.4.refs_1_, bf16[1024,1024]{1,0:T(8,128)(2,1)S(1)} %copy-done.22, bf16[1024,2048]{1,0:T(8,128)(2,1)S(1)} %copy-done.8), custom_call_target="tpu_custom_call" | custom-call | flops 2147483648 | bytes 10485760 | tf_op jit(solution)/shard_map/grad/pallas_call | solution.py:57
  59.0 8.7 %attend.2 = (bf16[512,512]{1,0:T(8,128)(2,1)S(1)}, bf16[512,512]{1,0:T(8,128)(2,1)S(1)}, f32[512,512]{1,0:T(8,128)S(1)}, f32[512,512]{1,0:T(8,128)S(1)}) custom-call(f32[16,64,1024]{2,1,0:T(8,128)S(1)} %grad.5.refs_0_, bf16[1024,512]{1,0:T(8,128)(2,1)S(1)} %copy-done.48, bf16[1024,512]{1,0:T(8,128)(2,1)S(1)} %copy-done.54, bf16[1024,512]{1,0:T(8,128)(2,1)S(1)} %copy-done.50, ...), custom_call_target="tpu_custom_call" | custom-call | flops 4026531840 | bytes 8388608 | tf_op jit(solution)/shard_map/attend/pallas_call | solution.py:57
  70.1 2.9 collective-permute-start.2
  73.0 5.6 %grad.6 = (f32[8,64,1024]{2,1,0:T(8,128)S(1)}, f32[8,64,1024]{2,1,0:T(8,128)}) custom-call(s32[77]{0:T(128)S(1)} %dynamic-slice_bitcast_fusion.refs_0_, f32[512,1024]{1,0:T(8,128)S(1)} %forward.2.refs_1_.refs_2_, bf16[1024,2048]{1,0:T(8,128)(2,1)S(1)} %copy-done.11, bf16[1024,1024]{1,0:T(8,128)(2,1)S(1)} %copy-done, ...), custom_call_target="tpu_custom_call" | custom-call | flops 2147483648 | bytes 14680064 | tf_op jit(solution)/shard_map/grad/pallas_call | solution.py:57
  80.5 6.0 %grad.7 = (f32[8,64,1024]{2,1,0:T(8,128)S(1)}, f32[8,64,1024]{2,1,0:T(8,128)}) custom-call(s32[77]{0:T(128)S(1)} %dynamic-slice_bitcast_fusion.refs_0_, f32[512,1024]{1,0:T(8,128)} %bitcast.5.refs_1_, bf16[1024,1024]{1,0:T(8,128)(2,1)S(1)} %copy-done.22, bf16[1024,2048]{1,0:T(8,128)(2,1)S(1)} %copy-done.8, f32[16,64,1024]{2,1,0:T(8,128)} %collective-permute-done.1.refs_4_), custom_call_target="tpu_custom_call" | custom-call | flops 2147483648 | bytes 14680064 | tf_op jit(solution)/shard_map/grad/pallas_call | solution.py:57
  91.9 17.3 %attend.3 = (bf16[512,512]{1,0:T(8,128)(2,1)S(1)}, bf16[512,512]{1,0:T(8,128)(2,1)S(1)}, bf16[1024,512]{1,0:T(8,128)(2,1)S(1)}, bf16[1024,512]{1,0:T(8,128)(2,1)S(1)}) custom-call(f32[512,1024]{1,0:T(8,128)} %bitcast.6.refs_0_, bf16[1024,512]{1,0:T(8,128)(2,1)S(1)} %copy-done.49, bf16[1024,512]{1,0:T(8,128)(2,1)S(1)} %copy-done.55, ...), custom_call_target="tpu_custom_call" | custom-call | flops 8053063680 | bytes 10485760 | tf_op jit(solution)/shard_map/attend/pallas_call | solution.py:57
  112.6 8.3 %tail.1 = (f32[1024,512]{1,0:T(8,128)S(1)}, f32[1152,512]{1,0:T(8,128)S(1)}, f32[1024,512]{1,0:T(8,128)}, f32[1152,512]{1,0:T(8,128)}) custom-call(s32[77]{0:T(128)S(1)} %dynamic-slice_bitcast_fusion.refs_0_, f32[512,1024]{1,0:T(8,128)} %forward.3.refs_1_.refs_3_, bf16[1024,1024]{1,0:T(8,128)(2,1)S(1)} %copy-done.23, bf16[512,512]{1,0:T(8,128)(2,1)S(1)} %copy-done.39, ...), custom_call_target="tpu_custom_call" | custom-call | flops 4294967296 | bytes 17301504 | tf_op jit(solution)/shard_map/tail/pallas_call | solution.py:57
  123.8 3.3 halve.13
  127.1 2.7 collective-permute-start.7
  131.6 9.3 %backward.1 = (f32[1024,1024]{1,0:T(8,128)}, f32[2,1024]{1,0:T(2,128)}) custom-call(f32[256,1024]{1,0:T(8,128)} %get-tuple-element.103.refs_0_, bf16[512,512]{1,0:T(8,128)(2,1)} %copy-done.32, bf16[512,512]{1,0:T(8,128)(2,1)} %copy-done.33, bf16[1024,512]{1,0:T(8,128)(2,1)} %copy-done.36, bf16[1024,512]{1,0:T(8,128)(2,1)} %copy-done.37, ...), custom_call_target="tpu_custom_call" | custom-call | flops 3221225472 | bytes 16785408 | tf_op jit(solution)/shard_map/backward/pallas_call | solution.py:57
  154.2 8.4 %collective-permute-done.9.refs_3_.refs_5_ = f32[512,512]{1,0:T(8,128)S(1)} collective-permute-done((f32[512,512]{1,0:T(8,128)S(1)}, f32[512,512]{1,0:T(8,128)S(1)}, u32[]{:S(2)}, u32[]{:S(2)}) %collective-permute-start.9) | collective-permute-done | bytes 1048608 | tf_op jit(solution)/shard_map/ppermute | solution.py:1032
  172.6 4.9 %collective-permute-done.14.refs_4_.refs_6_ = f32[256,512]{1,0:T(8,128)S(1)} collective-permute-done((f32[256,512]{1,0:T(8,128)S(1)}, f32[256,512]{1,0:T(8,128)S(1)}, u32[]{:S(2)}, u32[]{:S(2)}) %collective-permute-start.14) | collective-permute-done | bytes 524320 | tf_op jit(solution)/shard_map/ppermute | solution.py:1032
  181.6 6.0 %collective-permute-done.18.refs_3_.refs_5_ = f32[128,512]{1,0:T(8,128)S(1)} collective-permute-done((f32[128,512]{1,0:T(8,128)S(1)}, f32[128,512]{1,0:T(8,128)S(1)}, u32[]{:S(2)}, u32[]{:S(2)}) %collective-permute-start.18) | collective-permute-done | bytes 262176 | tf_op jit(solution)/shard_map/ppermute | solution.py:1032
  193.1 3.8 %collective-permute-done.21.refs_2_ = f32[64,512]{1,0:T(8,128)S(1)} collective-permute-done((f32[64,512]{1,0:T(8,128)S(1)}, f32[64,512]{1,0:T(8,128)S(1)}, u32[]{:S(2)}, u32[]{:S(2)}) %collective-permute-start.21) | collective-permute-done | bytes 131104 | tf_op jit(solution)/shard_map/ppermute | solution.py:1032
  197.0 3.1 collective-permute-done.23.refs_1_.refs_5_
  200.1 6.1 %collective-permute-done.24.refs_3_ = f32[136,512]{1,0:T(8,128)S(1)} collective-permute-done((f32[136,512]{1,0:T(8,128)S(1)}, f32[136,512]{1,0:T(8,128)S(1)}, u32[]{:S(2)}, u32[]{:S(2)}) %collective-permute-start.24) | collective-permute-done | bytes 278560 | tf_op jit(solution)/shard_map/ppermute | solution.py:1036
  211.2 2.8 collective-permute-start.31
  215.3 4.1 %collective-permute-done.25.refs_4_ = f32[64,512]{1,0:T(8,128)S(1)} collective-permute-done((f32[64,512]{1,0:T(8,128)S(1)}, f32[64,512]{1,0:T(8,128)S(1)}, u32[]{:S(2)}, u32[]{:S(2)}) %collective-permute-start.25) | collective-permute-done | bytes 131104 | tf_op jit(solution)/shard_map/ppermute | solution.py:1032
  223.9 7.3 %finish_out.1.refs_1_ = bf16[1024,1024]{1,0:T(8,128)(2,1)} custom-call(f32[144,512]{1,0:T(8,128)S(1)} %join.7.refs_0_.refs_2_, bf16[1024,1024]{1,0:T(8,128)(2,1)S(1)} %copy-done.3, f32[512,1024]{1,0:T(8,128)S(1)} %copy-done.7, f32[512,1024]{1,0:T(8,128)} %forward.3.refs_1_.refs_3_, f32[512,1024]{1,0:T(8,128)} %collective-permute-done.2.refs_2_.refs_4_, ...), custom_call_target="tpu_custom_call" | custom-call | bytes 12587008 | tf_op jit(solution)/shard_map/finish_out/pallas_call | solution.py:57
  237.7 4.9 %finish_grad.3.refs_1_ = bf16[1024,1024]{1,0:T(8,128)(2,1)} custom-call(f32[288,512]{1,0:T(8,128)} %copy-done.12, bf16[1024,1024]{1,0:T(8,128)(2,1)} %refs_2_.11, bf16[1024,1024]{1,0:T(8,128)(2,1)} %refs_3_.9, f32[128,1024]{1,0:T(8,128)} %copy-done.24, f32[256,1024]{1,0:T(8,128)} %copy-done.15, f32[128,1024]{1,0:T(8,128)} %copy-done.31, ...), custom_call_target="tpu_custom_call" | custom-call | bytes 9441280 | tf_op jit(solution)/shard_map/finish_grad/pallas_call | solution.py:57
  242.6 15.8 %collective-permute-done.30.refs_4_ = f32[256,512]{1,0:T(8,128)S(1)} collective-permute-done((f32[256,512]{1,0:T(8,128)S(1)}, f32[256,512]{1,0:T(8,128)S(1)}, u32[]{:S(2)}, u32[]{:S(2)}) %collective-permute-start.30) | collective-permute-done | bytes 524320 | tf_op jit(solution)/shard_map/ppermute | solution.py:1032
  267.8 7.6 %collective-permute-start.35 = (f32[576,512]{1,0:T(8,128)}, f32[576,512]{1,0:T(8,128)S(1)}, u32[]{:S(2)}, u32[]{:S(2)}) collective-permute-start(f32[576,512]{1,0:T(8,128)} %join.11.refs_0_.refs_2_.refs_4_), channel_id=1, source_target_pairs={{0,2},{2,0},{1,3},{3,1},{4,6},{6,4},{5,7},{7,5},{8,10},{10,8},{9,1... | collective-permute-start | bytes 3538952 | tf_op jit(solution)/shard_map/ppermute | solution.py:1036
  275.4 17.2 %spread.1 = (f32[1024,2048]{1,0:T(8,128)}, f32[2,1024,1024]{2,1,0:T(8,128)}) custom-call(f32[576,512]{1,0:T(8,128)} %join.11.refs_0_.refs_2_.refs_4_, f32[32,128,1024]{2,1,0:T(8,128)} %bitcast.27, f32[32,128,1024]{2,1,0:T(8,128)} %bitcast.28), custom_call_target="tpu_custom_call" | custom-call | bytes 50331648 | tf_op jit(solution)/shard_map/spread/pallas_call | solution.py:57
  293.6 3.4 %copy-done.20 = f32[1024,2048]{1,0:T(8,128)S(1)} copy-done((f32[1024,2048]{1,0:T(8,128)S(1)}, f32[1024,2048]{1,0:T(8,128)}, u32[]{:S(2)}) %copy-start.20) | copy-done | bytes 8388632
  301.2 2.9 collective-permute-start.39
  304.1 4.6 %finish_grad.4.refs_1_ = bf16[1024,1024]{1,0:T(8,128)(2,1)} custom-call(f32[512,512]{1,0:T(8,128)} %get-tuple-element.140.refs_0_.refs_3_, bf16[1024,1024]{1,0:T(8,128)(2,1)} %finish_grad.3.refs_1_, bf16[1024,1024]{1,0:T(8,128)(2,1)} %refs_2_.11, bf16[1024,1024]{1,0:T(8,128)(2,1)} %refs_3_.9, ...), custom_call_target="tpu_custom_call", output_to_operand_aliasing={{}: (1, {})} | custom-call | bytes 9441280 | tf_op jit(solution)/shard_map/finish_grad/pallas_call | solution.py:57
  313.0 8.2 %assemble.1 = (f32[3,1024,512]{2,1,0:T(8,128)}, f32[512,1024]{1,0:T(8,128)}) custom-call(s32[77]{0:T(128)S(1)} %dynamic-slice_bitcast_fusion.refs_0_, f32[16,512]{1,0:T(8,128)S(1)} %small_sums.1.refs_1_, f32[512,512]{1,0:T(8,128)S(1)} %join.10.refs_1_.refs_2_, f32[512,512]{1,0:T(8,128)} %get-tuple-element.140.refs_0_.refs_3_, ...), custom_call_target="tpu_custom_call" | custom-call | bytes 17301504 | tf_op jit(solution)/shard_map/assemble/pallas_call | solution.py:57
  321.2 6.0 %collective-permute-done.39.refs_5_ = f32[256,1024]{1,0:T(8,128)} collective-permute-done((f32[256,1024]{1,0:T(8,128)}, f32[256,1024]{1,0:T(8,128)}, u32[]{:S(2)}, u32[]{:S(2)}) %collective-permute-start.39) | collective-permute-done | bytes 1048608 | tf_op jit(solution)/shard_map/ppermute | solution.py:1036
  327.2 3.0 finish_grad.5
  (228 shorter events, 92.4 us)
Async XLA Ops:
  7.2 268.2 %all-gather.3.cloned.1.call-start = ((), (), s32[]{:S(2)}) async-start(), calls=%async_computation | async-start | bytes 17301504 | tf_op jit(solution)/shard_map/all_gather | solution.py:1138
  53.1 19.9 %collective-permute-start = (f32[16,64,1024]{2,1,0:T(8,128)S(1)}, f32[16,64,1024]{2,1,0:T(8,128)S(1)}, u32[]{:S(2)}, u32[]{:S(2)}) collective-permute-start(f32[16,64,1024]{2,1,0:T(8,128)S(1)} %grad.4.refs_1_), channel_id=1, source_target_pairs={{0,2},{2,0},{1,3},{3,1},{4,6},{6,4},{5,7},{7,5},{8,10},{10,8},{9,1... | collective-permute-start | bytes 12582920 | tf_op jit(solution)/shard_map/ppermute | solution.py:1036
  58.5 22.1 %collective-permute-start.1 = (f32[16,64,1024]{2,1,0:T(8,128)S(1)}, f32[16,64,1024]{2,1,0:T(8,128)}, u32[]{:S(2)}, u32[]{:S(2)}) collective-permute-start(f32[16,64,1024]{2,1,0:T(8,128)S(1)} %grad.5.refs_0_), channel_id=1, source_target_pairs={{0,2},{2,0},{1,3},{3,1},{4,6},{6,4},{5,7},{7,5},{8,10},{10,8},{9,1... | collective-permute-start | bytes 12582920 | tf_op jit(solution)/shard_map/ppermute | solution.py:1036
  70.1 51.7 %collective-permute-start.2 = (f32[512,1024]{1,0:T(8,128)S(1)}, f32[512,1024]{1,0:T(8,128)}, u32[]{:S(2)}, u32[]{:S(2)}) collective-permute-start(f32[512,1024]{1,0:T(8,128)S(1)} %forward.2.refs_1_.refs_2_), channel_id=1, source_target_pairs={{0,1},{1,0},{2,3},{3,2},{4,5},{5,4},{6,7},{7,6},{8,9},{9,8},{10,11... | collective-permute-start | bytes 6291464 | tf_op jit(solution)/shard_map/ppermute | solution.py:1036
  78.7 45.1 %collective-permute-start.3 = (f32[512,1024]{1,0:T(8,128)}, f32[512,1024]{1,0:T(8,128)}, u32[]{:S(2)}, u32[]{:S(2)}) collective-permute-start(f32[512,1024]{1,0:T(8,128)} %bitcast.5.refs_1_), channel_id=1, source_target_pairs={{0,4},{2,18},{4,0},{6,22},{8,12},{10,26},{12,8},{14,30},{16,20},{1... | collective-permute-start | bytes 6291464 | tf_op jit(solution)/shard_map/ppermute | solution.py:1032
  86.6 43.3 %collective-permute-start.4 = (f32[512,1024]{1,0:T(8,128)}, f32[512,1024]{1,0:T(8,128)S(1)}, u32[]{:S(2)}, u32[]{:S(2)}) collective-permute-start(f32[512,1024]{1,0:T(8,128)} %bitcast.6.refs_0_), channel_id=1, source_target_pairs={{0,12},{2,50},{4,8},{6,54},{8,4},{10,58},{12,0},{14,62},{16,28},{1... | collective-permute-start | bytes 6291464 | tf_op jit(solution)/shard_map/ppermute | solution.py:1032
  120.9 23.2 %collective-permute-start.6 = (f32[1152,512]{1,0:T(8,128)}, f32[1152,512]{1,0:T(8,128)}, u32[]{:S(2)}, u32[]{:S(2)}) collective-permute-start(f32[1152,512]{1,0:T(8,128)} %get-tuple-element.109), channel_id=1, source_target_pairs={{0,2},{2,0},{1,3},{3,1},{4,6},{6,4},{5,7},{7,5},{8,10},{10,8},{9,1... | collective-permute-start | bytes 7077896 | tf_op jit(solution)/shard_map/ppermute | solution.py:1036
  121.7 19.2 %collective-permute-start.5 = (f32[1024,512]{1,0:T(8,128)}, f32[1024,512]{1,0:T(8,128)}, u32[]{:S(2)}, u32[]{:S(2)}) collective-permute-start(f32[1024,512]{1,0:T(8,128)} %get-tuple-element.99.refs_1_), channel_id=1, source_target_pairs={{0,2},{2,0},{1,3},{3,1},{4,6},{6,4},{5,7},{7,5},{8,10},{10,8},{9,1... | collective-permute-start | bytes 6291464 | tf_op jit(solution)/shard_map/ppermute | solution.py:1036
  121.8 50.8 %collective-permute-start.13 = (f32[512,1024]{1,0:T(8,128)}, f32[512,1024]{1,0:T(8,128)}, u32[]{:S(2)}, u32[]{:S(2)}) collective-permute-start(f32[512,1024]{1,0:T(8,128)} %forward.3.refs_1_.refs_3_), channel_id=1, source_target_pairs={{0,1},{1,0},{2,3},{3,2},{4,5},{5,4},{6,7},{7,6},{8,9},{9,8},{10,11... | collective-permute-start | bytes 6291464 | tf_op jit(solution)/shard_map/ppermute | solution.py:1036
  127.1 21.5 %collective-permute-start.7 = (f32[256,1024]{1,0:T(8,128)}, f32[256,1024]{1,0:T(8,128)}, u32[]{:S(2)}, u32[]{:S(2)}) collective-permute-start(f32[256,1024]{1,0:T(8,128)} %get-tuple-element.101.refs_1_), channel_id=1, source_target_pairs={{0,16},{2,14},{4,20},{6,10},{8,24},{10,6},{12,28},{14,2},{16,0},{1... | collective-permute-start | bytes 3145736 | tf_op jit(solution)/shard_map/ppermute | solution.py:1032
  131.6 19.9 %collective-permute-start.8 = (f32[256,1024]{1,0:T(8,128)}, f32[256,1024]{1,0:T(8,128)}, u32[]{:S(2)}, u32[]{:S(2)}) collective-permute-start(f32[256,1024]{1,0:T(8,128)} %get-tuple-element.103.refs_0_), channel_id=1, source_target_pairs={{0,48},{2,6},{4,52},{6,2},{8,56},{10,14},{12,60},{14,10},{16,32},{... | collective-permute-start | bytes 3145736 | tf_op jit(solution)/shard_map/ppermute | solution.py:1032
  146.7 16.7 %collective-permute-start.10 = (f32[576,512]{1,0:T(8,128)S(1)}, f32[576,512]{1,0:T(8,128)S(1)}, u32[]{:S(2)}, u32[]{:S(2)}) collective-permute-start(f32[576,512]{1,0:T(8,128)S(1)} %get-tuple-element.110.refs_1_), channel_id=1, source_target_pairs={{0,12},{2,50},{4,8},{6,54},{8,4},{10,58},{12,0},{14,62},{16,28},{1... | collective-permute-start | bytes 3538952 | tf_op jit(solution)/shard_map/ppermute | solution.py:1032
  148.6 14.0 %collective-permute-start.9 = (f32[512,512]{1,0:T(8,128)S(1)}, f32[512,512]{1,0:T(8,128)S(1)}, u32[]{:S(2)}, u32[]{:S(2)}) collective-permute-start(f32[512,512]{1,0:T(8,128)S(1)} %get-tuple-element.107.refs_1_), channel_id=1, source_target_pairs={{0,4},{2,18},{4,0},{6,22},{8,12},{10,26},{12,8},{14,30},{16,20},{1... | collective-permute-start | bytes 3145736 | tf_op jit(solution)/shard_map/ppermute | solution.py:1032
  150.5 18.6 %collective-permute-start.11 = (f32[128,1024]{1,0:T(8,128)S(1)}, f32[128,1024]{1,0:T(8,128)S(1)}, u32[]{:S(2)}, u32[]{:S(2)}) collective-permute-start(f32[128,1024]{1,0:T(8,128)S(1)} %get-tuple-element.112.refs_1_), channel_id=1, source_target_pairs={{0,12},{2,50},{4,8},{6,54},{8,4},{10,58},{12,0},{14,62},{16,28},{1... | collective-permute-start | bytes 1572872 | tf_op jit(solution)/shard_map/ppermute | solution.py:1032
  153.3 16.4 %collective-permute-start.12 = (f32[128,1024]{1,0:T(8,128)S(1)}, f32[128,1024]{1,0:T(8,128)S(1)}, u32[]{:S(2)}, u32[]{:S(2)}) collective-permute-start(f32[128,1024]{1,0:T(8,128)S(1)} %get-tuple-element.114.refs_1_), channel_id=1, source_target_pairs={{0,4},{2,18},{4,0},{6,22},{8,12},{10,26},{12,8},{14,30},{16,20},{1... | collective-permute-start | bytes 1572872 | tf_op jit(solution)/shard_map/ppermute | solution.py:1032
  164.1 14.0 %collective-permute-start.15 = (f32[288,512]{1,0:T(8,128)S(1)}, f32[288,512]{1,0:T(8,128)S(1)}, u32[]{:S(2)}, u32[]{:S(2)}) collective-permute-start(f32[288,512]{1,0:T(8,128)S(1)} %get-tuple-element.118.refs_1_), channel_id=1, source_target_pairs={{0,48},{2,6},{4,52},{6,2},{8,56},{10,14},{12,60},{14,10},{16,32},{... | collective-permute-start | bytes 1769480 | tf_op jit(solution)/shard_map/ppermute | solution.py:1032
  165.6 11.9 %collective-permute-start.14 = (f32[256,512]{1,0:T(8,128)S(1)}, f32[256,512]{1,0:T(8,128)S(1)}, u32[]{:S(2)}, u32[]{:S(2)}) collective-permute-start(f32[256,512]{1,0:T(8,128)S(1)} %get-tuple-element.116.refs_1_), channel_id=1, source_target_pairs={{0,16},{2,14},{4,20},{6,10},{8,24},{10,6},{12,28},{14,2},{16,0},{1... | collective-permute-start | bytes 1572872 | tf_op jit(solution)/shard_map/ppermute | solution.py:1032
  170.3 9.8 %collective-permute-start.17 = (f32[64,1024]{1,0:T(8,128)S(1)}, f32[64,1024]{1,0:T(8,128)S(1)}, u32[]{:S(2)}, u32[]{:S(2)}) collective-permute-start(f32[64,1024]{1,0:T(8,128)S(1)} %get-tuple-element.122.refs_1_), channel_id=1, source_target_pairs={{0,16},{2,14},{4,20},{6,10},{8,24},{10,6},{12,28},{14,2},{16,0},{1... | collective-permute-start | bytes 786440 | tf_op jit(solution)/shard_map/ppermute | solution.py:1032
  189.8 10.4 %collective-permute-start.23 = (f32[128,1024]{1,0:T(8,128)S(1)}, f32[128,1024]{1,0:T(8,128)S(1)}, u32[]{:S(2)}, u32[]{:S(2)}) collective-permute-start(f32[128,1024]{1,0:T(8,128)S(1)} %hand.3.refs_1_.refs_3_), channel_id=1, source_target_pairs={{0,1},{1,0},{2,3},{3,2},{4,5},{5,4},{6,7},{7,6},{8,9},{9,8},{10,11... | collective-permute-start | bytes 1572872 | tf_op jit(solution)/shard_map/ppermute | solution.py:1036
  208.6 24.9 %collective-permute-start.27 = (f32[256,1024]{1,0:T(8,128)S(1)}, f32[256,1024]{1,0:T(8,128)S(1)}, u32[]{:S(2)}, u32[]{:S(2)}) collective-permute-start(f32[256,1024]{1,0:T(8,128)S(1)} %hand.4.refs_0_.refs_4_), channel_id=1, source_target_pairs={{0,1},{1,0},{2,3},{3,2},{4,5},{5,4},{6,7},{7,6},{8,9},{9,8},{10,11... | collective-permute-start | bytes 3145736 | tf_op jit(solution)/shard_map/ppermute | solution.py:1036
  211.2 52.0 %collective-permute-start.31 = (f32[384,1024]{1,0:T(8,128)}, f32[384,1024]{1,0:T(8,128)}, u32[]{:S(2)}, u32[]{:S(2)}) collective-permute-start(f32[384,1024]{1,0:T(8,128)} %get-tuple-element.137.refs_1_.refs_4_), channel_id=1, source_target_pairs={{0,1},{1,0},{2,3},{3,2},{4,5},{5,4},{6,7},{7,6},{8,9},{9,8},{10,11... | collective-permute-start | bytes 4718600 | tf_op jit(solution)/shard_map/ppermute | solution.py:1036
  221.3 14.9 %collective-permute-start.29 = (f32[144,512]{1,0:T(8,128)S(1)}, f32[144,512]{1,0:T(8,128)S(1)}, u32[]{:S(2)}, u32[]{:S(2)}) collective-permute-start(f32[144,512]{1,0:T(8,128)S(1)} %join.7.refs_0_.refs_2_), channel_id=1, source_target_pairs={{0,4},{2,18},{4,0},{6,22},{8,12},{10,26},{12,8},{14,30},{16,20},{1... | collective-permute-start | bytes 884744 | tf_op jit(solution)/shard_map/ppermute | solution.py:1032
  223.5 10.0 %collective-permute-start.28 = (f32[128,512]{1,0:T(8,128)S(1)}, f32[128,512]{1,0:T(8,128)S(1)}, u32[]{:S(2)}, u32[]{:S(2)}) collective-permute-start(f32[128,512]{1,0:T(8,128)S(1)} %join.6.refs_1_.refs_4_), channel_id=1, source_target_pairs={{0,12},{2,50},{4,8},{6,54},{8,4},{10,58},{12,0},{14,62},{16,28},{1... | collective-permute-start | bytes 786440 | tf_op jit(solution)/shard_map/ppermute | solution.py:1032
  236.9 26.3 %collective-permute-start.32 = (f32[288,512]{1,0:T(8,128)S(1)}, f32[288,512]{1,0:T(8,128)S(1)}, u32[]{:S(2)}, u32[]{:S(2)}) collective-permute-start(f32[288,512]{1,0:T(8,128)S(1)} %join.9.refs_0_.refs_2_.refs_3_), channel_id=1, source_target_pairs={{0,48},{2,6},{4,52},{6,2},{8,56},{10,14},{12,60},{14,10},{16,32},{... | collective-permute-start | bytes 1769480 | tf_op jit(solution)/shard_map/ppermute | solution.py:1032
  237.0 21.4 %collective-permute-start.30 = (f32[256,512]{1,0:T(8,128)S(1)}, f32[256,512]{1,0:T(8,128)S(1)}, u32[]{:S(2)}, u32[]{:S(2)}) collective-permute-start(f32[256,512]{1,0:T(8,128)S(1)} %join.8.refs_1_.refs_3_), channel_id=1, source_target_pairs={{0,16},{2,14},{4,20},{6,10},{8,24},{10,6},{12,28},{14,2},{16,0},{1... | collective-permute-start | bytes 1572872 | tf_op jit(solution)/shard_map/ppermute | solution.py:1032
  265.0 27.6 %collective-permute-start.34 = (f32[576,512]{1,0:T(8,128)}, f32[576,512]{1,0:T(8,128)S(1)}, u32[]{:S(2)}, u32[]{:S(2)}) collective-permute-start(f32[576,512]{1,0:T(8,128)} %join.11.refs_0_.refs_2_.refs_4_), channel_id=1, source_target_pairs={{0,12},{2,50},{4,8},{6,54},{8,4},{10,58},{12,0},{14,62},{16,28},{1... | collective-permute-start | bytes 3538952 | tf_op jit(solution)/shard_map/ppermute | solution.py:1032
  265.7 27.0 %collective-permute-start.33 = (f32[512,512]{1,0:T(8,128)S(1)}, f32[512,512]{1,0:T(8,128)}, u32[]{:S(2)}, u32[]{:S(2)}) collective-permute-start(f32[512,512]{1,0:T(8,128)S(1)} %join.10.refs_1_.refs_2_), channel_id=1, source_target_pairs={{0,4},{2,18},{4,0},{6,22},{8,12},{10,26},{12,8},{14,30},{16,20},{1... | collective-permute-start | bytes 3145736 | tf_op jit(solution)/shard_map/ppermute | solution.py:1032
  267.8 40.9 %collective-permute-start.35 = (f32[576,512]{1,0:T(8,128)}, f32[576,512]{1,0:T(8,128)S(1)}, u32[]{:S(2)}, u32[]{:S(2)}) collective-permute-start(f32[576,512]{1,0:T(8,128)} %join.11.refs_0_.refs_2_.refs_4_), channel_id=1, source_target_pairs={{0,2},{2,0},{1,3},{3,1},{4,6},{6,4},{5,7},{7,5},{8,10},{10,8},{9,1... | collective-permute-start | bytes 3538952 | tf_op jit(solution)/shard_map/ppermute | solution.py:1036
  300.7 12.3 %collective-permute-start.37 = (f32[512,512]{1,0:T(8,128)S(1)}, f32[512,512]{1,0:T(8,128)}, u32[]{:S(2)}, u32[]{:S(2)}) collective-permute-start(f32[512,512]{1,0:T(8,128)S(1)} %join.10.refs_1_.refs_2_), channel_id=1, source_target_pairs={{0,2},{2,0},{1,3},{3,1},{4,6},{6,4},{5,7},{7,5},{8,10},{10,8},{9,1... | collective-permute-start | bytes 3145736 | tf_op jit(solution)/shard_map/ppermute | solution.py:1036
  301.2 11.8 %collective-permute-start.38 = (f32[512,512]{1,0:T(8,128)}, f32[512,512]{1,0:T(8,128)}, u32[]{:S(2)}, u32[]{:S(2)}) collective-permute-start(f32[512,512]{1,0:T(8,128)} %get-tuple-element.140.refs_0_.refs_3_), channel_id=1, source_target_pairs={{0,2},{2,0},{1,3},{3,1},{4,6},{6,4},{5,7},{7,5},{8,10},{10,8},{9,1... | collective-permute-start | bytes 3145736 | tf_op jit(solution)/shard_map/ppermute | solution.py:1036
  301.2 26.1 %collective-permute-start.39 = (f32[256,1024]{1,0:T(8,128)}, f32[256,1024]{1,0:T(8,128)}, u32[]{:S(2)}, u32[]{:S(2)}) collective-permute-start(f32[256,1024]{1,0:T(8,128)} %get-tuple-element.143.refs_4_), channel_id=1, source_target_pairs={{0,1},{1,0},{2,3},{3,2},{4,5},{5,4},{6,7},{7,6},{8,9},{9,8},{10,11... | collective-permute-start | bytes 3145736 | tf_op jit(solution)/shard_map/ppermute | solution.py:1036
  311.6 18.6 %collective-permute-start.40 = (f32[2,1024]{1,0:T(2,128)S(1)}, f32[2,1024]{1,0:T(2,128)S(1)}, u32[]{:S(2)}, u32[]{:S(2)}) collective-permute-start(f32[2,1024]{1,0:T(2,128)S(1)} %reshape.48), channel_id=1, source_target_pairs={{0,1},{1,0},{2,3},{3,2},{4,5},{5,4},{6,7},{7,6},{8,9},{9,8},{10,11... | collective-permute-start | bytes 24584 | tf_op jit(solution)/shard_map/ppermute | solution.py:1036
  (70 other events, 407.6 us)
Sparse Core Ops, SparseCore 0:
  189.9 83.2 all-gather.2
where the time goes:
time: 343 us; the launch traced here: 338 us
  Pallas kernels  182 us (53%)
  waiting for transfers between devices  65.2 us (19%)
  starting transfers between devices  49.5 us (14%)
  local copies, waits for them, and re-layouts  26.4 us (8%)
  between operations  15.1 us (4%)
    pallas_call x47, Pallas kernels, launch(): pl.pallas_call(without, grid_spec=pltpu.PrefetchScalarGridSpec(num_scalar...  182 us
    ppermute x24, waiting for transfers between devices, send_step(): return lax.ppermute(x, RINGS, step_pairs(part, step))  48.4 us
    ppermute x24, starting transfers between devices, send_step(): return lax.ppermute(x, RINGS, step_pairs(part, step))  25.1 us
    unnamed x124, local copies, waits for them, and re-layouts  25.1 us
    ppermute x17, starting transfers between devices, exchange(): return lax.ppermute(x, axis, SWAP)  24.3 us
    ppermute x17, waiting for transfers between devices, exchange(): return lax.ppermute(x, axis, SWAP)  16.7 us
  transfers between devices with their start and end apart: 42, of which 14 were waited for; matrix products, arithmetic and copies ran while one was open for 0% of the time, Pallas kernels for 41%

commit v1 on v0

--- a/solution.py
+++ b/solution.py
@@ -77,6 +77,9 @@
     return got
 
 
+TOKEN = ((8, 128), F32, pl.BlockSpec((8, 128), lambda *_: (0, 0)))
+
+
 def whole(*shape):
     return pl.BlockSpec(shape, lambda *_: (0,) * len(shape))
 
@@ -86,7 +89,7 @@
 
 
 gelu_rate = float(np.sqrt(2 / np.pi))
-ROOM = 64
+SMALL = 16
 
 
 def norm_rows(x):
@@ -497,12 +500,18 @@
     )
 
 
-def backward_kernel(dq0, dq1, dk, dv, w, a, tok, out, sums):
+def backward_kernel(dq0, dq1, dk, dv, w, a, tok, *rest, cuts):
+    pieces, sums = rest[:-1], rest[-1]
     i = pl.program_id(0)
 
     def one(dq):
         total = nt(dq[...], w[0]) + nt(dk[...], w[1]) + nt(dv[...], w[2]) + a[...]
-        out[...] = total
+        for n, piece in enumerate(pieces):
+
+            @pl.when(jnp.logical_and(i >= cuts[n], i < cuts[n + 1]))
+            def _():
+                piece[...] = total
+
         unit, _ = norm_rows(tok[...].astype(F32))
         both = jnp.concatenate(
             [jnp.sum(total * unit, axis=0, keepdims=True), jnp.sum(total, axis=0, keepdims=True)],
@@ -528,14 +537,15 @@
         one(dq1)
 
 
-def backward_pass(after, dq0, dq1, dk, dv, w3, a, tok, rows=256):
+def backward_pass(after, dq0, dq1, dk, dv, w3, a, tok, sizes, rows=256):
     length, local = dk.shape
     width = w3.shape[1]
     steps = length // rows
+    cuts, specs = cut_specs(sizes, rows, width)
     here = pl.BlockSpec((rows, width), lambda i: (i, 0))
     narrow = pl.BlockSpec((rows, local), lambda i: (i, 0))
     return launch(
-        backward_kernel,
+        functools.partial(backward_kernel, cuts=cuts),
         "backward",
         (steps,),
         (),
@@ -549,86 +559,51 @@
             (a, here),
             (tok, here),
         ],
-        [((length, width), F32, here), ((2, width), F32, whole(2, width))],
+        [((n, width), F32, spec) for n, spec in zip(sizes, specs)]
+        + [((2, width), F32, whole(2, width))],
         vmem=60,
         flops=6 * length * width * local,
     )
 
 
-def hand_kernel(x, *pieces, cuts):
-    i = pl.program_id(0)
-    for n, piece in enumerate(pieces):
-
-        @pl.when(jnp.logical_and(i >= cuts[n], i < cuts[n + 1]))
-        def _():
-            piece[...] = x[...]
-
-
-def hand(after, x, start, sizes, rows=128):
-    width = x.shape[1]
-    first = start // rows
-    cuts, specs = cut_specs(sizes, rows, width)
-    return launch(
-        functools.partial(hand_kernel, cuts=cuts),
-        "hand",
-        (cuts[-1],),
-        (),
-        after,
-        [(x, pl.BlockSpec((rows, width), lambda i: (first + i, 0)))],
-        [((size, width), F32, spec) for size, spec in zip(sizes, specs)],
-    )
-
-
-def hand_all_kernel(*refs):
-    half = len(refs) // 2
-    for x, out in zip(refs[:half], refs[half:]):
-        out[...] = x[...]
-
-
-def hand_all(after, *arrays):
-    return launch(
-        hand_all_kernel,
-        "hand_all",
-        (1,),
-        (),
-        after,
-        [(x, once(*x.shape)) for x in arrays],
-        [(x.shape, F32, once(*x.shape)) for x in arrays],
-    )
+def gate_kernel(*refs):
+    pass
+
+
+def gate(after, *arrays):
+    anywhere = pl.BlockSpec(memory_space=pltpu.HBM)
+    n = len(after)
+    return pl.pallas_call(
+        gate_kernel,
+        in_specs=[anywhere] * (n + len(arrays)),
+        out_specs=[anywhere] * len(arrays),
+        out_shape=[jax.ShapeDtypeStruct(x.shape, x.dtype) for x in arrays],
+        input_output_aliases={n + i: i for i in range(len(arrays))},
+        name="gate",
+    )(*after, *arrays)
 
 
 def tail_kernel(place, normed_t, ho0, ho1, cot, dq0, dq1, dk, dv, own0, own1, other0, other1):
     n = normed_t[...]
-    width = n.shape[0]
     half = dq0.shape[0]
     first = place[0] == 0
 
-    def put(mine, x, roomy):
-        def store(ref):
-            if not roomy:
-                ref[...] = x
-                return
-            rows = width // 2
-            blank = jnp.zeros((ROOM, x.shape[1]), F32)
-            for k in range(2):
-                start = k * (rows + ROOM)
-                ref[start : start + rows, :] = x[k * rows : (k + 1) * rows]
-                ref[start + rows : start + rows + ROOM, :] = blank
-
+    def put(mine, x, own, other):
         @pl.when(mine)
         def _():
-            store(own1 if roomy else own0)
+            own[...] = x
 
         @pl.when(jnp.logical_not(mine))
         def _():
-            store(other1 if roomy else other0)
-
-    put(first, nn(n[:, :half], dq0[...]) + nn(n[:, half:], dq1[...]), False)
-    put(first, nn(n, dk[...]), True)
-    put(jnp.logical_not(first), nn(n, dv[...]), False)
+            other[...] = x
+
+    put(first, nn(n[:, :half], dq0[...]) + nn(n[:, half:], dq1[...]), own0, other0)
+    put(first, nn(n, dk[...]), own1, other1)
+    put(jnp.logical_not(first), nn(n, dv[...]), own0, other0)
     g = tn(ho0[...], cot[:half, :]) + tn(ho1[...], cot[half:, :])
     columns = g.shape[1] // 2
-    put(jnp.logical_not(first), jnp.concatenate([g[:, :columns], g[:, columns:]], axis=0), True)
+    g = jnp.concatenate([g[:, :columns], g[:, columns:]], axis=0)
+    put(jnp.logical_not(first), g, own1, other1)
 
 
 def tail(place, after, normed_t, ho0, ho1, cot, dq0, dq1, dk, dv):
@@ -636,7 +611,6 @@
     local = dk.shape[1]
     half = length // 2
     assert 2 * local == width
-    shapes = [(width, local), (width + 2 * ROOM, local)] * 2
     return launch(
         tail_kernel,
         "tail",
@@ -648,48 +622,15 @@
         + [(cot, once(length, width))]
         + [(x, once(half, local)) for x in (dq0, dq1)]
         + [(x, once(length, local)) for x in (dk, dv)],
-        [(shape, F32, once(*shape)) for shape in shapes],
+        [((width, local), F32, once(width, local))] * 4,
         vmem=36,
         flops=8 * length * width * local,
     )
 
 
-def halve_small_kernel(place, own, got, sums, outer, inner, keep, send, *, slot):
-    h, width = keep.shape
-    bit = place[slot]
-    stay = pl.ds(pl.multiple_of(bit * h, ROOM), h)
-    go = pl.ds(pl.multiple_of((1 - bit) * h, ROOM), h)
-    keep[...] = own[stay, :] + got[stay, :]
-    send[...] = own[go, :] + got[go, :]
-    rows = [x[i : i + 1, j : j + width] for x in (sums, outer, inner) for i in range(x.shape[0]) for j in range(0, x.shape[1], width)]
-
-    def put(ref):
-        for i, row in enumerate(rows):
-            ref[h - ROOM + i : h - ROOM + i + 1, :] += row
-
-    @pl.when(bit == 0)
-    def _():
-        put(keep)
-
-    @pl.when(bit == 1)
-    def _():
-        put(send)
-
-
-def halve_small(place, slot, after, own, got, *small):
-    n, width = own.shape
-    return launch(
-        functools.partial(halve_small_kernel, slot=slot),
-        "halve_small",
-        (1,),
-        (place,),
-        after,
-        [(x, once(*x.shape)) for x in (own, got, *small)],
-        [((n // 2, width), F32, once(n // 2, width))] * 2,
-    )
-
-
 def finish_kernel(*refs, cuts, last):
+    refs, token = refs[:-1], refs[-1]
+    token[...] = jnp.zeros_like(token)
     n = len(cuts) - 1
     wide, (mine, got), (row, out) = refs[: -2 * n - 2], (refs[-2 * n - 2 : -n - 2], refs[-n - 2 : -2]), refs[-2:]
     i = pl.program_id(0)
@@ -729,10 +670,10 @@
         + list(zip(mine, pieces))
         + list(zip(got, pieces))
         + [(row, whole(1, width))],
-        [((length, width), BF16, here)],
+        [((length, width), BF16, here), TOKEN],
         vmem=vmem,
         into=into,
-    )[0]
+    )
 
 
 def halve_kernel(place, a, b, c, d, keep, send):
@@ -763,21 +704,32 @@
     )
 
 
-def pack_kernel(a, b, c, d, out):
-    n = a.shape[0]
-    out[:n, :] = a[...] + b[...]
-    out[n:, :] = c[...] + d[...]
-
-
-def pack(after, a, b, c, d):
-    shape = (a.shape[0] + c.shape[0], a.shape[1])
+def pack_kernel(a, b, c, d, *rest):
+    small, out = rest[:-1], rest[-1]
+    n, width = a.shape
+    top = SMALL if small else 0
+    out[top : top + n, :] = a[...] + b[...]
+    out[top + n :, :] = c[...] + d[...]
+    if small:
+        rows = [
+            x[i : i + 1, j : j + width]
+            for x in small
+            for i in range(x.shape[0])
+            for j in range(0, x.shape[1], width)
+        ]
+        rows.append(jnp.zeros((SMALL - len(rows), width), F32))
+        out[:top, :] = jnp.concatenate(rows, axis=0)
+
+
+def pack(after, a, b, c, d, small=()):
+    shape = (a.shape[0] + c.shape[0] + (SMALL if small else 0), a.shape[1])
     return launch(
         pack_kernel,
         "pack",
         (1,),
         (),
         after,
-        [(x, whole(*x.shape)) for x in (a, b, c, d)],
+        [(x, whole(*x.shape)) for x in (a, b, c, d, *small)],
         [(shape, F32, whole(*shape))],
     )[0]
 
@@ -817,38 +769,47 @@
     )
 
 
-def join_kernel(place, *refs, slots):
-    parts, out, sems = refs[:-2], refs[-2], refs[-1]
-    copies = []
-    start = 0
-    for i, slot in enumerate(slots):
-        mine, got = parts[2 * i : 2 * i + 2]
-        h = mine.shape[0]
-        bit = 0 if slot is None else place[slot]
+def join_kernel(place, mine, got, out, *scratch, slot, top):
+    sems = scratch[-1]
+    h = mine.shape[0] - top
+    bit = place[slot]
+    copies = [
+        pltpu.make_async_copy(
+            mine.at[pl.ds(top, h)], out.at[pl.ds(pl.multiple_of(top + bit * h, 8), h)], sems.at[0]
+        ),
+        pltpu.make_async_copy(
+            got.at[pl.ds(top, h)],
+            out.at[pl.ds(pl.multiple_of(top + (1 - bit) * h, 8), h)],
+            sems.at[1],
+        ),
+    ]
+    if top:
+        small = scratch[0]
         copies += [
-            pltpu.make_async_copy(mine, out.at[pl.ds(start + bit * h, h)], sems.at[2 * i]),
-            pltpu.make_async_copy(got, out.at[pl.ds(start + (1 - bit) * h, h)], sems.at[2 * i + 1]),
+            pltpu.make_async_copy(x.at[pl.ds(0, top)], small.at[i], sems.at[2 + i])
+            for i, x in enumerate((mine, got))
         ]
-        start += 2 * h
     for copy in copies:
         copy.start()
     for copy in copies:
         copy.wait()
-
-
-def join(place, after, *parts):
-    width = parts[0][0].shape[1]
-    rows = sum(2 * mine.shape[0] for mine, _, _ in parts)
+    if top:
+        out[:top, :] = small[0] + small[1]
+
+
+def join(place, slot, after, mine, got, top=0):
+    n, width = mine.shape
     anywhere = pl.BlockSpec(memory_space=pltpu.HBM)
-    return launch(
-        functools.partial(join_kernel, slots=[slot for _, _, slot in parts]),
+    rows = 2 * n - top
+    return launch(
+        functools.partial(join_kernel, slot=slot, top=top),
         "join",
         (1,),
         (place,),
         after,
-        [(x, anywhere) for mine, got, _ in parts for x in (mine, got)],
+        [(mine, anywhere), (got, anywhere)],
         [((rows, width), F32, once(rows, width))],
-        [pltpu.SemaphoreType.DMA((2 * len(parts),))],
+        ([pltpu.VMEM((2, top, width), F32)] if top else []) + [pltpu.SemaphoreType.DMA((4,))],
     )[0]
 
 
@@ -868,30 +829,28 @@
 
                 @pl.when(mine & (j < 3))
                 def _():
-                    qkv[0] = x[:count, :]
+                    qkv[0] = x[x.shape[0] - count :, :]
 
                 @pl.when(mine & (j == 3))
                 def _():
-                    merge[...] = x[:count, :]
-
-
-def small_kernel(place, own0, own1, near0, near1, out):
-    one = jnp.where(place[bit_slot(1, 0)] == 0, own0[...], own1[...])
-    two = jnp.where(place[NEAR + 1] == 0, near0[...], near1[...])
-    out[...] = one + two
-
-
-def small_sums(place, after, arrays, rows=16):
-    n, width = arrays[0].shape
-    room = pl.BlockSpec((rows, width), lambda i, _: ((n - ROOM) // rows, 0))
+                    merge[...] = x[x.shape[0] - count :, :]
+
+
+def small_kernel(own0, own1, near0, near1, out):
+    out[...] = (own0[...] + own1[...]) + (near0[...] + near1[...])
+
+
+def small_sums(after, arrays):
+    width = arrays[0].shape[1]
+    top = pl.BlockSpec((SMALL, width), lambda i: (0, 0))
     return launch(
         small_kernel,
         "small_sums",
         (1,),
-        (place,),
-        after,
-        [(x, room) for x in arrays],
-        [((rows, width), F32, whole(rows, width))],
+        (),
+        after,
+        [(x, top) for x in arrays],
+        [((SMALL, width), F32, whole(SMALL, width))],
     )[0]
 
 
@@ -924,35 +883,69 @@
     )
 
 
-def spread_kernel(low, high, up, down):
-    piece, width = low.shape[1] // 2, low.shape[2]
-    down[0] = low[0, :piece, :]
-    down[1] = high[0, :piece, :]
-    up[:, :width] = low[0, piece:, :]
-    up[:, width:] = high[0, piece:, :]
-
-
-def spread(after, gathered):
+def spread_kernel(gathered, up, down, token, buf, in_sems, out_sems):
+    token[...] = jnp.zeros_like(token)
     count, rows, width = gathered.shape
     piece = rows // 2
     half = count // 2
+    slots = buf.shape[0]
+
+    def outs(n):
+        slot = n % slots
+        return (
+            pltpu.make_async_copy(
+                buf.at[slot, pl.ds(0, piece)],
+                down.at[n // half, pl.ds((n % half) * piece, piece)],
+                out_sems.at[2 * slot],
+            ),
+            pltpu.make_async_copy(
+                buf.at[slot, pl.ds(piece, piece)],
+                up.at[pl.ds((n % half) * piece, piece), pl.ds((n // half) * width, width)],
+                out_sems.at[2 * slot + 1],
+            ),
+        )
+
+    def arrive(n):
+        slot = n % slots
+        return pltpu.make_async_copy(gathered.at[n], buf.at[slot], in_sems.at[slot])
+
+    ahead = slots // 2
+    for n in range(count + ahead):
+        if n < count:
+            if n >= slots:
+                for copy in outs(n - slots):
+                    copy.wait()
+            arrive(n).start()
+        if n >= ahead:
+            arrive(n - ahead).wait()
+            for copy in outs(n - ahead):
+                copy.start()
+    for n in range(count - slots, count):
+        for copy in outs(n):
+            copy.wait()
+
+
+def spread(after, gathered, slots=16):
+    count, rows, width = gathered.shape
+    piece = rows // 2
+    half = count // 2
+    anywhere = pl.BlockSpec(memory_space=pltpu.HBM)
     return launch(
         spread_kernel,
         "spread",
-        (half,),
+        (1,),
         (),
         after,
+        [(gathered, anywhere)],
         [
-            (gathered, pl.BlockSpec((1, rows, width), lambda n: (n, 0, 0))),
-            (gathered, pl.BlockSpec((1, rows, width), lambda n: (half + n, 0, 0))),
+            ((half * piece, 2 * width), F32, anywhere),
+            ((2, half * piece, width), F32, anywhere),
+            TOKEN,
         ],
         [
-            ((half * piece, 2 * width), F32, pl.BlockSpec((piece, 2 * width), lambda n: (n, 0))),
-            (
-                (2, half * piece, width),
-                F32,
-                pl.BlockSpec((2, piece, width), lambda n: (0, n, 0)),
-            ),
+            pltpu.VMEM((slots, rows, width), F32),
+            pltpu.SemaphoreType.DMA((slots,)),
+            pltpu.SemaphoreType.DMA((2 * slots,)),
         ],
         vmem=60,
     )
@@ -1095,16 +1088,17 @@
     down_got = send_step(down_s, 0, 1)
     up_k, up_s = halve(place, None, (down_s,), up_k, up_got)
     up_got = send_step(up_s, 1, 1)
-    back, sums = backward_pass((up_s,), dq0, dq1, dk, dv, w3, dn_f, tokens)
-
-    tail_k0, tail_s0 = halve(place, bit_slot(0, 0), (sums,), own0, tail_got0)
+
+    tail_k0, tail_s0 = halve(place, bit_slot(0, 0), (up_s,), own0, tail_got0)
     tail_got0 = send_step(tail_s0, 0, 0)
-    tail_k1, tail_s1 = halve_small(
-        place, bit_slot(1, 0), (tail_s0,), own1, tail_got1, sums, outer_g, inner_g
-    )
+    tail_k1, tail_s1 = halve(place, bit_slot(1, 0), (tail_s0,), own1, tail_got1)
     tail_got1 = send_step(tail_s1, 1, 0)
 
-    down_k, down_s = halve(place, None, (tail_s1,), down_k, down_got)
+    *back, sums = backward_pass(
+        (tail_s1,), dq0, dq1, dk, dv, w3, dn_f, tokens, (512, 512)
+    )
+
+    down_k, down_s = halve(place, None, (sums,), down_k, down_got)
     down_got = send_step(down_s, 0, 2)
     up_k, up_s = halve(place, None, (down_s,), up_k, up_got)
     up_got = send_step(up_s, 1, 2)
@@ -1126,10 +1120,8 @@
 
     feed_x = pack((tail_s1,), down_k, down_got, up_k, up_got)
     feed_got = exchange(feed_x, "xlo")
-    (back0,) = hand((feed_x,), back, 0, (128,))
-    back_got0 = exchange(back0, "tensor")
-
-    tail_k0, tail_s0 = halve(place, bit_slot(0, 3), (back0,), tail_k0, tail_got0)
+
+    tail_k0, tail_s0 = halve(place, bit_slot(0, 3), (feed_x,), tail_k0, tail_got0)
     tail_got0 = send_step(tail_s0, 0, 3)
     tail_k1, tail_s1 = halve(place, bit_slot(1, 3), (tail_s0,), tail_k1, tail_got1)
     tail_got1 = send_step(tail_s1, 1, 3)
@@ -1137,57 +1129,52 @@
     feed_x = plus((tail_s1,), feed_x, feed_got)
     gathered = lax.all_gather(feed_x, ("core", "z", "y"))
 
-    tail_x = pack((feed_x,), tail_k0, tail_got0, tail_k1, tail_got1)
+    tail_x = pack(
+        (feed_x,), tail_k0, tail_got0, tail_k1, tail_got1, (sums, outer_g, inner_g)
+    )
     tail_got = exchange(tail_x, "xlo")
 
-    tail0, tail1 = part((tail_x, back_got0), tail_k0.shape[0], tail_x, tail_got)
+    tail0, tail1 = part((tail_x,), SMALL + tail_k0.shape[0], tail_x, tail_got)
     tail_got0 = send_step(tail0, 0, 3)
     tail_got1 = send_step(tail1, 1, 3)
 
-    backs = list(hand((tail1,), back, 128, (256,)))
-    backs += hand((backs[0],), back, 384, (384, 256))
-    back_gots = [exchange(x, "tensor") for x in backs]
-
-    turn = backs[1]
+    back = gate((tail1,), *back)
+    back_got = [exchange(x, "tensor") for x in back]
+
+    turn = back[0]
     for step in (3, 2, 1):
-        sink = (back_gots[0],) if step == 2 else ()
-        other = (back_gots[1],) if step == 1 else ()
-        tail0 = join(place, (turn, tail1, *sink), (tail0, tail_got0, bit_slot(0, step)))
+        tail0 = join(
+            place, bit_slot(0, step), (turn, tail1), tail0, tail_got0, top=SMALL
+        )
         tail_got0 = send_step(tail0, 0, step - 1)
-        tail1 = join(place, (tail0, *other), (tail1, tail_got1, bit_slot(1, step)))
+        sink = (back_got[0],) if step == 1 else ()
+        tail1 = join(place, bit_slot(1, step), (tail0, *sink), tail1, tail_got1)
         tail_got1 = send_step(tail1, 1, step - 1)
-        if step == 3:
-            block_out = finish(
+        turn = tail1
+        if step == 2:
+            block_out, turn = finish(
                 "finish_out", (tail1,), (tokens,), mine, theirs, outer_shift[None]
             )
-            turn = block_out
-        if step == 2:
-            token_grad = finish(
-                "finish_grad", (tail1,), (tokens, cotangent), (back0, backs[0]),
-                (back_got0, back_gots[0]), gain, vmem=60,
-            )
-            turn = token_grad
-
-    up_out, down_out = spread((tail1,), gathered)
+
+    up_out, down_out, turn = spread((tail1,), gathered)
     down_out = down_out.reshape(hidden, width)
 
     near0, near1 = exchange(tail0, "core"), exchange(tail1, "core")
-    tail_got0, tail_got1 = hand_all((up_out,), tail_got0, tail_got1)
+    tail_got0, tail_got1 = gate((turn,), tail_got0, tail_got1)
     near_got0, near_got1 = exchange(tail_got0, "core"), exchange(tail_got1, "core")
-    token_grad = finish(
-        "finish_grad", (tail_got0,), (tokens, cotangent), (backs[1],), (back_gots[1],), gain,
-        start=384, into=token_grad, vmem=60,
+    token_grad, turn = finish(
+        "finish_grad", (tail_got0,), (tokens, cotangent), back[:1], back_got[:1], gain, vmem=60
     )
     own = (tail0, tail_got0, tail1, tail_got1)
     near = (near0, near_got0, near1, near_got1)
-    small = small_sums(place, (token_grad,), (*own[2:], *near[2:]))
-    pair = small[:4].reshape(2, width)
-    pair = pair + exchange(pair, "tensor")
+    small = small_sums((turn,), (*own[:2], *near[:2]))
+    small_got = exchange(small, "tensor")
     qkv_out, merge_out = assemble(place, (small,), (*own, *near), width)
-    token_grad = finish(
-        "finish_grad", (merge_out,), (tokens, cotangent), (backs[2],), (back_gots[2],), gain,
-        start=768, into=token_grad, vmem=60,
-    )
+    token_grad, _ = finish(
+        "finish_grad", (merge_out,), (tokens, cotangent), back[1:], back_got[1:], gain,
+        start=length // 2, into=token_grad, vmem=60,
+    )
+    pair = (small[:4] + small_got[:4]).reshape(2, width)
     return (
         block_out,
         token_grad,

time: 343 us -> 326 us (0.950)
  starting transfers between devices: 49.5 us -> 65.2 us
  waiting for transfers between devices: 65.2 us -> 52.9 us
  Pallas kernels: 182 us -> 171 us
  local copies, waits for them, and re-layouts: 26.4 us -> 15.8 us
    ppermute x17 -> x15, starting transfers between devices: 24.3 us -> 39.1 us  [exchange(): return lax.ppermute(x, axis, SWAP)]
    pallas_call x47 -> x42, Pallas kernels: 182 us -> 171 us  [launch(): pl.pallas_call(without, grid_spec=pltpu.PrefetchScalarGridSpec(num_scalar...]
    unnamed x124 -> x100, local copies, waits for them, and re-layouts: 25.1 us -> 15.1 us
    ppermute x24, waiting for transfers between devices: 48.4 us -> 39 us  [send_step(): return lax.ppermute(x, RINGS, step_pairs(part, step))]
    ppermute x17 -> x15, waiting for transfers between devices: 16.7 us -> 10.7 us  [exchange(): return lax.ppermute(x, axis, SWAP)]
  transfers between devices with their start and end apart: 42 -> 40, of which waited for: 14 -> 17; matrix products, arithmetic and copies ran while one was open for 0% -> 0% of each run, Pallas kernels for 41% -> 40%
where the time goes in v1:
time: 326 us; the launch traced here: 320 us
  Pallas kernels  171 us (52%)
  starting transfers between devices  65.2 us (20%)
  waiting for transfers between devices  52.9 us (16%)
  local copies, waits for them, and re-layouts  15.8 us (5%)
  between operations  15 us (5%)
    pallas_call x42, Pallas kernels, launch(): pl.pallas_call(without, grid_spec=pltpu.PrefetchScalarGridSpec(num_scalar...  171 us
    ppermute x15, starting transfers between devices, exchange(): return lax.ppermute(x, axis, SWAP)  39.1 us
    ppermute x24, waiting for transfers between devices, send_step(): return lax.ppermute(x, RINGS, step_pairs(part, step))  39 us
    ppermute x24, starting transfers between devices, send_step(): return lax.ppermute(x, RINGS, step_pairs(part, step))  26.1 us
    unnamed x100, local copies, waits for them, and re-layouts  15.1 us
    ppermute x15, waiting for transfers between devices, exchange(): return lax.ppermute(x, axis, SWAP)  10.7 us
  transfers between devices with their start and end apart: 40, of which 17 were waited for; matrix products, arithmetic and copies ran while one was open for 0% of the time, Pallas kernels for 40%

profile of v1, /device:TPU:1, one launch (start us, length us, event | category | flops | bytes accessed | tf_op | source)
XLA Modules:
  0.0 320.2 jit_solution(10809145319893070809)
XLA Ops:
  7.9 11.5 %project.1 = (bf16[1024,1024]{1,0:T(8,128)(2,1)}, bf16[1024,1024]{1,0:T(8,128)(2,1)}, bf16[1024,512]{1,0:T(8,128)(2,1)}, bf16[1024,512]{1,0:T(8,128)(2,1)}, bf16...) custom-call(bf16[1024,1024]{1,0:T(8,128)(2,1)} %refs_2_.9, f32[1,1024]{1,0:T(1,128)} %bitcast.34, ...), custom_call_target="tpu_custom_call" | custom-call | flops 4294967296 | bytes 17838080 | tf_op jit(solution)/shard_map/project/pallas_call | solution.py:57
  19.5 26.8 %hidden.1 = (f32[1024,1024]{1,0:T(8,128)}, f32[1024,1024]{1,0:T(8,128)}, bf16[1024,2048]{1,0:T(8,128)(2,1)}, bf16[1024,2048]{1,0:T(8,128)(2,1)}, f32[1,2048]{1,0:T(1,128)}) custom-call(f32[1,1024]{1,0:T(1,128)} %get-tuple-element.85.refs_0_.refs_6_, bf16[1024,1024]{1,0:T(8,128)(2,1)} %get-tuple-element.86.refs_1_, bf16[1024,1024]{1,0:T(8,128)(2,1)} %refs_3_.7, ...), custom_call_target="tpu_custom_call" | custom-call | flops 19327352832 | bytes 29376512 | tf_op jit(solution)/shard_map/hidden/pallas_call | solution.py:57
  49.2 3.8 %grad.4.refs_1_ = f32[16,64,1024]{2,1,0:T(8,128)S(1)} custom-call(s32[77]{0:T(128)S(1)} %dynamic-slice_bitcast_fusion.refs_0_, f32[1,2048]{1,0:T(1,128)S(1)} %copy-done.27, bf16[1024,2048]{1,0:T(8,128)(2,1)S(1)} %copy-done.9, bf16[1024,1024]{1,0:T(8,128)(2,1)S(1)} %copy-done.1), custom_call_target="tpu_custom_call" | custom-call | flops 2147483648 | bytes 10485760 | tf_op jit(solution)/shard_map/grad/pallas_call | solution.py:57
  54.6 3.8 %grad.5.refs_0_ = f32[16,64,1024]{2,1,0:T(8,128)S(1)} custom-call(s32[77]{0:T(128)S(1)} %dynamic-slice_bitcast_fusion.refs_0_, f32[16,64,1024]{2,1,0:T(8,128)S(1)} %grad.4.refs_1_, bf16[1024,1024]{1,0:T(8,128)(2,1)S(1)} %copy-done.13, bf16[1024,2048]{1,0:T(8,128)(2,1)S(1)} %copy-done.7), custom_call_target="tpu_custom_call" | custom-call | flops 2147483648 | bytes 10485760 | tf_op jit(solution)/shard_map/grad/pallas_call | solution.py:57
  59.0 8.7 %attend.2 = (bf16[512,512]{1,0:T(8,128)(2,1)S(1)}, bf16[512,512]{1,0:T(8,128)(2,1)S(1)}, f32[512,512]{1,0:T(8,128)S(1)}, f32[512,512]{1,0:T(8,128)S(1)}) custom-call(f32[16,64,1024]{2,1,0:T(8,128)S(1)} %grad.5.refs_0_, bf16[1024,512]{1,0:T(8,128)(2,1)S(1)} %copy-done.36, bf16[1024,512]{1,0:T(8,128)(2,1)S(1)} %copy-done.41, bf16[1024,512]{1,0:T(8,128)(2,1)S(1)} %copy-done.37, ...), custom_call_target="tpu_custom_call" | custom-call | flops 4026531840 | bytes 8388608 | tf_op jit(solution)/shard_map/attend/pallas_call | solution.py:57
  70.0 2.9 collective-permute-start.2
  73.0 5.5 %grad.6 = (f32[8,64,1024]{2,1,0:T(8,128)S(1)}, f32[8,64,1024]{2,1,0:T(8,128)}) custom-call(s32[77]{0:T(128)S(1)} %dynamic-slice_bitcast_fusion.refs_0_, f32[512,1024]{1,0:T(8,128)S(1)} %forward.2.refs_1_.refs_2_, bf16[1024,2048]{1,0:T(8,128)(2,1)S(1)} %copy-done.10, bf16[1024,1024]{1,0:T(8,128)(2,1)S(1)} %copy-done.1, ...), custom_call_target="tpu_custom_call" | custom-call | flops 2147483648 | bytes 14680064 | tf_op jit(solution)/shard_map/grad/pallas_call | solution.py:57
  80.4 6.0 %grad.7 = (f32[8,64,1024]{2,1,0:T(8,128)S(1)}, f32[8,64,1024]{2,1,0:T(8,128)}) custom-call(s32[77]{0:T(128)S(1)} %dynamic-slice_bitcast_fusion.refs_0_, f32[512,1024]{1,0:T(8,128)} %bitcast.5.refs_1_, bf16[1024,1024]{1,0:T(8,128)(2,1)S(1)} %copy-done.13, bf16[1024,2048]{1,0:T(8,128)(2,1)S(1)} %copy-done.7, f32[16,64,1024]{2,1,0:T(8,128)} %collective-permute-done.1.refs_4_), custom_call_target="tpu_custom_call" | custom-call | flops 2147483648 | bytes 14680064 | tf_op jit(solution)/shard_map/grad/pallas_call | solution.py:57
  90.4 17.3 %attend.3 = (bf16[512,512]{1,0:T(8,128)(2,1)S(1)}, bf16[512,512]{1,0:T(8,128)(2,1)S(1)}, bf16[1024,512]{1,0:T(8,128)(2,1)S(1)}, bf16[1024,512]{1,0:T(8,128)(2,1)S(1)}) custom-call(f32[512,1024]{1,0:T(8,128)} %bitcast.6.refs_0_, bf16[1024,512]{1,0:T(8,128)(2,1)S(1)} %copy-done.36, bf16[1024,512]{1,0:T(8,128)(2,1)S(1)} %copy-done.42, ...), custom_call_target="tpu_custom_call" | custom-call | flops 8053063680 | bytes 10485760 | tf_op jit(solution)/shard_map/attend/pallas_call | solution.py:57
  107.7 2.6 forward.3.refs_1_.refs_3_
  111.1 9.2 %tail.1 = (f32[1024,512]{1,0:T(8,128)S(1)}, f32[1024,512]{1,0:T(8,128)S(1)}, f32[1024,512]{1,0:T(8,128)}, f32[1024,512]{1,0:T(8,128)S(1)}) custom-call(s32[77]{0:T(128)S(1)} %dynamic-slice_bitcast_fusion.refs_0_, f32[512,1024]{1,0:T(8,128)} %forward.3.refs_1_.refs_3_, bf16[1024,1024]{1,0:T(8,128)(2,1)S(1)} %copy-done.14, bf16[512,512]{1,0:T(8,128)(2,1)S(1)} %copy-done.26, ...), custom_call_target="tpu_custom_call" | custom-call | flops 4294967296 | bytes 16777216 | tf_op jit(solution)/shard_map/tail/pallas_call | solution.py:57
  124.8 2.7 collective-permute-start.7
  135.8 10.6 %backward.1 = (f32[512,1024]{1,0:T(8,128)}, f32[512,1024]{1,0:T(8,128)}, f32[2,1024]{1,0:T(2,128)}) custom-call(f32[512,512]{1,0:T(8,128)} %get-tuple-element.115.refs_0_, bf16[512,512]{1,0:T(8,128)(2,1)} %copy-done.19, bf16[512,512]{1,0:T(8,128)(2,1)} %copy-done.20, bf16[1024,512]{1,0:T(8,128)(2,1)} %copy-done.23, bf16[1024,512]{1,0:T(8,128)(2,1)} %copy-done.24, ...), custom_call_target="tpu_custom_call" | custom-call | flops 3221225472 | bytes 16785408 | tf_op jit(solution)/shard_map/backward/pallas_call | solution.py:57
  159.7 3.2 %collective-permute-done.11.refs_3_.refs_5_ = f32[128,1024]{1,0:T(8,128)S(1)} collective-permute-done((f32[128,1024]{1,0:T(8,128)S(1)}, f32[128,1024]{1,0:T(8,128)S(1)}, u32[]{:S(2)}, u32[]{:S(2)}) %collective-permute-start.11) | collective-permute-done | bytes 524320 | tf_op jit(solution)/shard_map/ppermute | solution.py:1025
  166.6 3.0 collective-permute-done.13.refs_2_.refs_5_
  171.2 2.4 collective-permute-done.16.refs_2_
  174.0 2.6 collective-permute-start.18
  176.6 3.8 %collective-permute-done.18.refs_3_.refs_5_ = f32[128,512]{1,0:T(8,128)S(1)} collective-permute-done((f32[128,512]{1,0:T(8,128)S(1)}, f32[128,512]{1,0:T(8,128)S(1)}, u32[]{:S(2)}, u32[]{:S(2)}) %collective-permute-start.18) | collective-permute-done | bytes 262176 | tf_op jit(solution)/shard_map/ppermute | solution.py:1025
  182.7 2.3 collective-permute-done.20.refs_2_
  191.7 5.4 %collective-permute-done.23.refs_2_ = f32[144,512]{1,0:T(8,128)S(1)} collective-permute-done((f32[144,512]{1,0:T(8,128)S(1)}, f32[144,512]{1,0:T(8,128)S(1)}, u32[]{:S(2)}, u32[]{:S(2)}) %collective-permute-start.23) | collective-permute-done | bytes 294944 | tf_op jit(solution)/shard_map/ppermute | solution.py:1029
  201.4 4.1 %collective-permute-done.24.refs_4_ = f32[80,512]{1,0:T(8,128)S(1)} collective-permute-done((f32[80,512]{1,0:T(8,128)S(1)}, f32[80,512]{1,0:T(8,128)S(1)}, u32[]{:S(2)}, u32[]{:S(2)}) %collective-permute-start.24) | collective-permute-done | bytes 163872 | tf_op jit(solution)/shard_map/ppermute | solution.py:1025
  208.2 3.7 %collective-permute-start.26 = (f32[144,512]{1,0:T(8,128)S(1)}, f32[144,512]{1,0:T(8,128)S(1)}, u32[]{:S(2)}, u32[]{:S(2)}) collective-permute-start(f32[144,512]{1,0:T(8,128)S(1)} %join.6.refs_1_.refs_3_), channel_id=1, source_target_pairs={{0,12},{2,50},{4,8},{6,54},{8,4},{10,58},{12,0},{14,62},{16,28},{1... | collective-permute-start | bytes 884744 | tf_op jit(solution)/shard_map/ppermute | solution.py:1025
  213.0 5.0 %collective-permute-done.26.refs_4_ = f32[144,512]{1,0:T(8,128)S(1)} collective-permute-done((f32[144,512]{1,0:T(8,128)S(1)}, f32[144,512]{1,0:T(8,128)S(1)}, u32[]{:S(2)}, u32[]{:S(2)}) %collective-permute-start.26) | collective-permute-done | bytes 294944 | tf_op jit(solution)/shard_map/ppermute | solution.py:1025
  221.0 7.6 %finish_out.1 = (bf16[1024,1024]{1,0:T(8,128)(2,1)}, f32[8,128]{1,0:T(8,128)S(1)}) custom-call(f32[256,512]{1,0:T(8,128)S(1)} %join.9.refs_0_.refs_2_.refs_3_, bf16[1024,1024]{1,0:T(8,128)(2,1)S(1)} %copy-done, f32[512,1024]{1,0:T(8,128)S(1)} %copy-done.3, f32[512,1024]{1,0:T(8,128)} %forward.3.refs_1_.refs_3_, ...), custom_call_target="tpu_custom_call" | custom-call | bytes 12591104 | tf_op jit(solution)/shard_map/finish_out/pallas_call | solution.py:57
  228.6 11.9 %collective-permute-done.28.refs_4_ = f32[272,512]{1,0:T(8,128)S(1)} collective-permute-done((f32[272,512]{1,0:T(8,128)S(1)}, f32[272,512]{1,0:T(8,128)S(1)}, u32[]{:S(2)}, u32[]{:S(2)}) %collective-permute-start.28) | collective-permute-done | bytes 557088 | tf_op jit(solution)/shard_map/ppermute | solution.py:1025
  244.8 3.3 %collective-permute-start.37 = (f32[512,1024]{1,0:T(8,128)}, f32[512,1024]{1,0:T(8,128)}, u32[]{:S(2)}, u32[]{:S(2)}) collective-permute-start(f32[512,1024]{1,0:T(8,128)} %get-tuple-element.155.refs_4_), channel_id=1, source_target_pairs={{0,1},{1,0},{2,3},{3,2},{4,5},{5,4},{6,7},{7,6},{8,9},{9,8},{10,11... | collective-permute-start | bytes 6291464 | tf_op jit(solution)/shard_map/ppermute | solution.py:1029
  248.1 23.2 %collective-permute-start.33 = (f32[528,512]{1,0:T(8,128)S(1)}, f32[528,512]{1,0:T(8,128)S(1)}, u32[]{:S(2)}, u32[]{:S(2)}) collective-permute-start(f32[528,512]{1,0:T(8,128)S(1)} %join.10.refs_1_.refs_2_), channel_id=1, source_target_pairs={{0,2},{2,0},{1,3},{3,1},{4,6},{6,4},{5,7},{7,5},{8,10},{10,8},{9,1... | collective-permute-start | bytes 3244040 | tf_op jit(solution)/shard_map/ppermute | solution.py:1029
  271.3 3.1 all-gather.3.cloned.1.call-done
  274.4 12.6 %spread.1 = (f32[1024,2048]{1,0:T(8,128)}, f32[2,1024,1024]{2,1,0:T(8,128)}, f32[8,128]{1,0:T(8,128)}) custom-call(f32[512,512]{1,0:T(8,128)} %join.11.refs_0_.refs_4_, f32[32,128,1024]{2,1,0:T(8,128)} %bitcast.31), custom_call_target="tpu_custom_call" | custom-call | bytes 33558528 | tf_op jit(solution)/shard_map/spread/pallas_call | solution.py:57
  288.8 5.2 %finish_grad.2 = (bf16[1024,1024]{1,0:T(8,128)(2,1)}, f32[8,128]{1,0:T(8,128)}) custom-call(f32[528,512]{1,0:T(8,128)} %get-tuple-element.150.refs_0_.refs_2_.refs_3_, bf16[1024,1024]{1,0:T(8,128)(2,1)} %refs_2_.9, bf16[1024,1024]{1,0:T(8,128)(2,1)} %refs_3_.7, f32[512,1024]{1,0:T(8,128)} %get-tuple-element.145.refs_1_.refs_3_, f32[512,1024]{1,0:T(8,128)} %copy-done.15, ...), custom_call_target="tpu_custom_call" | custom-call | bytes 10493952 | tf_op jit(solution)/shard_map/finish_grad/pallas_call | solution.py:57
  298.0 8.2 %assemble.1 = (f32[3,1024,512]{2,1,0:T(8,128)}, f32[512,1024]{1,0:T(8,128)}) custom-call(s32[77]{0:T(128)S(1)} %dynamic-slice_bitcast_fusion.refs_0_, f32[16,512]{1,0:T(8,128)S(1)} %small_sums.1.refs_1_, f32[528,512]{1,0:T(8,128)S(1)} %join.10.refs_1_.refs_2_, f32[528,512]{1,0:T(8,128)S(1)} %copy-done.6, f32[512,512]{1,0:T(8,128)} %join.11.refs_0_.refs_4_, ...), custom_call_target="tpu_custom_call" | custom-call | bytes 16908288 | tf_op jit(solution)/shard_map/assemble/pallas_call | solution.py:57
  306.2 5.1 %finish_grad.3 = (bf16[1024,1024]{1,0:T(8,128)(2,1)}, f32[8,128]{1,0:T(8,128)}) custom-call(f32[512,1024]{1,0:T(8,128)} %get-tuple-element.80.refs_0_, bf16[1024,1024]{1,0:T(8,128)(2,1)} %get-tuple-element.154.refs_1_, bf16[1024,1024]{1,0:T(8,128)(2,1)} %refs_2_.9, bf16[1024,1024]{1,0:T(8,128)(2,1)} %refs_3_.7, ...), custom_call_target="tpu_custom_call", output_to_operand_aliasing={{0}: (1, {})} | custom-call | bytes 10493952 | tf_op jit(solution)/shard_map/finish_grad/pallas_call | solution.py:57
  (195 shorter events, 77.9 us)
Async XLA Ops:
  7.2 267.3 %all-gather.3.cloned.1.call-start = ((), (), s32[]{:S(2)}) async-start(), calls=%async_computation | async-start | bytes 17301504 | tf_op jit(solution)/shard_map/all_gather | solution.py:1130
  53.1 19.9 %collective-permute-start = (f32[16,64,1024]{2,1,0:T(8,128)S(1)}, f32[16,64,1024]{2,1,0:T(8,128)S(1)}, u32[]{:S(2)}, u32[]{:S(2)}) collective-permute-start(f32[16,64,1024]{2,1,0:T(8,128)S(1)} %grad.4.refs_1_), channel_id=1, source_target_pairs={{0,2},{2,0},{1,3},{3,1},{4,6},{6,4},{5,7},{7,5},{8,10},{10,8},{9,1... | collective-permute-start | bytes 12582920 | tf_op jit(solution)/shard_map/ppermute | solution.py:1029
  58.4 22.0 %collective-permute-start.1 = (f32[16,64,1024]{2,1,0:T(8,128)S(1)}, f32[16,64,1024]{2,1,0:T(8,128)}, u32[]{:S(2)}, u32[]{:S(2)}) collective-permute-start(f32[16,64,1024]{2,1,0:T(8,128)S(1)} %grad.5.refs_0_), channel_id=1, source_target_pairs={{0,2},{2,0},{1,3},{3,1},{4,6},{6,4},{5,7},{7,5},{8,10},{10,8},{9,1... | collective-permute-start | bytes 12582920 | tf_op jit(solution)/shard_map/ppermute | solution.py:1029
  70.0 51.1 %collective-permute-start.2 = (f32[512,1024]{1,0:T(8,128)S(1)}, f32[512,1024]{1,0:T(8,128)}, u32[]{:S(2)}, u32[]{:S(2)}) collective-permute-start(f32[512,1024]{1,0:T(8,128)S(1)} %forward.2.refs_1_.refs_2_), channel_id=1, source_target_pairs={{0,1},{1,0},{2,3},{3,2},{4,5},{5,4},{6,7},{7,6},{8,9},{9,8},{10,11... | collective-permute-start | bytes 6291464 | tf_op jit(solution)/shard_map/ppermute | solution.py:1029
  78.5 44.5 %collective-permute-start.3 = (f32[512,1024]{1,0:T(8,128)}, f32[512,1024]{1,0:T(8,128)S(1)}, u32[]{:S(2)}, u32[]{:S(2)}) collective-permute-start(f32[512,1024]{1,0:T(8,128)} %bitcast.5.refs_1_), channel_id=1, source_target_pairs={{0,4},{2,18},{4,0},{6,22},{8,12},{10,26},{12,8},{14,30},{16,20},{1... | collective-permute-start | bytes 6291464 | tf_op jit(solution)/shard_map/ppermute | solution.py:1025
  86.4 41.1 %collective-permute-start.4 = (f32[512,1024]{1,0:T(8,128)}, f32[512,1024]{1,0:T(8,128)S(1)}, u32[]{:S(2)}, u32[]{:S(2)}) collective-permute-start(f32[512,1024]{1,0:T(8,128)} %bitcast.6.refs_0_), channel_id=1, source_target_pairs={{0,12},{2,50},{4,8},{6,54},{8,4},{10,58},{12,0},{14,62},{16,28},{1... | collective-permute-start | bytes 6291464 | tf_op jit(solution)/shard_map/ppermute | solution.py:1025
  120.3 9.9 %collective-permute-start.5 = (f32[1024,512]{1,0:T(8,128)}, f32[1024,512]{1,0:T(8,128)S(1)}, u32[]{:S(2)}, u32[]{:S(2)}) collective-permute-start(f32[1024,512]{1,0:T(8,128)} %get-tuple-element.106.refs_1_), channel_id=1, source_target_pairs={{0,2},{2,0},{1,3},{3,1},{4,6},{6,4},{5,7},{7,5},{8,10},{10,8},{9,1... | collective-permute-start | bytes 6291464 | tf_op jit(solution)/shard_map/ppermute | solution.py:1029
  121.1 11.1 %collective-permute-start.6 = (f32[1024,512]{1,0:T(8,128)S(1)}, f32[1024,512]{1,0:T(8,128)S(1)}, u32[]{:S(2)}, u32[]{:S(2)}) collective-permute-start(f32[1024,512]{1,0:T(8,128)S(1)} %get-tuple-element.114), channel_id=1, source_target_pairs={{0,2},{2,0},{1,3},{3,1},{4,6},{6,4},{5,7},{7,5},{8,10},{10,8},{9,1... | collective-permute-start | bytes 6291464 | tf_op jit(solution)/shard_map/ppermute | solution.py:1029
  121.1 48.5 %collective-permute-start.13 = (f32[512,1024]{1,0:T(8,128)}, f32[512,1024]{1,0:T(8,128)}, u32[]{:S(2)}, u32[]{:S(2)}) collective-permute-start(f32[512,1024]{1,0:T(8,128)} %forward.3.refs_1_.refs_3_), channel_id=1, source_target_pairs={{0,1},{1,0},{2,3},{3,2},{4,5},{5,4},{6,7},{7,6},{8,9},{9,8},{10,11... | collective-permute-start | bytes 6291464 | tf_op jit(solution)/shard_map/ppermute | solution.py:1029
  124.8 21.6 %collective-permute-start.7 = (f32[256,1024]{1,0:T(8,128)}, f32[256,1024]{1,0:T(8,128)}, u32[]{:S(2)}, u32[]{:S(2)}) collective-permute-start(f32[256,1024]{1,0:T(8,128)} %get-tuple-element.108.refs_1_), channel_id=1, source_target_pairs={{0,16},{2,14},{4,20},{6,10},{8,24},{10,6},{12,28},{14,2},{16,0},{1... | collective-permute-start | bytes 3145736 | tf_op jit(solution)/shard_map/ppermute | solution.py:1025
  130.2 20.7 %collective-permute-start.8 = (f32[256,1024]{1,0:T(8,128)}, f32[256,1024]{1,0:T(8,128)}, u32[]{:S(2)}, u32[]{:S(2)}) collective-permute-start(f32[256,1024]{1,0:T(8,128)} %get-tuple-element.110.refs_1_), channel_id=1, source_target_pairs={{0,48},{2,6},{4,52},{6,2},{8,56},{10,14},{12,60},{14,10},{16,32},{... | collective-permute-start | bytes 3145736 | tf_op jit(solution)/shard_map/ppermute | solution.py:1025
  131.9 20.9 %collective-permute-start.9 = (f32[512,512]{1,0:T(8,128)}, f32[512,512]{1,0:T(8,128)}, u32[]{:S(2)}, u32[]{:S(2)}) collective-permute-start(f32[512,512]{1,0:T(8,128)} %get-tuple-element.112.refs_1_), channel_id=1, source_target_pairs={{0,4},{2,18},{4,0},{6,22},{8,12},{10,26},{12,8},{14,30},{16,20},{1... | collective-permute-start | bytes 3145736 | tf_op jit(solution)/shard_map/ppermute | solution.py:1025
  133.9 23.4 %collective-permute-start.10 = (f32[512,512]{1,0:T(8,128)}, f32[512,512]{1,0:T(8,128)}, u32[]{:S(2)}, u32[]{:S(2)}) collective-permute-start(f32[512,512]{1,0:T(8,128)} %get-tuple-element.115.refs_0_), channel_id=1, source_target_pairs={{0,12},{2,50},{4,8},{6,54},{8,4},{10,58},{12,0},{14,62},{16,28},{1... | collective-permute-start | bytes 3145736 | tf_op jit(solution)/shard_map/ppermute | solution.py:1025
  148.9 14.0 %collective-permute-start.11 = (f32[128,1024]{1,0:T(8,128)S(1)}, f32[128,1024]{1,0:T(8,128)S(1)}, u32[]{:S(2)}, u32[]{:S(2)}) collective-permute-start(f32[128,1024]{1,0:T(8,128)S(1)} %get-tuple-element.119.refs_1_), channel_id=1, source_target_pairs={{0,12},{2,50},{4,8},{6,54},{8,4},{10,58},{12,0},{14,62},{16,28},{1... | collective-permute-start | bytes 1572872 | tf_op jit(solution)/shard_map/ppermute | solution.py:1025
  152.7 11.4 %collective-permute-start.12 = (f32[128,1024]{1,0:T(8,128)S(1)}, f32[128,1024]{1,0:T(8,128)S(1)}, u32[]{:S(2)}, u32[]{:S(2)}) collective-permute-start(f32[128,1024]{1,0:T(8,128)S(1)} %get-tuple-element.121.refs_1_), channel_id=1, source_target_pairs={{0,4},{2,18},{4,0},{6,22},{8,12},{10,26},{12,8},{14,30},{16,20},{1... | collective-permute-start | bytes 1572872 | tf_op jit(solution)/shard_map/ppermute | solution.py:1025
  154.7 14.9 %collective-permute-start.14 = (f32[256,512]{1,0:T(8,128)S(1)}, f32[256,512]{1,0:T(8,128)S(1)}, u32[]{:S(2)}, u32[]{:S(2)}) collective-permute-start(f32[256,512]{1,0:T(8,128)S(1)} %get-tuple-element.123.refs_1_), channel_id=1, source_target_pairs={{0,16},{2,14},{4,20},{6,10},{8,24},{10,6},{12,28},{14,2},{16,0},{1... | collective-permute-start | bytes 1572872 | tf_op jit(solution)/shard_map/ppermute | solution.py:1025
  159.2 11.4 %collective-permute-start.15 = (f32[256,512]{1,0:T(8,128)S(1)}, f32[256,512]{1,0:T(8,128)S(1)}, u32[]{:S(2)}, u32[]{:S(2)}) collective-permute-start(f32[256,512]{1,0:T(8,128)S(1)} %get-tuple-element.125.refs_1_), channel_id=1, source_target_pairs={{0,48},{2,6},{4,52},{6,2},{8,56},{10,14},{12,60},{14,10},{16,32},{... | collective-permute-start | bytes 1572872 | tf_op jit(solution)/shard_map/ppermute | solution.py:1025
  163.6 10.0 %collective-permute-start.16 = (f32[64,1024]{1,0:T(8,128)S(1)}, f32[64,1024]{1,0:T(8,128)S(1)}, u32[]{:S(2)}, u32[]{:S(2)}) collective-permute-start(f32[64,1024]{1,0:T(8,128)S(1)} %get-tuple-element.127.refs_1_), channel_id=1, source_target_pairs={{0,48},{2,6},{4,52},{6,2},{8,56},{10,14},{12,60},{14,10},{16,32},{... | collective-permute-start | bytes 786440 | tf_op jit(solution)/shard_map/ppermute | solution.py:1025
  164.7 8.9 %collective-permute-start.17 = (f32[64,1024]{1,0:T(8,128)S(1)}, f32[64,1024]{1,0:T(8,128)S(1)}, u32[]{:S(2)}, u32[]{:S(2)}) collective-permute-start(f32[64,1024]{1,0:T(8,128)S(1)} %get-tuple-element.129.refs_1_), channel_id=1, source_target_pairs={{0,16},{2,14},{4,20},{6,10},{8,24},{10,6},{12,28},{14,2},{16,0},{1... | collective-permute-start | bytes 786440 | tf_op jit(solution)/shard_map/ppermute | solution.py:1025
  173.6 11.4 %collective-permute-start.20 = (f32[128,1024]{1,0:T(8,128)S(1)}, f32[128,1024]{1,0:T(8,128)S(1)}, u32[]{:S(2)}, u32[]{:S(2)}) collective-permute-start(f32[128,1024]{1,0:T(8,128)S(1)} %pack.2.refs_1_), channel_id=1, source_target_pairs={{0,64},{64,0},{1,65},{65,1},{2,66},{66,2},{3,67},{67,3},{4,68},{68... | collective-permute-start | bytes 1572872 | tf_op jit(solution)/shard_map/ppermute | solution.py:1029
  197.7 44.8 %collective-permute-start.29 = (f32[512,1024]{1,0:T(8,128)}, f32[512,1024]{1,0:T(8,128)S(1)}, u32[]{:S(2)}, u32[]{:S(2)}) collective-permute-start(f32[512,1024]{1,0:T(8,128)} %get-tuple-element.145.refs_1_.refs_3_), channel_id=1, source_target_pairs={{0,1},{1,0},{2,3},{3,2},{4,5},{5,4},{6,7},{7,6},{8,9},{9,8},{10,11... | collective-permute-start | bytes 6291464 | tf_op jit(solution)/shard_map/ppermute | solution.py:1029
  199.3 12.7 %collective-permute-start.25 = (f32[64,512]{1,0:T(8,128)S(1)}, f32[64,512]{1,0:T(8,128)S(1)}, u32[]{:S(2)}, u32[]{:S(2)}) collective-permute-start(f32[64,512]{1,0:T(8,128)S(1)} %copy-done.22), channel_id=1, source_target_pairs={{0,16},{2,14},{4,20},{6,10},{8,24},{10,6},{12,28},{14,2},{16,0},{1... | collective-permute-start | bytes 393224 | tf_op jit(solution)/shard_map/ppermute | solution.py:1025
  208.2 9.8 %collective-permute-start.26 = (f32[144,512]{1,0:T(8,128)S(1)}, f32[144,512]{1,0:T(8,128)S(1)}, u32[]{:S(2)}, u32[]{:S(2)}) collective-permute-start(f32[144,512]{1,0:T(8,128)S(1)} %join.6.refs_1_.refs_3_), channel_id=1, source_target_pairs={{0,12},{2,50},{4,8},{6,54},{8,4},{10,58},{12,0},{14,62},{16,28},{1... | collective-permute-start | bytes 884744 | tf_op jit(solution)/shard_map/ppermute | solution.py:1025
  218.7 21.9 %collective-permute-start.28 = (f32[272,512]{1,0:T(8,128)S(1)}, f32[272,512]{1,0:T(8,128)S(1)}, u32[]{:S(2)}, u32[]{:S(2)}) collective-permute-start(f32[272,512]{1,0:T(8,128)S(1)} %join.8.refs_1_.refs_3_), channel_id=1, source_target_pairs={{0,16},{2,14},{4,20},{6,10},{8,24},{10,6},{12,28},{14,2},{16,0},{1... | collective-permute-start | bytes 1671176 | tf_op jit(solution)/shard_map/ppermute | solution.py:1025
  220.7 21.8 %collective-permute-start.30 = (f32[256,512]{1,0:T(8,128)S(1)}, f32[256,512]{1,0:T(8,128)S(1)}, u32[]{:S(2)}, u32[]{:S(2)}) collective-permute-start(f32[256,512]{1,0:T(8,128)S(1)} %join.9.refs_0_.refs_2_.refs_3_), channel_id=1, source_target_pairs={{0,48},{2,6},{4,52},{6,2},{8,56},{10,14},{12,60},{14,10},{16,32},{... | collective-permute-start | bytes 1572872 | tf_op jit(solution)/shard_map/ppermute | solution.py:1025
  241.3 45.8 %collective-permute-start.31 = (f32[528,512]{1,0:T(8,128)S(1)}, f32[528,512]{1,0:T(8,128)S(1)}, u32[]{:S(2)}, u32[]{:S(2)}) collective-permute-start(f32[528,512]{1,0:T(8,128)S(1)} %join.10.refs_1_.refs_2_), channel_id=1, source_target_pairs={{0,4},{2,18},{4,0},{6,22},{8,12},{10,26},{12,8},{14,30},{16,20},{1... | collective-permute-start | bytes 3244040 | tf_op jit(solution)/shard_map/ppermute | solution.py:1025
  244.3 42.8 %collective-permute-start.32 = (f32[512,512]{1,0:T(8,128)}, f32[512,512]{1,0:T(8,128)}, u32[]{:S(2)}, u32[]{:S(2)}) collective-permute-start(f32[512,512]{1,0:T(8,128)} %join.11.refs_0_.refs_4_), channel_id=1, source_target_pairs={{0,12},{2,50},{4,8},{6,54},{8,4},{10,58},{12,0},{14,62},{16,28},{1... | collective-permute-start | bytes 3145736 | tf_op jit(solution)/shard_map/ppermute | solution.py:1025
  244.8 61.4 %collective-permute-start.37 = (f32[512,1024]{1,0:T(8,128)}, f32[512,1024]{1,0:T(8,128)}, u32[]{:S(2)}, u32[]{:S(2)}) collective-permute-start(f32[512,1024]{1,0:T(8,128)} %get-tuple-element.155.refs_4_), channel_id=1, source_target_pairs={{0,1},{1,0},{2,3},{3,2},{4,5},{5,4},{6,7},{7,6},{8,9},{9,8},{10,11... | collective-permute-start | bytes 6291464 | tf_op jit(solution)/shard_map/ppermute | solution.py:1029
  248.1 45.9 %collective-permute-start.33 = (f32[528,512]{1,0:T(8,128)S(1)}, f32[528,512]{1,0:T(8,128)S(1)}, u32[]{:S(2)}, u32[]{:S(2)}) collective-permute-start(f32[528,512]{1,0:T(8,128)S(1)} %join.10.refs_1_.refs_2_), channel_id=1, source_target_pairs={{0,2},{2,0},{1,3},{3,1},{4,6},{6,4},{5,7},{7,5},{8,10},{10,8},{9,1... | collective-permute-start | bytes 3244040 | tf_op jit(solution)/shard_map/ppermute | solution.py:1029
  288.3 9.7 %collective-permute-start.35 = (f32[512,512]{1,0:T(8,128)}, f32[512,512]{1,0:T(8,128)}, u32[]{:S(2)}, u32[]{:S(2)}) collective-permute-start(f32[512,512]{1,0:T(8,128)} %join.11.refs_0_.refs_4_), channel_id=1, source_target_pairs={{0,2},{2,0},{1,3},{3,1},{4,6},{6,4},{5,7},{7,5},{8,10},{10,8},{9,1... | collective-permute-start | bytes 3145736 | tf_op jit(solution)/shard_map/ppermute | solution.py:1029
  288.6 9.4 %collective-permute-start.36 = (f32[512,512]{1,0:T(8,128)}, f32[512,512]{1,0:T(8,128)}, u32[]{:S(2)}, u32[]{:S(2)}) collective-permute-start(f32[512,512]{1,0:T(8,128)} %get-tuple-element.152.refs_5_), channel_id=1, source_target_pairs={{0,2},{2,0},{1,3},{3,1},{4,6},{6,4},{5,7},{7,5},{8,10},{10,8},{9,1... | collective-permute-start | bytes 3145736 | tf_op jit(solution)/shard_map/ppermute | solution.py:1029
  295.5 15.8 %collective-permute-start.38 = (f32[16,512]{1,0:T(8,128)S(1)}, f32[16,512]{1,0:T(8,128)S(1)}, u32[]{:S(2)}, u32[]{:S(2)}) collective-permute-start(f32[16,512]{1,0:T(8,128)S(1)} %small_sums.1.refs_1_), channel_id=1, source_target_pairs={{0,1},{1,0},{2,3},{3,2},{4,5},{5,4},{6,7},{7,6},{8,9},{9,8},{10,11... | collective-permute-start | bytes 98312 | tf_op jit(solution)/shard_map/ppermute | solution.py:1029
  (55 other events, 343.8 us)
Sparse Core Ops, SparseCore 0:
  186.0 88.3 all-gather.2

commit v2 on v1

--- a/solution.py
+++ b/solution.py
@@ -47,8 +47,8 @@
 
 
 def launch(kernel, name, grid, scalars, after, ins, outs, scratch=(), vmem=16, flops=0, into=None):
-    if into is not None:
-        after = (*after, into)
+    into = into or {}
+    after = (*after, *into.values())
     first, skipped = len(scalars), len(after)
 
     def without(*refs):
@@ -65,7 +65,9 @@
         ),
         out_shape=[jax.ShapeDtypeStruct(shape, dtype) for shape, dtype, _ in outs],
         compiler_params=pltpu.CompilerParams(vmem_limit_bytes=vmem << 20),
-        input_output_aliases={} if into is None else {first + skipped - 1: 0},
+        input_output_aliases={
+            first + skipped - len(into) + i: out for i, out in enumerate(into)
+        },
         cost_estimate=pl.CostEstimate(
             flops=flops,
             bytes_accessed=sum(x.size * x.dtype.itemsize for x, _ in ins)
@@ -813,27 +815,56 @@
     )[0]
 
 
-def assemble_kernel(place, *refs):
-    arrays, (qkv, merge) = refs[:8], refs[8:]
-    count = qkv.shape[1]
-    j, t = pl.program_id(0), pl.program_id(1)
-    core = place[0]
-    for other in range(2):
-        for p in range(2):
-            bit = place[bit_slot(p, 0)] if other == 0 else place[NEAR + p]
-            for half in range(2):
-                x = arrays[4 * other + 2 * p + half]
-                mine = (j == 2 * (core if other == 0 else 1 - core) + p) & (
-                    t == (bit if half == 0 else 1 - bit)
-                )
-
-                @pl.when(mine & (j < 3))
-                def _():
-                    qkv[0] = x[x.shape[0] - count :, :]
-
-                @pl.when(mine & (j == 3))
-                def _():
-                    merge[...] = x[x.shape[0] - count :, :]
+def place_kernel(place, *refs, pieces, rows):
+    srcs, (qkv, merge, token, buf, in_sems, out_sems) = refs[: len(pieces)], refs[len(pieces) :]
+    token[...] = jnp.zeros_like(token)
+    arriving = [
+        pltpu.make_async_copy(src.at[pl.ds(src.shape[0] - rows, rows)], buf.at[i], in_sems.at[i])
+        for i, src in enumerate(srcs)
+    ]
+    for copy in arriving:
+        copy.start()
+    for i, (near, part, mine) in enumerate(pieces):
+        j = 2 * (1 - place[0] if near else place[0]) + part
+        bit = place[NEAR + part] if near else place[bit_slot(part, 0)]
+        start = pl.multiple_of((bit if mine else 1 - bit) * rows, rows)
+        arriving[i].wait()
+
+        @pl.when(j < 3)
+        def _():
+            pltpu.make_async_copy(
+                buf.at[i], qkv.at[jnp.minimum(j, 2), pl.ds(start, rows)], out_sems.at[i]
+            ).start()
+
+        @pl.when(j == 3)
+        def _():
+            pltpu.make_async_copy(
+                buf.at[i], merge.at[:, pl.ds(start, rows)], out_sems.at[i]
+            ).start()
+
+    for i in range(len(pieces)):
+        pltpu.make_async_copy(buf.at[i], qkv.at[0, pl.ds(0, rows)], out_sems.at[i]).wait()
+
+
+def place_pieces(place, after, arrays, pieces, width, into=None):
+    local = arrays[0].shape[1]
+    rows = width // 2
+    anywhere = pl.BlockSpec(memory_space=pltpu.HBM)
+    return launch(
+        functools.partial(place_kernel, pieces=pieces, rows=rows),
+        "place",
+        (1,),
+        (place,),
+        after,
+        [(x, anywhere) for x in arrays],
+        [((3, width, local), F32, anywhere), ((local, width), F32, anywhere), TOKEN],
+        [
+            pltpu.VMEM((len(arrays), rows, local), F32),
+            pltpu.SemaphoreType.DMA((len(arrays),)),
+            pltpu.SemaphoreType.DMA((len(arrays),)),
+        ],
+        into=into,
+    )
 
 
 def small_kernel(own0, own1, near0, near1, out):
@@ -852,35 +883,6 @@
         [(x, top) for x in arrays],
         [((SMALL, width), F32, whole(SMALL, width))],
     )[0]
-
-
-def assemble(place, after, arrays, width):
-    local = arrays[0].shape[1]
-    half = width // 2
-    return launch(
-        assemble_kernel,
-        "assemble",
-        (4, 2),
-        (place,),
-        after,
-        [(x, once(*x.shape)) for x in arrays],
-        [
-            (
-                (3, width, local),
-                F32,
-                pl.BlockSpec(
-                    (1, half, local),
-                    lambda j, t, _: (jnp.minimum(j, 2), jnp.where(j < 3, t, 1), 0),
-                ),
-            ),
-            (
-                (local, width),
-                F32,
-                pl.BlockSpec((local, half), lambda j, t, _: (0, jnp.where(j < 3, 0, t))),
-            ),
-        ],
-        vmem=40,
-    )
 
 
 def spread_kernel(gathered, up, down, token, buf, in_sems, out_sems):
@@ -1156,23 +1158,35 @@
                 "finish_out", (tail1,), (tokens,), mine, theirs, outer_shift[None]
             )
 
-    up_out, down_out, turn = spread((tail1,), gathered)
+    token_grad, turn = finish(
+        "finish_grad", (tail1,), (tokens, cotangent), back[:1], back_got[:1], gain, vmem=60
+    )
+    near0, near1 = exchange(tail0, "core"), exchange(tail1, "core")
+    up_out, down_out, turn = spread((turn, near0, near1), gathered)
     down_out = down_out.reshape(hidden, width)
-
-    near0, near1 = exchange(tail0, "core"), exchange(tail1, "core")
     tail_got0, tail_got1 = gate((turn,), tail_got0, tail_got1)
     near_got0, near_got1 = exchange(tail_got0, "core"), exchange(tail_got1, "core")
-    token_grad, turn = finish(
-        "finish_grad", (tail_got0,), (tokens, cotangent), back[:1], back_got[:1], gain, vmem=60
-    )
-    own = (tail0, tail_got0, tail1, tail_got1)
-    near = (near0, near_got0, near1, near_got1)
-    small = small_sums((turn,), (*own[:2], *near[:2]))
+    kinds = [(near, part) for near in (False, True) for part in range(2)]
+    qkv_out, merge_out, turn = place_pieces(
+        place,
+        (tail_got0,),
+        (tail0, tail1, near0, near1),
+        [(*kind, True) for kind in kinds],
+        width,
+    )
+    small = small_sums((turn,), (tail0, tail_got0, near0, near_got0))
     small_got = exchange(small, "tensor")
-    qkv_out, merge_out = assemble(place, (small,), (*own, *near), width)
+    qkv_out, merge_out, turn = place_pieces(
+        place,
+        (small,),
+        (tail_got0, tail_got1, near_got0, near_got1),
+        [(*kind, False) for kind in kinds],
+        width,
+        into={0: qkv_out, 1: merge_out},
+    )
     token_grad, _ = finish(
-        "finish_grad", (merge_out,), (tokens, cotangent), back[1:], back_got[1:], gain,
-        start=length // 2, into=token_grad, vmem=60,
+        "finish_grad", (turn,), (tokens, cotangent), back[1:], back_got[1:], gain,
+        start=length // 2, into={0: token_grad}, vmem=60,
     )
     pair = (small[:4] + small_got[:4]).reshape(2, width)
     return (

time: 326 us -> 329 us (level)
  the two profiles are of different devices: /device:TPU:1 before, /device:TPU:18 now
where the time goes in v2:
time: 329 us; the launch traced here: 325 us
  Pallas kernels  169 us (51%)
  waiting for transfers between devices  76.5 us (23%)
  starting transfers between devices  45.8 us (14%)
  local copies, waits for them, and re-layouts  18.1 us (6%)
  between operations  15.1 us (5%)
    pallas_call x43, Pallas kernels, launch(): pl.pallas_call(without, grid_spec=pltpu.PrefetchScalarGridSpec(num_scalar...  169 us
    ppermute x24, waiting for transfers between devices, send_step(): return lax.ppermute(x, RINGS, step_pairs(part, step))  47.4 us
    ppermute x24, starting transfers between devices, send_step(): return lax.ppermute(x, RINGS, step_pairs(part, step))  29.7 us
    ppermute x15, waiting for transfers between devices, exchange(): return lax.ppermute(x, axis, SWAP)  29 us
    unnamed x106, local copies, waits for them, and re-layouts  17.4 us
    ppermute x15, starting transfers between devices, exchange(): return lax.ppermute(x, axis, SWAP)  16 us
  transfers between devices with their start and end apart: 40, of which 16 were waited for; matrix products, arithmetic and copies ran while one was open for 0% of the time, Pallas kernels for 39%

profile of v2, /device:TPU:18, one launch (start us, length us, event | category | flops | bytes accessed | tf_op | source)
XLA Modules:
  0.0 324.7 jit_solution(1391137896428429381)
XLA Ops:
  7.9 11.5 %project.1 = (bf16[1024,1024]{1,0:T(8,128)(2,1)}, bf16[1024,1024]{1,0:T(8,128)(2,1)}, bf16[1024,512]{1,0:T(8,128)(2,1)}, bf16[1024,512]{1,0:T(8,128)(2,1)}, bf16...) custom-call(bf16[1024,1024]{1,0:T(8,128)(2,1)} %refs_2_.9, f32[1,1024]{1,0:T(1,128)} %bitcast.35, ...), custom_call_target="tpu_custom_call" | custom-call | flops 4294967296 | bytes 17838080 | tf_op jit(solution)/shard_map/project/pallas_call | solution.py:57
  19.4 26.9 %hidden.1 = (f32[1024,1024]{1,0:T(8,128)}, f32[1024,1024]{1,0:T(8,128)}, bf16[1024,2048]{1,0:T(8,128)(2,1)}, bf16[1024,2048]{1,0:T(8,128)(2,1)}, f32[1,2048]{1,0:T(1,128)}) custom-call(f32[1,1024]{1,0:T(1,128)} %get-tuple-element.89.refs_0_.refs_6_, bf16[1024,1024]{1,0:T(8,128)(2,1)} %get-tuple-element.90.refs_1_, bf16[1024,1024]{1,0:T(8,128)(2,1)} %refs_3_.7, ...), custom_call_target="tpu_custom_call" | custom-call | flops 19327352832 | bytes 29376512 | tf_op jit(solution)/shard_map/hidden/pallas_call | solution.py:57
  49.2 3.8 %grad.4.refs_1_ = f32[16,64,1024]{2,1,0:T(8,128)S(1)} custom-call(s32[77]{0:T(128)S(1)} %dynamic-slice_bitcast_fusion.refs_0_, f32[1,2048]{1,0:T(1,128)S(1)} %copy-done.30, bf16[1024,2048]{1,0:T(8,128)(2,1)S(1)} %copy-done.10, bf16[1024,1024]{1,0:T(8,128)(2,1)S(1)} %copy-done.1), custom_call_target="tpu_custom_call" | custom-call | flops 2147483648 | bytes 10485760 | tf_op jit(solution)/shard_map/grad/pallas_call | solution.py:57
  53.2 3.8 %grad.5.refs_0_ = f32[16,64,1024]{2,1,0:T(8,128)S(1)} custom-call(s32[77]{0:T(128)S(1)} %dynamic-slice_bitcast_fusion.refs_0_, f32[16,64,1024]{2,1,0:T(8,128)S(1)} %grad.4.refs_1_, bf16[1024,1024]{1,0:T(8,128)(2,1)S(1)} %copy-done.16, bf16[1024,2048]{1,0:T(8,128)(2,1)S(1)} %copy-done.8), custom_call_target="tpu_custom_call" | custom-call | flops 2147483648 | bytes 10485760 | tf_op jit(solution)/shard_map/grad/pallas_call | solution.py:57
  58.0 8.7 %attend.2 = (bf16[512,512]{1,0:T(8,128)(2,1)S(1)}, bf16[512,512]{1,0:T(8,128)(2,1)S(1)}, f32[512,512]{1,0:T(8,128)S(1)}, f32[512,512]{1,0:T(8,128)S(1)}) custom-call(f32[16,64,1024]{2,1,0:T(8,128)S(1)} %grad.5.refs_0_, bf16[1024,512]{1,0:T(8,128)(2,1)S(1)} %copy-done.39, bf16[1024,512]{1,0:T(8,128)(2,1)S(1)} %copy-done.44, bf16[1024,512]{1,0:T(8,128)(2,1)S(1)} %copy-done.40, ...), custom_call_target="tpu_custom_call" | custom-call | flops 4026531840 | bytes 8388608 | tf_op jit(solution)/shard_map/attend/pallas_call | solution.py:57
  71.3 5.5 %grad.6 = (f32[8,64,1024]{2,1,0:T(8,128)S(1)}, f32[8,64,1024]{2,1,0:T(8,128)}) custom-call(s32[77]{0:T(128)S(1)} %dynamic-slice_bitcast_fusion.refs_0_, f32[512,1024]{1,0:T(8,128)S(1)} %forward.2.refs_1_.refs_2_, bf16[1024,2048]{1,0:T(8,128)(2,1)S(1)} %copy-done.11, bf16[1024,1024]{1,0:T(8,128)(2,1)S(1)} %copy-done.1, ...), custom_call_target="tpu_custom_call" | custom-call | flops 2147483648 | bytes 14680064 | tf_op jit(solution)/shard_map/grad/pallas_call | solution.py:57
  78.3 5.6 %grad.7 = (f32[8,64,1024]{2,1,0:T(8,128)S(1)}, f32[8,64,1024]{2,1,0:T(8,128)}) custom-call(s32[77]{0:T(128)S(1)} %dynamic-slice_bitcast_fusion.refs_0_, f32[512,1024]{1,0:T(8,128)} %bitcast.5.refs_1_, bf16[1024,1024]{1,0:T(8,128)(2,1)S(1)} %copy-done.16, bf16[1024,2048]{1,0:T(8,128)(2,1)S(1)} %copy-done.8, f32[16,64,1024]{2,1,0:T(8,128)} %collective-permute-done.1.refs_4_), custom_call_target="tpu_custom_call" | custom-call | flops 2147483648 | bytes 14680064 | tf_op jit(solution)/shard_map/grad/pallas_call | solution.py:57
  86.5 17.3 %attend.3 = (bf16[512,512]{1,0:T(8,128)(2,1)S(1)}, bf16[512,512]{1,0:T(8,128)(2,1)S(1)}, bf16[1024,512]{1,0:T(8,128)(2,1)S(1)}, bf16[1024,512]{1,0:T(8,128)(2,1)S(1)}) custom-call(f32[512,1024]{1,0:T(8,128)} %bitcast.6.refs_0_, bf16[1024,512]{1,0:T(8,128)(2,1)S(1)} %copy-done.39, bf16[1024,512]{1,0:T(8,128)(2,1)S(1)} %copy-done.45, ...), custom_call_target="tpu_custom_call" | custom-call | flops 8053063680 | bytes 10485760 | tf_op jit(solution)/shard_map/attend/pallas_call | solution.py:57
  103.9 2.6 forward.3.refs_1_.refs_3_
  107.2 9.1 %tail.1 = (f32[1024,512]{1,0:T(8,128)S(1)}, f32[1024,512]{1,0:T(8,128)S(1)}, f32[1024,512]{1,0:T(8,128)}, f32[1024,512]{1,0:T(8,128)S(1)}) custom-call(s32[77]{0:T(128)S(1)} %dynamic-slice_bitcast_fusion.refs_0_, f32[512,1024]{1,0:T(8,128)} %forward.3.refs_1_.refs_3_, bf16[1024,1024]{1,0:T(8,128)(2,1)S(1)} %copy-done.17, bf16[512,512]{1,0:T(8,128)(2,1)S(1)} %copy-done.29, ...), custom_call_target="tpu_custom_call" | custom-call | flops 4294967296 | bytes 16777216 | tf_op jit(solution)/shard_map/tail/pallas_call | solution.py:57
  126.8 2.5 collective-permute-start.8
  134.7 10.6 %backward.1 = (f32[512,1024]{1,0:T(8,128)}, f32[512,1024]{1,0:T(8,128)}, f32[2,1024]{1,0:T(2,128)}) custom-call(f32[512,512]{1,0:T(8,128)} %get-tuple-element.119.refs_0_, bf16[512,512]{1,0:T(8,128)(2,1)} %copy-done.22, bf16[512,512]{1,0:T(8,128)(2,1)} %copy-done.23, bf16[1024,512]{1,0:T(8,128)(2,1)} %copy-done.26, bf16[1024,512]{1,0:T(8,128)(2,1)} %copy-done.27, ...), custom_call_target="tpu_custom_call" | custom-call | flops 3221225472 | bytes 16785408 | tf_op jit(solution)/shard_map/backward/pallas_call | solution.py:57
  158.5 3.0 collective-permute-start.15
  162.5 2.5 collective-permute-done.12.refs_3_.refs_5_
  165.7 2.9 collective-permute-done.13.refs_2_.refs_5_
  173.8 2.5 collective-permute-start.19
  176.3 3.6 %collective-permute-done.18.refs_3_.refs_5_ = f32[128,512]{1,0:T(8,128)S(1)} collective-permute-done((f32[128,512]{1,0:T(8,128)S(1)}, f32[128,512]{1,0:T(8,128)S(1)}, u32[]{:S(2)}, u32[]{:S(2)}) %collective-permute-start.18) | collective-permute-done | bytes 262176 | tf_op jit(solution)/shard_map/ppermute | solution.py:1027
  181.2 3.1 collective-permute-done.20.refs_2_
  185.2 2.8 collective-permute-start.21
  188.1 3.6 %collective-permute-done.21.refs_2_ = f32[64,512]{1,0:T(8,128)S(1)} collective-permute-done((f32[64,512]{1,0:T(8,128)S(1)}, f32[64,512]{1,0:T(8,128)S(1)}, u32[]{:S(2)}, u32[]{:S(2)}) %collective-permute-start.21) | collective-permute-done | bytes 131104 | tf_op jit(solution)/shard_map/ppermute | solution.py:1027
  194.6 7.2 %collective-permute-done.23.refs_2_ = f32[144,512]{1,0:T(8,128)S(1)} collective-permute-done((f32[144,512]{1,0:T(8,128)S(1)}, f32[144,512]{1,0:T(8,128)S(1)}, u32[]{:S(2)}, u32[]{:S(2)}) %collective-permute-start.23) | collective-permute-done | bytes 294944 | tf_op jit(solution)/shard_map/ppermute | solution.py:1031
  203.5 9.7 %collective-permute-done.24.refs_4_ = f32[80,512]{1,0:T(8,128)S(1)} collective-permute-done((f32[80,512]{1,0:T(8,128)S(1)}, f32[80,512]{1,0:T(8,128)S(1)}, u32[]{:S(2)}, u32[]{:S(2)}) %collective-permute-start.24) | collective-permute-done | bytes 163872 | tf_op jit(solution)/shard_map/ppermute | solution.py:1027
  220.1 9.8 %collective-permute-done.26.refs_4_ = f32[144,512]{1,0:T(8,128)S(1)} collective-permute-done((f32[144,512]{1,0:T(8,128)S(1)}, f32[144,512]{1,0:T(8,128)S(1)}, u32[]{:S(2)}, u32[]{:S(2)}) %collective-permute-start.26) | collective-permute-done | bytes 294944 | tf_op jit(solution)/shard_map/ppermute | solution.py:1027
  233.1 7.3 %finish_out.1 = (bf16[1024,1024]{1,0:T(8,128)(2,1)}, f32[8,128]{1,0:T(8,128)S(1)}) custom-call(f32[256,512]{1,0:T(8,128)S(1)} %join.9.refs_0_.refs_2_.refs_3_, bf16[1024,1024]{1,0:T(8,128)(2,1)S(1)} %copy-done, f32[512,1024]{1,0:T(8,128)S(1)} %copy-done.3, f32[512,1024]{1,0:T(8,128)} %forward.3.refs_1_.refs_3_, ...), custom_call_target="tpu_custom_call" | custom-call | bytes 12591104 | tf_op jit(solution)/shard_map/finish_out/pallas_call | solution.py:57
  240.3 11.7 %collective-permute-done.28.refs_4_ = f32[272,512]{1,0:T(8,128)S(1)} collective-permute-done((f32[272,512]{1,0:T(8,128)S(1)}, f32[272,512]{1,0:T(8,128)S(1)}, u32[]{:S(2)}, u32[]{:S(2)}) %collective-permute-start.28) | collective-permute-done | bytes 557088 | tf_op jit(solution)/shard_map/ppermute | solution.py:1027
  252.9 5.7 %collective-permute-start.33 = (f32[528,512]{1,0:T(8,128)S(1)}, f32[528,512]{1,0:T(8,128)S(1)}, u32[]{:S(2)}, u32[]{:S(2)}) collective-permute-start(f32[528,512]{1,0:T(8,128)S(1)} %join.10.refs_1_.refs_2_), channel_id=1, source_target_pairs={{0,4},{2,18},{4,0},{6,22},{8,12},{10,26},{12,8},{14,30},{16,20},{1... | collective-permute-start | bytes 3244040 | tf_op jit(solution)/shard_map/ppermute | solution.py:1027
  262.7 5.1 %finish_grad.2 = (bf16[1024,1024]{1,0:T(8,128)(2,1)}, f32[8,128]{1,0:T(8,128)}) custom-call(f32[512,512]{1,0:T(8,128)} %join.11.refs_0_.refs_3_, bf16[1024,1024]{1,0:T(8,128)(2,1)} %refs_2_.9, bf16[1024,1024]{1,0:T(8,128)(2,1)} %refs_3_.7, f32[512,1024]{1,0:T(8,128)} %get-tuple-element.149.refs_1_.refs_3_, f32[512,1024]{1,0:T(8,128)} %copy-done.18, ...), custom_call_target="tpu_custom_call" | custom-call | bytes 10493952 | tf_op jit(solution)/shard_map/finish_grad/pallas_call | solution.py:57
  268.8 12.6 %spread.1 = (f32[1024,2048]{1,0:T(8,128)}, f32[2,1024,1024]{2,1,0:T(8,128)}, f32[8,128]{1,0:T(8,128)}) custom-call(f32[8,128]{1,0:T(8,128)} %get-tuple-element.153.refs_0_, f32[528,512]{1,0:T(8,128)} %copy-done.12, f32[512,512]{1,0:T(8,128)} %collective-permute-done.32.refs_2_.refs_5_, f32[32,128,1024]{2,1,0:T(8,128)} %bitcast.31), custom_call_target="tpu_custom_call" | custom-call | bytes 33558528 | tf_op jit(solution)/shard_map/spread/pallas_call | solution.py:57
  284.3 3.9 %place.2 = (f32[3,1024,512]{2,1,0:T(8,128)}, f32[512,1024]{1,0:T(8,128)}, f32[8,128]{1,0:T(8,128)S(1)}) custom-call(s32[77]{0:T(128)S(1)} %dynamic-slice_bitcast_fusion.refs_0_, f32[528,512]{1,0:T(8,128)S(1)} %copy-done.6, f32[528,512]{1,0:T(8,128)S(1)} %join.10.refs_1_.refs_2_, f32[512,512]{1,0:T(8,128)} %join.11.refs_0_.refs_3_, ...), custom_call_target="tpu_custom_call" | custom-call | bytes 12652544 | tf_op jit(solution)/shard_map/place/pallas_call | solution.py:57
  290.4 3.9 %place.3 = (f32[3,1024,512]{2,1,0:T(8,128)}, f32[512,1024]{1,0:T(8,128)}, f32[8,128]{1,0:T(8,128)S(1)}) custom-call(s32[77]{0:T(128)S(1)} %dynamic-slice_bitcast_fusion.refs_0_, f32[16,512]{1,0:T(8,128)S(1)} %small_sums.1.refs_1_, f32[3,1024,512]{2,1,0:T(8,128)} %get-tuple-element.157.refs_2_, ...), custom_call_target="tpu_custom_call", output_to_operand_aliasing={{0}: (2, {}), {1}: (3, {})} | custom-call | bytes 12652544 | tf_op jit(solution)/shard_map/place/pallas_call | solution.py:57
  295.0 15.7 %collective-permute-done.37.refs_5_ = f32[512,1024]{1,0:T(8,128)} collective-permute-done((f32[512,1024]{1,0:T(8,128)}, f32[512,1024]{1,0:T(8,128)}, u32[]{:S(2)}, u32[]{:S(2)}) %collective-permute-start.37) | collective-permute-done | bytes 2097184 | tf_op jit(solution)/shard_map/ppermute | solution.py:1031
  310.7 5.1 %finish_grad.3 = (bf16[1024,1024]{1,0:T(8,128)(2,1)}, f32[8,128]{1,0:T(8,128)}) custom-call(f32[8,128]{1,0:T(8,128)} %copy-done.36, bf16[1024,1024]{1,0:T(8,128)(2,1)} %get-tuple-element.161.refs_1_, bf16[1024,1024]{1,0:T(8,128)(2,1)} %refs_2_.9, bf16[1024,1024]{1,0:T(8,128)(2,1)} %refs_3_.7, ...), custom_call_target="tpu_custom_call", output_to_operand_aliasing={{0}: (1, {})} | custom-call | bytes 10493952 | tf_op jit(solution)/shard_map/finish_grad/pallas_call | solution.py:57
  (202 shorter events, 79.8 us)
Async XLA Ops:
  7.2 260.7 %all-gather.3.cloned.1.call-start = ((), (), s32[]{:S(2)}) async-start(), calls=%async_computation | async-start | bytes 17301504 | tf_op jit(solution)/shard_map/all_gather | solution.py:1132
  53.0 18.2 %collective-permute-start = (f32[16,64,1024]{2,1,0:T(8,128)S(1)}, f32[16,64,1024]{2,1,0:T(8,128)S(1)}, u32[]{:S(2)}, u32[]{:S(2)}) collective-permute-start(f32[16,64,1024]{2,1,0:T(8,128)S(1)} %grad.4.refs_1_), channel_id=1, source_target_pairs={{0,2},{2,0},{1,3},{3,1},{4,6},{6,4},{5,7},{7,5},{8,10},{10,8},{9,1... | collective-permute-start | bytes 12582920 | tf_op jit(solution)/shard_map/ppermute | solution.py:1031
  57.0 21.3 %collective-permute-start.1 = (f32[16,64,1024]{2,1,0:T(8,128)S(1)}, f32[16,64,1024]{2,1,0:T(8,128)}, u32[]{:S(2)}, u32[]{:S(2)}) collective-permute-start(f32[16,64,1024]{2,1,0:T(8,128)S(1)} %grad.5.refs_0_), channel_id=1, source_target_pairs={{0,2},{2,0},{1,3},{3,1},{4,6},{6,4},{5,7},{7,5},{8,10},{10,8},{9,1... | collective-permute-start | bytes 12582920 | tf_op jit(solution)/shard_map/ppermute | solution.py:1031
  69.0 49.7 %collective-permute-start.2 = (f32[512,1024]{1,0:T(8,128)S(1)}, f32[512,1024]{1,0:T(8,128)}, u32[]{:S(2)}, u32[]{:S(2)}) collective-permute-start(f32[512,1024]{1,0:T(8,128)S(1)} %forward.2.refs_1_.refs_2_), channel_id=1, source_target_pairs={{0,1},{1,0},{2,3},{3,2},{4,5},{5,4},{6,7},{7,6},{8,9},{9,8},{10,11... | collective-permute-start | bytes 6291464 | tf_op jit(solution)/shard_map/ppermute | solution.py:1031
  76.9 44.0 %collective-permute-start.3 = (f32[512,1024]{1,0:T(8,128)}, f32[512,1024]{1,0:T(8,128)S(1)}, u32[]{:S(2)}, u32[]{:S(2)}) collective-permute-start(f32[512,1024]{1,0:T(8,128)} %bitcast.5.refs_1_), channel_id=1, source_target_pairs={{0,4},{2,18},{4,0},{6,22},{8,12},{10,26},{12,8},{14,30},{16,20},{1... | collective-permute-start | bytes 6291464 | tf_op jit(solution)/shard_map/ppermute | solution.py:1027
  83.9 40.2 %collective-permute-start.4 = (f32[512,1024]{1,0:T(8,128)}, f32[512,1024]{1,0:T(8,128)S(1)}, u32[]{:S(2)}, u32[]{:S(2)}) collective-permute-start(f32[512,1024]{1,0:T(8,128)} %bitcast.6.refs_0_), channel_id=1, source_target_pairs={{0,12},{2,50},{4,8},{6,54},{8,4},{10,58},{12,0},{14,62},{16,28},{1... | collective-permute-start | bytes 6291464 | tf_op jit(solution)/shard_map/ppermute | solution.py:1027
  116.3 13.0 %collective-permute-start.5 = (f32[1024,512]{1,0:T(8,128)}, f32[1024,512]{1,0:T(8,128)S(1)}, u32[]{:S(2)}, u32[]{:S(2)}) collective-permute-start(f32[1024,512]{1,0:T(8,128)} %get-tuple-element.110.refs_1_), channel_id=1, source_target_pairs={{0,2},{2,0},{1,3},{3,1},{4,6},{6,4},{5,7},{7,5},{8,10},{10,8},{9,1... | collective-permute-start | bytes 6291464 | tf_op jit(solution)/shard_map/ppermute | solution.py:1031
  118.7 13.6 %collective-permute-start.6 = (f32[1024,512]{1,0:T(8,128)S(1)}, f32[1024,512]{1,0:T(8,128)S(1)}, u32[]{:S(2)}, u32[]{:S(2)}) collective-permute-start(f32[1024,512]{1,0:T(8,128)S(1)} %get-tuple-element.118), channel_id=1, source_target_pairs={{0,2},{2,0},{1,3},{3,1},{4,6},{6,4},{5,7},{7,5},{8,10},{10,8},{9,1... | collective-permute-start | bytes 6291464 | tf_op jit(solution)/shard_map/ppermute | solution.py:1031
  118.7 49.9 %collective-permute-start.13 = (f32[512,1024]{1,0:T(8,128)}, f32[512,1024]{1,0:T(8,128)}, u32[]{:S(2)}, u32[]{:S(2)}) collective-permute-start(f32[512,1024]{1,0:T(8,128)} %forward.3.refs_1_.refs_3_), channel_id=1, source_target_pairs={{0,1},{1,0},{2,3},{3,2},{4,5},{5,4},{6,7},{7,6},{8,9},{9,8},{10,11... | collective-permute-start | bytes 6291464 | tf_op jit(solution)/shard_map/ppermute | solution.py:1031
  122.6 22.7 %collective-permute-start.7 = (f32[256,1024]{1,0:T(8,128)}, f32[256,1024]{1,0:T(8,128)}, u32[]{:S(2)}, u32[]{:S(2)}) collective-permute-start(f32[256,1024]{1,0:T(8,128)} %get-tuple-element.112.refs_1_), channel_id=1, source_target_pairs={{0,16},{2,14},{4,20},{6,10},{8,24},{10,6},{12,28},{14,2},{16,0},{1... | collective-permute-start | bytes 3145736 | tf_op jit(solution)/shard_map/ppermute | solution.py:1027
  126.8 23.7 %collective-permute-start.8 = (f32[256,1024]{1,0:T(8,128)}, f32[256,1024]{1,0:T(8,128)}, u32[]{:S(2)}, u32[]{:S(2)}) collective-permute-start(f32[256,1024]{1,0:T(8,128)} %get-tuple-element.114.refs_1_), channel_id=1, source_target_pairs={{0,48},{2,6},{4,52},{6,2},{8,56},{10,14},{12,60},{14,10},{16,32},{... | collective-permute-start | bytes 3145736 | tf_op jit(solution)/shard_map/ppermute | solution.py:1027
  131.1 23.6 %collective-permute-start.9 = (f32[512,512]{1,0:T(8,128)}, f32[512,512]{1,0:T(8,128)}, u32[]{:S(2)}, u32[]{:S(2)}) collective-permute-start(f32[512,512]{1,0:T(8,128)} %get-tuple-element.116.refs_1_), channel_id=1, source_target_pairs={{0,4},{2,18},{4,0},{6,22},{8,12},{10,26},{12,8},{14,30},{16,20},{1... | collective-permute-start | bytes 3145736 | tf_op jit(solution)/shard_map/ppermute | solution.py:1027
  134.1 22.6 %collective-permute-start.10 = (f32[512,512]{1,0:T(8,128)}, f32[512,512]{1,0:T(8,128)}, u32[]{:S(2)}, u32[]{:S(2)}) collective-permute-start(f32[512,512]{1,0:T(8,128)} %get-tuple-element.119.refs_0_), channel_id=1, source_target_pairs={{0,12},{2,50},{4,8},{6,54},{8,4},{10,58},{12,0},{14,62},{16,28},{1... | collective-permute-start | bytes 3145736 | tf_op jit(solution)/shard_map/ppermute | solution.py:1027
  147.8 13.7 %collective-permute-start.11 = (f32[128,1024]{1,0:T(8,128)S(1)}, f32[128,1024]{1,0:T(8,128)S(1)}, u32[]{:S(2)}, u32[]{:S(2)}) collective-permute-start(f32[128,1024]{1,0:T(8,128)S(1)} %get-tuple-element.123.refs_1_), channel_id=1, source_target_pairs={{0,12},{2,50},{4,8},{6,54},{8,4},{10,58},{12,0},{14,62},{16,28},{1... | collective-permute-start | bytes 1572872 | tf_op jit(solution)/shard_map/ppermute | solution.py:1027
  152.3 12.7 %collective-permute-start.12 = (f32[128,1024]{1,0:T(8,128)S(1)}, f32[128,1024]{1,0:T(8,128)S(1)}, u32[]{:S(2)}, u32[]{:S(2)}) collective-permute-start(f32[128,1024]{1,0:T(8,128)S(1)} %get-tuple-element.125.refs_1_), channel_id=1, source_target_pairs={{0,4},{2,18},{4,0},{6,22},{8,12},{10,26},{12,8},{14,30},{16,20},{1... | collective-permute-start | bytes 1572872 | tf_op jit(solution)/shard_map/ppermute | solution.py:1027
  156.5 12.0 %collective-permute-start.14 = (f32[256,512]{1,0:T(8,128)S(1)}, f32[256,512]{1,0:T(8,128)S(1)}, u32[]{:S(2)}, u32[]{:S(2)}) collective-permute-start(f32[256,512]{1,0:T(8,128)S(1)} %get-tuple-element.127.refs_1_), channel_id=1, source_target_pairs={{0,16},{2,14},{4,20},{6,10},{8,24},{10,6},{12,28},{14,2},{16,0},{1... | collective-permute-start | bytes 1572872 | tf_op jit(solution)/shard_map/ppermute | solution.py:1027
  158.5 10.7 %collective-permute-start.15 = (f32[256,512]{1,0:T(8,128)S(1)}, f32[256,512]{1,0:T(8,128)S(1)}, u32[]{:S(2)}, u32[]{:S(2)}) collective-permute-start(f32[256,512]{1,0:T(8,128)S(1)} %get-tuple-element.129.refs_1_), channel_id=1, source_target_pairs={{0,48},{2,6},{4,52},{6,2},{8,56},{10,14},{12,60},{14,10},{16,32},{... | collective-permute-start | bytes 1572872 | tf_op jit(solution)/shard_map/ppermute | solution.py:1027
  162.1 9.7 %collective-permute-start.16 = (f32[64,1024]{1,0:T(8,128)S(1)}, f32[64,1024]{1,0:T(8,128)S(1)}, u32[]{:S(2)}, u32[]{:S(2)}) collective-permute-start(f32[64,1024]{1,0:T(8,128)S(1)} %get-tuple-element.131.refs_1_), channel_id=1, source_target_pairs={{0,48},{2,6},{4,52},{6,2},{8,56},{10,14},{12,60},{14,10},{16,32},{... | collective-permute-start | bytes 786440 | tf_op jit(solution)/shard_map/ppermute | solution.py:1027
  172.1 12.3 %collective-permute-start.20 = (f32[128,1024]{1,0:T(8,128)S(1)}, f32[128,1024]{1,0:T(8,128)S(1)}, u32[]{:S(2)}, u32[]{:S(2)}) collective-permute-start(f32[128,1024]{1,0:T(8,128)S(1)} %pack.2.refs_1_), channel_id=1, source_target_pairs={{0,64},{64,0},{1,65},{65,1},{2,66},{66,2},{3,67},{67,3},{4,68},{68... | collective-permute-start | bytes 1572872 | tf_op jit(solution)/shard_map/ppermute | solution.py:1031
  193.1 8.7 %collective-permute-start.23 = (f32[144,512]{1,0:T(8,128)S(1)}, f32[144,512]{1,0:T(8,128)S(1)}, u32[]{:S(2)}, u32[]{:S(2)}) collective-permute-start(f32[144,512]{1,0:T(8,128)S(1)} %pack.3.refs_0_.refs_1_), channel_id=1, source_target_pairs={{0,64},{64,0},{1,65},{65,1},{2,66},{66,2},{3,67},{67,3},{4,68},{68... | collective-permute-start | bytes 884744 | tf_op jit(solution)/shard_map/ppermute | solution.py:1031
  202.5 56.1 %collective-permute-start.29 = (f32[512,1024]{1,0:T(8,128)}, f32[512,1024]{1,0:T(8,128)S(1)}, u32[]{:S(2)}, u32[]{:S(2)}) collective-permute-start(f32[512,1024]{1,0:T(8,128)} %get-tuple-element.149.refs_1_.refs_3_), channel_id=1, source_target_pairs={{0,1},{1,0},{2,3},{3,2},{4,5},{5,4},{6,7},{7,6},{8,9},{9,8},{10,11... | collective-permute-start | bytes 6291464 | tf_op jit(solution)/shard_map/ppermute | solution.py:1031
  203.5 9.7 %collective-permute-start.24 = (f32[80,512]{1,0:T(8,128)S(1)}, f32[80,512]{1,0:T(8,128)S(1)}, u32[]{:S(2)}, u32[]{:S(2)}) collective-permute-start(f32[80,512]{1,0:T(8,128)S(1)} %get-tuple-element.150.refs_3_), channel_id=1, source_target_pairs={{0,48},{2,6},{4,52},{6,2},{8,56},{10,14},{12,60},{14,10},{16,32},{... | collective-permute-start | bytes 491528 | tf_op jit(solution)/shard_map/ppermute | solution.py:1027
  203.5 13.6 %collective-permute-start.25 = (f32[64,512]{1,0:T(8,128)S(1)}, f32[64,512]{1,0:T(8,128)S(1)}, u32[]{:S(2)}, u32[]{:S(2)}) collective-permute-start(f32[64,512]{1,0:T(8,128)S(1)} %copy-done.25), channel_id=1, source_target_pairs={{0,16},{2,14},{4,20},{6,10},{8,24},{10,6},{12,28},{14,2},{16,0},{1... | collective-permute-start | bytes 393224 | tf_op jit(solution)/shard_map/ppermute | solution.py:1027
  215.9 14.0 %collective-permute-start.26 = (f32[144,512]{1,0:T(8,128)S(1)}, f32[144,512]{1,0:T(8,128)S(1)}, u32[]{:S(2)}, u32[]{:S(2)}) collective-permute-start(f32[144,512]{1,0:T(8,128)S(1)} %join.6.refs_1_.refs_3_), channel_id=1, source_target_pairs={{0,12},{2,50},{4,8},{6,54},{8,4},{10,58},{12,0},{14,62},{16,28},{1... | collective-permute-start | bytes 884744 | tf_op jit(solution)/shard_map/ppermute | solution.py:1027
  218.0 14.3 %collective-permute-start.27 = (f32[128,512]{1,0:T(8,128)S(1)}, f32[128,512]{1,0:T(8,128)S(1)}, u32[]{:S(2)}, u32[]{:S(2)}) collective-permute-start(f32[128,512]{1,0:T(8,128)S(1)} %join.7.refs_1_.refs_2_), channel_id=1, source_target_pairs={{0,4},{2,18},{4,0},{6,22},{8,12},{10,26},{12,8},{14,30},{16,20},{1... | collective-permute-start | bytes 786440 | tf_op jit(solution)/shard_map/ppermute | solution.py:1027
  230.5 21.5 %collective-permute-start.28 = (f32[272,512]{1,0:T(8,128)S(1)}, f32[272,512]{1,0:T(8,128)S(1)}, u32[]{:S(2)}, u32[]{:S(2)}) collective-permute-start(f32[272,512]{1,0:T(8,128)S(1)} %join.8.refs_1_.refs_3_), channel_id=1, source_target_pairs={{0,16},{2,14},{4,20},{6,10},{8,24},{10,6},{12,28},{14,2},{16,0},{1... | collective-permute-start | bytes 1671176 | tf_op jit(solution)/shard_map/ppermute | solution.py:1027
  232.9 25.7 %collective-permute-start.30 = (f32[256,512]{1,0:T(8,128)S(1)}, f32[256,512]{1,0:T(8,128)S(1)}, u32[]{:S(2)}, u32[]{:S(2)}) collective-permute-start(f32[256,512]{1,0:T(8,128)S(1)} %join.9.refs_0_.refs_2_.refs_3_), channel_id=1, source_target_pairs={{0,48},{2,6},{4,52},{6,2},{8,56},{10,14},{12,60},{14,10},{16,32},{... | collective-permute-start | bytes 1572872 | tf_op jit(solution)/shard_map/ppermute | solution.py:1027
  252.8 15.0 %collective-permute-start.31 = (f32[528,512]{1,0:T(8,128)S(1)}, f32[528,512]{1,0:T(8,128)S(1)}, u32[]{:S(2)}, u32[]{:S(2)}) collective-permute-start(f32[528,512]{1,0:T(8,128)S(1)} %join.10.refs_1_.refs_2_), channel_id=1, source_target_pairs={{0,2},{2,0},{1,3},{3,1},{4,6},{6,4},{5,7},{7,5},{8,10},{10,8},{9,1... | collective-permute-start | bytes 3244040 | tf_op jit(solution)/shard_map/ppermute | solution.py:1031
  252.9 28.5 %collective-permute-start.33 = (f32[528,512]{1,0:T(8,128)S(1)}, f32[528,512]{1,0:T(8,128)S(1)}, u32[]{:S(2)}, u32[]{:S(2)}) collective-permute-start(f32[528,512]{1,0:T(8,128)S(1)} %join.10.refs_1_.refs_2_), channel_id=1, source_target_pairs={{0,4},{2,18},{4,0},{6,22},{8,12},{10,26},{12,8},{14,30},{16,20},{1... | collective-permute-start | bytes 3244040 | tf_op jit(solution)/shard_map/ppermute | solution.py:1027
  260.5 21.0 %collective-permute-start.34 = (f32[512,512]{1,0:T(8,128)}, f32[512,512]{1,0:T(8,128)}, u32[]{:S(2)}, u32[]{:S(2)}) collective-permute-start(f32[512,512]{1,0:T(8,128)} %join.11.refs_0_.refs_3_), channel_id=1, source_target_pairs={{0,12},{2,50},{4,8},{6,54},{8,4},{10,58},{12,0},{14,62},{16,28},{1... | collective-permute-start | bytes 3145736 | tf_op jit(solution)/shard_map/ppermute | solution.py:1027
  260.6 50.1 %collective-permute-start.37 = (f32[512,1024]{1,0:T(8,128)}, f32[512,1024]{1,0:T(8,128)}, u32[]{:S(2)}, u32[]{:S(2)}) collective-permute-start(f32[512,1024]{1,0:T(8,128)} %get-tuple-element.162.refs_4_), channel_id=1, source_target_pairs={{0,1},{1,0},{2,3},{3,2},{4,5},{5,4},{6,7},{7,6},{8,9},{9,8},{10,11... | collective-permute-start | bytes 6291464 | tf_op jit(solution)/shard_map/ppermute | solution.py:1031
  288.3 27.5 %collective-permute-start.38 = (f32[16,512]{1,0:T(8,128)S(1)}, f32[16,512]{1,0:T(8,128)S(1)}, u32[]{:S(2)}, u32[]{:S(2)}) collective-permute-start(f32[16,512]{1,0:T(8,128)S(1)} %small_sums.1.refs_1_), channel_id=1, source_target_pairs={{0,1},{1,0},{2,3},{3,2},{4,5},{5,4},{6,7},{7,6},{8,9},{9,8},{10,11... | collective-permute-start | bytes 98312 | tf_op jit(solution)/shard_map/ppermute | solution.py:1031
  (58 other events, 362.0 us)
Sparse Core Ops, SparseCore 0:
  185.3 82.2 all-gather.2

commit v3 on v2

--- a/solution.py
+++ b/solution.py
@@ -502,18 +502,33 @@
     )
 
 
-def backward_kernel(dq0, dq1, dk, dv, w, a, tok, *rest, cuts):
-    pieces, sums = rest[:-1], rest[-1]
+def backward_kernel(dq0, dq1, dk, dv, w, a, tok, *rest, spots):
+    pieces, (sums, buf, sems) = rest[:-3], rest[-3:]
     i = pl.program_id(0)
+    steps = len(spots)
+    rows = buf.shape[1]
+    slot = i % 2
+
+    def leaving(step):
+        return [
+            pltpu.make_async_copy(
+                buf.at[step % 2, pl.ds(half * rows // 2, rows // 2)],
+                pieces[k].at[pl.ds(start, rows // 2)],
+                sems.at[step % 2, half],
+            )
+            for half, (k, start) in enumerate(spots[step])
+        ]
+
+    for step in range(2, steps):
+
+        @pl.when(i == step)
+        def _():
+            for copy in leaving(step - 2):
+                copy.wait()
 
     def one(dq):
         total = nt(dq[...], w[0]) + nt(dk[...], w[1]) + nt(dv[...], w[2]) + a[...]
-        for n, piece in enumerate(pieces):
-
-            @pl.when(jnp.logical_and(i >= cuts[n], i < cuts[n + 1]))
-            def _():
-                piece[...] = total
-
+        buf[slot] = total
         unit, _ = norm_rows(tok[...].astype(F32))
         both = jnp.concatenate(
             [jnp.sum(total * unit, axis=0, keepdims=True), jnp.sum(total, axis=0, keepdims=True)],
@@ -528,26 +543,39 @@
         def _():
             sums[...] += both
 
-    half = pl.num_programs(0) // 2
-
-    @pl.when(i < half)
+    @pl.when(i < steps // 2)
     def _():
         one(dq0)
 
-    @pl.when(i >= half)
+    @pl.when(i >= steps // 2)
     def _():
         one(dq1)
+
+    for step in range(steps):
+
+        @pl.when(i == step)
+        def _():
+            for copy in leaving(step):
+                copy.start()
+
+    @pl.when(i == steps - 1)
+    def _():
+        for step in (steps - 2, steps - 1):
+            for copy in leaving(step):
+                copy.wait()
 
 
 def backward_pass(after, dq0, dq1, dk, dv, w3, a, tok, sizes, rows=256):
     length, local = dk.shape
     width = w3.shape[1]
     steps = length // rows
-    cuts, specs = cut_specs(sizes, rows, width)
+    spots = [(k, start) for k, n in enumerate(sizes) for start in range(0, n, rows // 2)]
+    spots = [spots[2 * i : 2 * i + 2] for i in range(steps)]
     here = pl.BlockSpec((rows, width), lambda i: (i, 0))
     narrow = pl.BlockSpec((rows, local), lambda i: (i, 0))
-    return launch(
-        functools.partial(backward_kernel, cuts=cuts),
+    anywhere = pl.BlockSpec(memory_space=pltpu.HBM)
+    return launch(
+        functools.partial(backward_kernel, spots=spots),
         "backward",
         (steps,),
         (),
@@ -561,8 +589,8 @@
             (a, here),
             (tok, here),
         ],
-        [((n, width), F32, spec) for n, spec in zip(sizes, specs)]
-        + [((2, width), F32, whole(2, width))],
+        [((n, width), F32, anywhere) for n in sizes] + [((2, width), F32, whole(2, width))],
+        [pltpu.VMEM((2, rows, width), F32), pltpu.SemaphoreType.DMA((2, 2))],
         vmem=60,
         flops=6 * length * width * local,
     )
@@ -1097,7 +1125,7 @@
     tail_got1 = send_step(tail_s1, 1, 0)
 
     *back, sums = backward_pass(
-        (tail_s1,), dq0, dq1, dk, dv, w3, dn_f, tokens, (512, 512)
+        (tail_s1,), dq0, dq1, dk, dv, w3, dn_f, tokens, (128, 256, 512, 128)
     )
 
     down_k, down_s = halve(place, None, (sums,), down_k, down_got)
@@ -1122,6 +1150,8 @@
 
     feed_x = pack((tail_s1,), down_k, down_got, up_k, up_got)
     feed_got = exchange(feed_x, "xlo")
+    back[0] = gate((feed_x,), back[0])[0]
+    back_got = [exchange(back[0], "tensor")]
 
     tail_k0, tail_s0 = halve(place, bit_slot(0, 3), (feed_x,), tail_k0, tail_got0)
     tail_got0 = send_step(tail_s0, 0, 3)
@@ -1136,20 +1166,20 @@
     )
     tail_got = exchange(tail_x, "xlo")
 
-    tail0, tail1 = part((tail_x,), SMALL + tail_k0.shape[0], tail_x, tail_got)
+    tail0, tail1 = part((tail_x, back_got[0]), SMALL + tail_k0.shape[0], tail_x, tail_got)
     tail_got0 = send_step(tail0, 0, 3)
     tail_got1 = send_step(tail1, 1, 3)
 
-    back = gate((tail1,), *back)
-    back_got = [exchange(x, "tensor") for x in back]
-
-    turn = back[0]
+    back[1:] = gate((tail1,), *back[1:])
+    back_got += [exchange(x, "tensor") for x in back[1:]]
+
+    turn = back[1]
     for step in (3, 2, 1):
         tail0 = join(
             place, bit_slot(0, step), (turn, tail1), tail0, tail_got0, top=SMALL
         )
         tail_got0 = send_step(tail0, 0, step - 1)
-        sink = (back_got[0],) if step == 1 else ()
+        sink = (back_got[1],) if step == 2 else ()
         tail1 = join(place, bit_slot(1, step), (tail0, *sink), tail1, tail_got1)
         tail_got1 = send_step(tail1, 1, step - 1)
         turn = tail1
@@ -1159,12 +1189,12 @@
             )
 
     token_grad, turn = finish(
-        "finish_grad", (tail1,), (tokens, cotangent), back[:1], back_got[:1], gain, vmem=60
+        "finish_grad", (tail1,), (tokens, cotangent), back[:2], back_got[:2], gain, vmem=60
     )
     near0, near1 = exchange(tail0, "core"), exchange(tail1, "core")
     up_out, down_out, turn = spread((turn, near0, near1), gathered)
     down_out = down_out.reshape(hidden, width)
-    tail_got0, tail_got1 = gate((turn,), tail_got0, tail_got1)
+    tail_got0, tail_got1 = gate((turn, back_got[2]), tail_got0, tail_got1)
     near_got0, near_got1 = exchange(tail_got0, "core"), exchange(tail_got1, "core")
     kinds = [(near, part) for near in (False, True) for part in range(2)]
     qkv_out, merge_out, turn = place_pieces(
@@ -1184,10 +1214,11 @@
         width,
         into={0: qkv_out, 1: merge_out},
     )
-    token_grad, _ = finish(
-        "finish_grad", (turn,), (tokens, cotangent), back[1:], back_got[1:], gain,
-        start=length // 2, into={0: token_grad}, vmem=60,
-    )
+    for k, start in ((2, 384), (3, 896)):
+        token_grad, turn = finish(
+            "finish_grad", (turn,), (tokens, cotangent), back[k : k + 1], back_got[k : k + 1],
+            gain, start=start, into={0: token_grad}, vmem=60,
+        )
     pair = (small[:4] + small_got[:4]).reshape(2, width)
     return (
         block_out,

time: 329 us -> 320 us (0.973)
  the two profiles are of different devices: /device:TPU:18 before, /device:TPU:1 now
where the time goes in v3:
time: 320 us; the launch traced here: 316 us
  Pallas kernels  171 us (53%)
  starting transfers between devices  57.5 us (18%)
  waiting for transfers between devices  55 us (17%)
  local copies, waits for them, and re-layouts  17.7 us (6%)
  between operations  15 us (5%)
    pallas_call x44, Pallas kernels, launch(): pl.pallas_call(without, grid_spec=pltpu.PrefetchScalarGridSpec(num_scalar...  171 us
    ppermute x24, waiting for transfers between devices, send_step(): return lax.ppermute(x, RINGS, step_pairs(part, step))  36.6 us
    ppermute x17, starting transfers between devices, exchange(): return lax.ppermute(x, axis, SWAP)  30.1 us
    ppermute x24, starting transfers between devices, send_step(): return lax.ppermute(x, RINGS, step_pairs(part, step))  27.4 us
    unnamed x112, local copies, waits for them, and re-layouts  17 us
    ppermute x17, waiting for transfers between devices, exchange(): return lax.ppermute(x, axis, SWAP)  16.3 us
  transfers between devices with their start and end apart: 42, of which 19 were waited for; matrix products, arithmetic and copies ran while one was open for 0% of the time, Pallas kernels for 40%

profile of v3, /device:TPU:1, one launch (start us, length us, event | category | flops | bytes accessed | tf_op | source)
XLA Modules:
  0.0 316.4 jit_solution(15458317408026534013)
XLA Ops:
  7.9 11.5 %project.1 = (bf16[1024,1024]{1,0:T(8,128)(2,1)}, bf16[1024,1024]{1,0:T(8,128)(2,1)}, bf16[1024,512]{1,0:T(8,128)(2,1)}, bf16[1024,512]{1,0:T(8,128)(2,1)}, bf16...) custom-call(bf16[1024,1024]{1,0:T(8,128)(2,1)} %refs_2_.11, f32[1,1024]{1,0:T(1,128)} %bitcast.35, ...), custom_call_target="tpu_custom_call" | custom-call | flops 4294967296 | bytes 17838080 | tf_op jit(solution)/shard_map/project/pallas_call | solution.py:57
  19.4 26.9 %hidden.1 = (f32[1024,1024]{1,0:T(8,128)}, f32[1024,1024]{1,0:T(8,128)}, bf16[1024,2048]{1,0:T(8,128)(2,1)}, bf16[1024,2048]{1,0:T(8,128)(2,1)}, f32[1,2048]{1,0:T(1,128)}) custom-call(f32[1,1024]{1,0:T(1,128)} %get-tuple-element.94.refs_0_.refs_6_, bf16[1024,1024]{1,0:T(8,128)(2,1)} %get-tuple-element.95.refs_1_, bf16[1024,1024]{1,0:T(8,128)(2,1)} %refs_3_.9, ...), custom_call_target="tpu_custom_call" | custom-call | flops 19327352832 | bytes 29376512 | tf_op jit(solution)/shard_map/hidden/pallas_call | solution.py:57
  49.2 3.8 %grad.4.refs_1_ = f32[16,64,1024]{2,1,0:T(8,128)S(1)} custom-call(s32[77]{0:T(128)S(1)} %dynamic-slice_bitcast_fusion.refs_0_, f32[1,2048]{1,0:T(1,128)S(1)} %copy-done.32, bf16[1024,2048]{1,0:T(8,128)(2,1)S(1)} %copy-done.9, bf16[1024,1024]{1,0:T(8,128)(2,1)S(1)} %copy-done.1), custom_call_target="tpu_custom_call" | custom-call | flops 2147483648 | bytes 10485760 | tf_op jit(solution)/shard_map/grad/pallas_call | solution.py:57
  54.6 3.8 %grad.5.refs_0_ = f32[16,64,1024]{2,1,0:T(8,128)S(1)} custom-call(s32[77]{0:T(128)S(1)} %dynamic-slice_bitcast_fusion.refs_0_, f32[16,64,1024]{2,1,0:T(8,128)S(1)} %grad.4.refs_1_, bf16[1024,1024]{1,0:T(8,128)(2,1)S(1)} %copy-done.17, bf16[1024,2048]{1,0:T(8,128)(2,1)S(1)} %copy-done.7), custom_call_target="tpu_custom_call" | custom-call | flops 2147483648 | bytes 10485760 | tf_op jit(solution)/shard_map/grad/pallas_call | solution.py:57
  59.0 8.7 %attend.2 = (bf16[512,512]{1,0:T(8,128)(2,1)S(1)}, bf16[512,512]{1,0:T(8,128)(2,1)S(1)}, f32[512,512]{1,0:T(8,128)S(1)}, f32[512,512]{1,0:T(8,128)S(1)}) custom-call(f32[16,64,1024]{2,1,0:T(8,128)S(1)} %grad.5.refs_0_, bf16[1024,512]{1,0:T(8,128)(2,1)S(1)} %copy-done.41, bf16[1024,512]{1,0:T(8,128)(2,1)S(1)} %copy-done.46, bf16[1024,512]{1,0:T(8,128)(2,1)S(1)} %copy-done.42, ...), custom_call_target="tpu_custom_call" | custom-call | flops 4026531840 | bytes 8388608 | tf_op jit(solution)/shard_map/attend/pallas_call | solution.py:57
  70.0 2.9 collective-permute-start.2
  72.9 5.5 %grad.6 = (f32[8,64,1024]{2,1,0:T(8,128)S(1)}, f32[8,64,1024]{2,1,0:T(8,128)}) custom-call(s32[77]{0:T(128)S(1)} %dynamic-slice_bitcast_fusion.refs_0_, f32[512,1024]{1,0:T(8,128)S(1)} %forward.2.refs_1_.refs_2_, bf16[1024,2048]{1,0:T(8,128)(2,1)S(1)} %copy-done.10, bf16[1024,1024]{1,0:T(8,128)(2,1)S(1)} %copy-done.1, ...), custom_call_target="tpu_custom_call" | custom-call | flops 2147483648 | bytes 14680064 | tf_op jit(solution)/shard_map/grad/pallas_call | solution.py:57
  80.3 6.0 %grad.7 = (f32[8,64,1024]{2,1,0:T(8,128)S(1)}, f32[8,64,1024]{2,1,0:T(8,128)}) custom-call(s32[77]{0:T(128)S(1)} %dynamic-slice_bitcast_fusion.refs_0_, f32[512,1024]{1,0:T(8,128)} %bitcast.5.refs_1_, bf16[1024,1024]{1,0:T(8,128)(2,1)S(1)} %copy-done.17, bf16[1024,2048]{1,0:T(8,128)(2,1)S(1)} %copy-done.7, f32[16,64,1024]{2,1,0:T(8,128)} %collective-permute-done.1.refs_4_), custom_call_target="tpu_custom_call" | custom-call | flops 2147483648 | bytes 14680064 | tf_op jit(solution)/shard_map/grad/pallas_call | solution.py:57
  90.3 17.3 %attend.3 = (bf16[512,512]{1,0:T(8,128)(2,1)S(1)}, bf16[512,512]{1,0:T(8,128)(2,1)S(1)}, bf16[1024,512]{1,0:T(8,128)(2,1)S(1)}, bf16[1024,512]{1,0:T(8,128)(2,1)S(1)}) custom-call(f32[512,1024]{1,0:T(8,128)} %bitcast.6.refs_0_, bf16[1024,512]{1,0:T(8,128)(2,1)S(1)} %copy-done.41, bf16[1024,512]{1,0:T(8,128)(2,1)S(1)} %copy-done.47, ...), custom_call_target="tpu_custom_call" | custom-call | flops 8053063680 | bytes 10485760 | tf_op jit(solution)/shard_map/attend/pallas_call | solution.py:57
  107.7 2.6 forward.3.refs_1_.refs_3_
  111.0 9.2 %tail.1 = (f32[1024,512]{1,0:T(8,128)S(1)}, f32[1024,512]{1,0:T(8,128)S(1)}, f32[1024,512]{1,0:T(8,128)}, f32[1024,512]{1,0:T(8,128)S(1)}) custom-call(s32[77]{0:T(128)S(1)} %dynamic-slice_bitcast_fusion.refs_0_, f32[512,1024]{1,0:T(8,128)} %forward.3.refs_1_.refs_3_, bf16[1024,1024]{1,0:T(8,128)(2,1)S(1)} %copy-done.18, bf16[512,512]{1,0:T(8,128)(2,1)S(1)} %copy-done.31, ...), custom_call_target="tpu_custom_call" | custom-call | flops 4294967296 | bytes 16777216 | tf_op jit(solution)/shard_map/tail/pallas_call | solution.py:57
  124.8 2.7 collective-permute-start.7
  135.8 9.9 %backward.1 = (f32[128,1024]{1,0:T(8,128)}, f32[256,1024]{1,0:T(8,128)}, f32[512,1024]{1,0:T(8,128)}, f32[128,1024]{1,0:T(8,128)}, f32[2,1024]{1,0:T(2,128)}) custom-call(f32[512,512]{1,0:T(8,128)} %get-tuple-element.124.refs_0_, bf16[512,512]{1,0:T(8,128)(2,1)} %copy-done.23, bf16[512,512]{1,0:T(8,128)(2,1)} %copy-done.24, bf16[1024,512]{1,0:T(8,128)(2,1)} %copy-done.28, ...), custom_call_target="tpu_custom_call" | custom-call | flops 3221225472 | bytes 16785408 | tf_op jit(solution)/shard_map/backward/pallas_call | solution.py:57
  159.7 3.2 %collective-permute-done.11.refs_3_.refs_5_ = f32[128,1024]{1,0:T(8,128)S(1)} collective-permute-done((f32[128,1024]{1,0:T(8,128)S(1)}, f32[128,1024]{1,0:T(8,128)S(1)}, u32[]{:S(2)}, u32[]{:S(2)}) %collective-permute-start.11) | collective-permute-done | bytes 524320 | tf_op jit(solution)/shard_map/ppermute | solution.py:1055
  166.6 3.0 collective-permute-done.13.refs_2_.refs_5_
  174.0 2.6 collective-permute-start.18
  176.6 3.8 %collective-permute-done.18.refs_3_.refs_5_ = f32[128,512]{1,0:T(8,128)S(1)} collective-permute-done((f32[128,512]{1,0:T(8,128)S(1)}, f32[128,512]{1,0:T(8,128)S(1)}, u32[]{:S(2)}, u32[]{:S(2)}) %collective-permute-start.18) | collective-permute-done | bytes 262176 | tf_op jit(solution)/shard_map/ppermute | solution.py:1055
  193.2 4.9 %collective-permute-done.23.refs_1_.refs_5_ = f32[128,1024]{1,0:T(8,128)S(1)} collective-permute-done((f32[128,1024]{1,0:T(8,128)}, f32[128,1024]{1,0:T(8,128)S(1)}, u32[]{:S(2)}, u32[]{:S(2)}) %collective-permute-start.23) | collective-permute-done | bytes 524320 | tf_op jit(solution)/shard_map/ppermute | solution.py:1059
  198.1 5.0 %collective-permute-done.24.refs_3_ = f32[144,512]{1,0:T(8,128)S(1)} collective-permute-done((f32[144,512]{1,0:T(8,128)S(1)}, f32[144,512]{1,0:T(8,128)S(1)}, u32[]{:S(2)}, u32[]{:S(2)}) %collective-permute-start.24) | collective-permute-done | bytes 294944 | tf_op jit(solution)/shard_map/ppermute | solution.py:1059
  208.9 3.5 %collective-permute-done.25.refs_4_ = f32[80,512]{1,0:T(8,128)S(1)} collective-permute-done((f32[80,512]{1,0:T(8,128)S(1)}, f32[80,512]{1,0:T(8,128)S(1)}, u32[]{:S(2)}, u32[]{:S(2)}) %collective-permute-start.25) | collective-permute-done | bytes 163872 | tf_op jit(solution)/shard_map/ppermute | solution.py:1055
  218.1 3.7 %collective-permute-done.27.refs_4_ = f32[144,512]{1,0:T(8,128)S(1)} collective-permute-done((f32[144,512]{1,0:T(8,128)S(1)}, f32[144,512]{1,0:T(8,128)S(1)}, u32[]{:S(2)}, u32[]{:S(2)}) %collective-permute-start.27) | collective-permute-done | bytes 294944 | tf_op jit(solution)/shard_map/ppermute | solution.py:1055
  228.5 7.2 %finish_out.1 = (bf16[1024,1024]{1,0:T(8,128)(2,1)}, f32[8,128]{1,0:T(8,128)S(1)}) custom-call(f32[256,512]{1,0:T(8,128)S(1)} %join.9.refs_0_.refs_2_, bf16[1024,1024]{1,0:T(8,128)(2,1)S(1)} %copy-done, f32[512,1024]{1,0:T(8,128)S(1)} %copy-done.3, f32[512,1024]{1,0:T(8,128)} %forward.3.refs_1_.refs_3_, f32[512,1024]{1,0:T(8,128)} %collective-permute-done.2.refs_2_.refs_4_, ...), custom_call_target="tpu_custom_call" | custom-call | bytes 12591104 | tf_op jit(solution)/shard_map/finish_out/pallas_call | solution.py:57
  235.7 10.5 %collective-permute-done.30.refs_4_ = f32[272,512]{1,0:T(8,128)S(1)} collective-permute-done((f32[272,512]{1,0:T(8,128)S(1)}, f32[272,512]{1,0:T(8,128)S(1)}, u32[]{:S(2)}, u32[]{:S(2)}) %collective-permute-start.30) | collective-permute-done | bytes 557088 | tf_op jit(solution)/shard_map/ppermute | solution.py:1055
  247.0 9.9 %collective-permute-start.32 = (f32[528,512]{1,0:T(8,128)S(1)}, f32[528,512]{1,0:T(8,128)S(1)}, u32[]{:S(2)}, u32[]{:S(2)}) collective-permute-start(f32[528,512]{1,0:T(8,128)S(1)} %join.10.refs_1_.refs_2_), channel_id=1, source_target_pairs={{0,2},{2,0},{1,3},{3,1},{4,6},{6,4},{5,7},{7,5},{8,10},{10,8},{9,1... | collective-permute-start | bytes 3244040 | tf_op jit(solution)/shard_map/ppermute | solution.py:1059
  259.7 2.7 collective-permute-start.36
  262.3 4.8 %finish_grad.3 = (bf16[1024,1024]{1,0:T(8,128)(2,1)}, f32[8,128]{1,0:T(8,128)}) custom-call(f32[512,512]{1,0:T(8,128)} %join.11.refs_0_.refs_3_, bf16[1024,1024]{1,0:T(8,128)(2,1)} %refs_2_.11, bf16[1024,1024]{1,0:T(8,128)(2,1)} %refs_3_.9, f32[128,1024]{1,0:T(8,128)} %gate.3.refs_3_, f32[256,1024]{1,0:T(8,128)} %get-tuple-element.156.refs_1_.refs_4_, ...), custom_call_target="tpu_custom_call" | custom-call | bytes 9445376 | tf_op jit(solution)/shard_map/finish_grad/pallas_call | solution.py:57
  269.2 12.6 %spread.1 = (f32[1024,2048]{1,0:T(8,128)}, f32[2,1024,1024]{2,1,0:T(8,128)}, f32[8,128]{1,0:T(8,128)}) custom-call(f32[8,128]{1,0:T(8,128)} %get-tuple-element.160.refs_0_, f32[528,512]{1,0:T(8,128)} %copy-done.11, f32[512,512]{1,0:T(8,128)} %collective-permute-done.33.refs_2_.refs_5_, f32[32,128,1024]{2,1,0:T(8,128)} %bitcast.31), custom_call_target="tpu_custom_call" | custom-call | bytes 33558528 | tf_op jit(solution)/shard_map/spread/pallas_call | solution.py:57
  283.3 4.6 %collective-permute-start.39 = (f32[128,1024]{1,0:T(8,128)}, f32[128,1024]{1,0:T(8,128)S(1)}, u32[]{:S(2)}, u32[]{:S(2)}) collective-permute-start(f32[128,1024]{1,0:T(8,128)} %get-tuple-element.172.refs_4_), channel_id=1, source_target_pairs={{0,1},{1,0},{2,3},{3,2},{4,5},{5,4},{6,7},{7,6},{8,9},{9,8},{10,11... | collective-permute-start | bytes 1572872 | tf_op jit(solution)/shard_map/ppermute | solution.py:1059
  289.2 3.9 %place.2 = (f32[3,1024,512]{2,1,0:T(8,128)}, f32[512,1024]{1,0:T(8,128)}, f32[8,128]{1,0:T(8,128)S(1)}) custom-call(s32[77]{0:T(128)S(1)} %dynamic-slice_bitcast_fusion.refs_0_, f32[528,512]{1,0:T(8,128)S(1)} %copy-done.5, f32[528,512]{1,0:T(8,128)S(1)} %join.10.refs_1_.refs_2_, f32[512,512]{1,0:T(8,128)} %join.11.refs_0_.refs_3_, ...), custom_call_target="tpu_custom_call" | custom-call | bytes 12652544 | tf_op jit(solution)/shard_map/place/pallas_call | solution.py:57
  294.6 3.9 %place.3 = (f32[3,1024,512]{2,1,0:T(8,128)}, f32[512,1024]{1,0:T(8,128)}, f32[8,128]{1,0:T(8,128)S(1)}) custom-call(s32[77]{0:T(128)S(1)} %dynamic-slice_bitcast_fusion.refs_0_, f32[16,512]{1,0:T(8,128)S(1)} %small_sums.1.refs_1_, f32[3,1024,512]{2,1,0:T(8,128)} %get-tuple-element.165.refs_2_, ...), custom_call_target="tpu_custom_call", output_to_operand_aliasing={{0}: (2, {}), {1}: (3, {})} | custom-call | bytes 12652544 | tf_op jit(solution)/shard_map/place/pallas_call | solution.py:57
  299.1 5.1 %finish_grad.4 = (bf16[1024,1024]{1,0:T(8,128)(2,1)}, f32[8,128]{1,0:T(8,128)}) custom-call(f32[8,128]{1,0:T(8,128)} %copy-done.38, bf16[1024,1024]{1,0:T(8,128)(2,1)} %get-tuple-element.169.refs_1_, bf16[1024,1024]{1,0:T(8,128)(2,1)} %refs_2_.11, bf16[1024,1024]{1,0:T(8,128)(2,1)} %refs_3_.9, ...), custom_call_target="tpu_custom_call", output_to_operand_aliasing={{0}: (1, {})} | custom-call | bytes 10493952 | tf_op jit(solution)/shard_map/finish_grad/pallas_call | solution.py:57
  305.1 2.5 finish_grad.5
  (214 shorter events, 92.9 us)
Async XLA Ops:
  7.2 262.0 %all-gather.3.cloned.1.call-start = ((), (), s32[]{:S(2)}) async-start(), calls=%async_computation | async-start | bytes 17301504 | tf_op jit(solution)/shard_map/all_gather | solution.py:1162
  53.1 19.9 %collective-permute-start = (f32[16,64,1024]{2,1,0:T(8,128)S(1)}, f32[16,64,1024]{2,1,0:T(8,128)S(1)}, u32[]{:S(2)}, u32[]{:S(2)}) collective-permute-start(f32[16,64,1024]{2,1,0:T(8,128)S(1)} %grad.4.refs_1_), channel_id=1, source_target_pairs={{0,2},{2,0},{1,3},{3,1},{4,6},{6,4},{5,7},{7,5},{8,10},{10,8},{9,1... | collective-permute-start | bytes 12582920 | tf_op jit(solution)/shard_map/ppermute | solution.py:1059
  58.4 22.0 %collective-permute-start.1 = (f32[16,64,1024]{2,1,0:T(8,128)S(1)}, f32[16,64,1024]{2,1,0:T(8,128)}, u32[]{:S(2)}, u32[]{:S(2)}) collective-permute-start(f32[16,64,1024]{2,1,0:T(8,128)S(1)} %grad.5.refs_0_), channel_id=1, source_target_pairs={{0,2},{2,0},{1,3},{3,1},{4,6},{6,4},{5,7},{7,5},{8,10},{10,8},{9,1... | collective-permute-start | bytes 12582920 | tf_op jit(solution)/shard_map/ppermute | solution.py:1059
  70.0 51.1 %collective-permute-start.2 = (f32[512,1024]{1,0:T(8,128)S(1)}, f32[512,1024]{1,0:T(8,128)}, u32[]{:S(2)}, u32[]{:S(2)}) collective-permute-start(f32[512,1024]{1,0:T(8,128)S(1)} %forward.2.refs_1_.refs_2_), channel_id=1, source_target_pairs={{0,1},{1,0},{2,3},{3,2},{4,5},{5,4},{6,7},{7,6},{8,9},{9,8},{10,11... | collective-permute-start | bytes 6291464 | tf_op jit(solution)/shard_map/ppermute | solution.py:1059
  78.5 44.5 %collective-permute-start.3 = (f32[512,1024]{1,0:T(8,128)}, f32[512,1024]{1,0:T(8,128)S(1)}, u32[]{:S(2)}, u32[]{:S(2)}) collective-permute-start(f32[512,1024]{1,0:T(8,128)} %bitcast.5.refs_1_), channel_id=1, source_target_pairs={{0,4},{2,18},{4,0},{6,22},{8,12},{10,26},{12,8},{14,30},{16,20},{1... | collective-permute-start | bytes 6291464 | tf_op jit(solution)/shard_map/ppermute | solution.py:1055
  86.4 41.1 %collective-permute-start.4 = (f32[512,1024]{1,0:T(8,128)}, f32[512,1024]{1,0:T(8,128)S(1)}, u32[]{:S(2)}, u32[]{:S(2)}) collective-permute-start(f32[512,1024]{1,0:T(8,128)} %bitcast.6.refs_0_), channel_id=1, source_target_pairs={{0,12},{2,50},{4,8},{6,54},{8,4},{10,58},{12,0},{14,62},{16,28},{1... | collective-permute-start | bytes 6291464 | tf_op jit(solution)/shard_map/ppermute | solution.py:1055
  120.3 9.9 %collective-permute-start.5 = (f32[1024,512]{1,0:T(8,128)}, f32[1024,512]{1,0:T(8,128)S(1)}, u32[]{:S(2)}, u32[]{:S(2)}) collective-permute-start(f32[1024,512]{1,0:T(8,128)} %get-tuple-element.115.refs_1_), channel_id=1, source_target_pairs={{0,2},{2,0},{1,3},{3,1},{4,6},{6,4},{5,7},{7,5},{8,10},{10,8},{9,1... | collective-permute-start | bytes 6291464 | tf_op jit(solution)/shard_map/ppermute | solution.py:1059
  121.1 11.0 %collective-permute-start.6 = (f32[1024,512]{1,0:T(8,128)S(1)}, f32[1024,512]{1,0:T(8,128)S(1)}, u32[]{:S(2)}, u32[]{:S(2)}) collective-permute-start(f32[1024,512]{1,0:T(8,128)S(1)} %get-tuple-element.123), channel_id=1, source_target_pairs={{0,2},{2,0},{1,3},{3,1},{4,6},{6,4},{5,7},{7,5},{8,10},{10,8},{9,1... | collective-permute-start | bytes 6291464 | tf_op jit(solution)/shard_map/ppermute | solution.py:1059
  121.1 48.5 %collective-permute-start.13 = (f32[512,1024]{1,0:T(8,128)}, f32[512,1024]{1,0:T(8,128)}, u32[]{:S(2)}, u32[]{:S(2)}) collective-permute-start(f32[512,1024]{1,0:T(8,128)} %forward.3.refs_1_.refs_3_), channel_id=1, source_target_pairs={{0,1},{1,0},{2,3},{3,2},{4,5},{5,4},{6,7},{7,6},{8,9},{9,8},{10,11... | collective-permute-start | bytes 6291464 | tf_op jit(solution)/shard_map/ppermute | solution.py:1059
  124.8 20.9 %collective-permute-start.7 = (f32[256,1024]{1,0:T(8,128)}, f32[256,1024]{1,0:T(8,128)}, u32[]{:S(2)}, u32[]{:S(2)}) collective-permute-start(f32[256,1024]{1,0:T(8,128)} %get-tuple-element.117.refs_1_), channel_id=1, source_target_pairs={{0,16},{2,14},{4,20},{6,10},{8,24},{10,6},{12,28},{14,2},{16,0},{1... | collective-permute-start | bytes 3145736 | tf_op jit(solution)/shard_map/ppermute | solution.py:1055
  130.1 20.7 %collective-permute-start.8 = (f32[256,1024]{1,0:T(8,128)}, f32[256,1024]{1,0:T(8,128)}, u32[]{:S(2)}, u32[]{:S(2)}) collective-permute-start(f32[256,1024]{1,0:T(8,128)} %get-tuple-element.119.refs_1_), channel_id=1, source_target_pairs={{0,48},{2,6},{4,52},{6,2},{8,56},{10,14},{12,60},{14,10},{16,32},{... | collective-permute-start | bytes 3145736 | tf_op jit(solution)/shard_map/ppermute | solution.py:1055
  131.9 20.9 %collective-permute-start.9 = (f32[512,512]{1,0:T(8,128)}, f32[512,512]{1,0:T(8,128)}, u32[]{:S(2)}, u32[]{:S(2)}) collective-permute-start(f32[512,512]{1,0:T(8,128)} %get-tuple-element.121.refs_1_), channel_id=1, source_target_pairs={{0,4},{2,18},{4,0},{6,22},{8,12},{10,26},{12,8},{14,30},{16,20},{1... | collective-permute-start | bytes 3145736 | tf_op jit(solution)/shard_map/ppermute | solution.py:1055
  133.9 23.5 %collective-permute-start.10 = (f32[512,512]{1,0:T(8,128)}, f32[512,512]{1,0:T(8,128)}, u32[]{:S(2)}, u32[]{:S(2)}) collective-permute-start(f32[512,512]{1,0:T(8,128)} %get-tuple-element.124.refs_0_), channel_id=1, source_target_pairs={{0,12},{2,50},{4,8},{6,54},{8,4},{10,58},{12,0},{14,62},{16,28},{1... | collective-permute-start | bytes 3145736 | tf_op jit(solution)/shard_map/ppermute | solution.py:1055
  148.2 14.8 %collective-permute-start.11 = (f32[128,1024]{1,0:T(8,128)S(1)}, f32[128,1024]{1,0:T(8,128)S(1)}, u32[]{:S(2)}, u32[]{:S(2)}) collective-permute-start(f32[128,1024]{1,0:T(8,128)S(1)} %get-tuple-element.128.refs_1_), channel_id=1, source_target_pairs={{0,12},{2,50},{4,8},{6,54},{8,4},{10,58},{12,0},{14,62},{16,28},{1... | collective-permute-start | bytes 1572872 | tf_op jit(solution)/shard_map/ppermute | solution.py:1055
  152.7 11.4 %collective-permute-start.12 = (f32[128,1024]{1,0:T(8,128)S(1)}, f32[128,1024]{1,0:T(8,128)S(1)}, u32[]{:S(2)}, u32[]{:S(2)}) collective-permute-start(f32[128,1024]{1,0:T(8,128)S(1)} %get-tuple-element.130.refs_1_), channel_id=1, source_target_pairs={{0,4},{2,18},{4,0},{6,22},{8,12},{10,26},{12,8},{14,30},{16,20},{1... | collective-permute-start | bytes 1572872 | tf_op jit(solution)/shard_map/ppermute | solution.py:1055
  154.6 15.0 %collective-permute-start.14 = (f32[256,512]{1,0:T(8,128)S(1)}, f32[256,512]{1,0:T(8,128)S(1)}, u32[]{:S(2)}, u32[]{:S(2)}) collective-permute-start(f32[256,512]{1,0:T(8,128)S(1)} %get-tuple-element.132.refs_1_), channel_id=1, source_target_pairs={{0,16},{2,14},{4,20},{6,10},{8,24},{10,6},{12,28},{14,2},{16,0},{1... | collective-permute-start | bytes 1572872 | tf_op jit(solution)/shard_map/ppermute | solution.py:1055
  159.2 11.6 %collective-permute-start.15 = (f32[256,512]{1,0:T(8,128)S(1)}, f32[256,512]{1,0:T(8,128)S(1)}, u32[]{:S(2)}, u32[]{:S(2)}) collective-permute-start(f32[256,512]{1,0:T(8,128)S(1)} %get-tuple-element.134.refs_1_), channel_id=1, source_target_pairs={{0,48},{2,6},{4,52},{6,2},{8,56},{10,14},{12,60},{14,10},{16,32},{... | collective-permute-start | bytes 1572872 | tf_op jit(solution)/shard_map/ppermute | solution.py:1055
  163.5 10.0 %collective-permute-start.16 = (f32[64,1024]{1,0:T(8,128)S(1)}, f32[64,1024]{1,0:T(8,128)S(1)}, u32[]{:S(2)}, u32[]{:S(2)}) collective-permute-start(f32[64,1024]{1,0:T(8,128)S(1)} %get-tuple-element.136.refs_1_), channel_id=1, source_target_pairs={{0,48},{2,6},{4,52},{6,2},{8,56},{10,14},{12,60},{14,10},{16,32},{... | collective-permute-start | bytes 786440 | tf_op jit(solution)/shard_map/ppermute | solution.py:1055
  173.6 11.4 %collective-permute-start.20 = (f32[128,1024]{1,0:T(8,128)S(1)}, f32[128,1024]{1,0:T(8,128)S(1)}, u32[]{:S(2)}, u32[]{:S(2)}) collective-permute-start(f32[128,1024]{1,0:T(8,128)S(1)} %pack.2.refs_1_.refs_0_), channel_id=1, source_target_pairs={{0,64},{64,0},{1,65},{65,1},{2,66},{66,2},{3,67},{67,3},{4,68},{68... | collective-permute-start | bytes 1572872 | tf_op jit(solution)/shard_map/ppermute | solution.py:1059
  185.9 12.2 %collective-permute-start.23 = (f32[128,1024]{1,0:T(8,128)}, f32[128,1024]{1,0:T(8,128)S(1)}, u32[]{:S(2)}, u32[]{:S(2)}) collective-permute-start(f32[128,1024]{1,0:T(8,128)} %gate.3.refs_3_), channel_id=1, source_target_pairs={{0,1},{1,0},{2,3},{3,2},{4,5},{5,4},{6,7},{7,6},{8,9},{9,8},{10,11... | collective-permute-start | bytes 1572872 | tf_op jit(solution)/shard_map/ppermute | solution.py:1059
  192.8 10.2 %collective-permute-start.24 = (f32[144,512]{1,0:T(8,128)S(1)}, f32[144,512]{1,0:T(8,128)S(1)}, u32[]{:S(2)}, u32[]{:S(2)}) collective-permute-start(f32[144,512]{1,0:T(8,128)S(1)} %pack.3.refs_0_.refs_2_), channel_id=1, source_target_pairs={{0,64},{64,0},{1,65},{65,1},{2,66},{66,2},{3,67},{67,3},{4,68},{68... | collective-permute-start | bytes 884744 | tf_op jit(solution)/shard_map/ppermute | solution.py:1059
  203.8 22.6 %collective-permute-start.28 = (f32[256,1024]{1,0:T(8,128)}, f32[256,1024]{1,0:T(8,128)S(1)}, u32[]{:S(2)}, u32[]{:S(2)}) collective-permute-start(f32[256,1024]{1,0:T(8,128)} %get-tuple-element.156.refs_1_.refs_4_), channel_id=1, source_target_pairs={{0,1},{1,0},{2,3},{3,2},{4,5},{5,4},{6,7},{7,6},{8,9},{9,8},{10,11... | collective-permute-start | bytes 3145736 | tf_op jit(solution)/shard_map/ppermute | solution.py:1059
  205.9 75.9 %collective-permute-start.34 = (f32[512,1024]{1,0:T(8,128)}, f32[512,1024]{1,0:T(8,128)}, u32[]{:S(2)}, u32[]{:S(2)}) collective-permute-start(f32[512,1024]{1,0:T(8,128)} %get-tuple-element.162.refs_4_), channel_id=1, source_target_pairs={{0,1},{1,0},{2,3},{3,2},{4,5},{5,4},{6,7},{7,6},{8,9},{9,8},{10,11... | collective-permute-start | bytes 6291464 | tf_op jit(solution)/shard_map/ppermute | solution.py:1059
  222.5 23.7 %collective-permute-start.30 = (f32[272,512]{1,0:T(8,128)S(1)}, f32[272,512]{1,0:T(8,128)S(1)}, u32[]{:S(2)}, u32[]{:S(2)}) collective-permute-start(f32[272,512]{1,0:T(8,128)S(1)} %join.8.refs_1_.refs_3_), channel_id=1, source_target_pairs={{0,16},{2,14},{4,20},{6,10},{8,24},{10,6},{12,28},{14,2},{16,0},{1... | collective-permute-start | bytes 1671176 | tf_op jit(solution)/shard_map/ppermute | solution.py:1055
  227.3 29.6 %collective-permute-start.31 = (f32[256,512]{1,0:T(8,128)S(1)}, f32[256,512]{1,0:T(8,128)S(1)}, u32[]{:S(2)}, u32[]{:S(2)}) collective-permute-start(f32[256,512]{1,0:T(8,128)S(1)} %join.9.refs_0_.refs_2_), channel_id=1, source_target_pairs={{0,48},{2,6},{4,52},{6,2},{8,56},{10,14},{12,60},{14,10},{16,32},{... | collective-permute-start | bytes 1572872 | tf_op jit(solution)/shard_map/ppermute | solution.py:1055
  247.0 20.2 %collective-permute-start.32 = (f32[528,512]{1,0:T(8,128)S(1)}, f32[528,512]{1,0:T(8,128)S(1)}, u32[]{:S(2)}, u32[]{:S(2)}) collective-permute-start(f32[528,512]{1,0:T(8,128)S(1)} %join.10.refs_1_.refs_2_), channel_id=1, source_target_pairs={{0,2},{2,0},{1,3},{3,1},{4,6},{6,4},{5,7},{7,5},{8,10},{10,8},{9,1... | collective-permute-start | bytes 3244040 | tf_op jit(solution)/shard_map/ppermute | solution.py:1059
  256.9 24.9 %collective-permute-start.35 = (f32[528,512]{1,0:T(8,128)S(1)}, f32[528,512]{1,0:T(8,128)S(1)}, u32[]{:S(2)}, u32[]{:S(2)}) collective-permute-start(f32[528,512]{1,0:T(8,128)S(1)} %join.10.refs_1_.refs_2_), channel_id=1, source_target_pairs={{0,4},{2,18},{4,0},{6,22},{8,12},{10,26},{12,8},{14,30},{16,20},{1... | collective-permute-start | bytes 3244040 | tf_op jit(solution)/shard_map/ppermute | solution.py:1055
  259.7 22.2 %collective-permute-start.36 = (f32[512,512]{1,0:T(8,128)}, f32[512,512]{1,0:T(8,128)}, u32[]{:S(2)}, u32[]{:S(2)}) collective-permute-start(f32[512,512]{1,0:T(8,128)} %join.11.refs_0_.refs_3_), channel_id=1, source_target_pairs={{0,12},{2,50},{4,8},{6,54},{8,4},{10,58},{12,0},{14,62},{16,28},{1... | collective-permute-start | bytes 3145736 | tf_op jit(solution)/shard_map/ppermute | solution.py:1055
  282.8 10.3 %collective-permute-start.37 = (f32[528,512]{1,0:T(8,128)}, f32[528,512]{1,0:T(8,128)S(1)}, u32[]{:S(2)}, u32[]{:S(2)}) collective-permute-start(f32[528,512]{1,0:T(8,128)} %get-tuple-element.163.refs_1_.refs_2_.refs_4_), channel_id=1, source_target_pairs={{0,2},{2,0},{1,3},{3,1},{4,6},{6,4},{5,7},{7,5},{8,10},{10,8},{9,1... | collective-permute-start | bytes 3244040 | tf_op jit(solution)/shard_map/ppermute | solution.py:1059
  283.1 11.5 %collective-permute-start.38 = (f32[512,512]{1,0:T(8,128)}, f32[512,512]{1,0:T(8,128)S(1)}, u32[]{:S(2)}, u32[]{:S(2)}) collective-permute-start(f32[512,512]{1,0:T(8,128)} %get-tuple-element.167.refs_5_), channel_id=1, source_target_pairs={{0,2},{2,0},{1,3},{3,1},{4,6},{6,4},{5,7},{7,5},{8,10},{10,8},{9,1... | collective-permute-start | bytes 3145736 | tf_op jit(solution)/shard_map/ppermute | solution.py:1059
  283.3 20.9 %collective-permute-start.39 = (f32[128,1024]{1,0:T(8,128)}, f32[128,1024]{1,0:T(8,128)S(1)}, u32[]{:S(2)}, u32[]{:S(2)}) collective-permute-start(f32[128,1024]{1,0:T(8,128)} %get-tuple-element.172.refs_4_), channel_id=1, source_target_pairs={{0,1},{1,0},{2,3},{3,2},{4,5},{5,4},{6,7},{7,6},{8,9},{9,8},{10,11... | collective-permute-start | bytes 1572872 | tf_op jit(solution)/shard_map/ppermute | solution.py:1059
  293.2 14.3 %collective-permute-start.40 = (f32[16,512]{1,0:T(8,128)S(1)}, f32[16,512]{1,0:T(8,128)S(1)}, u32[]{:S(2)}, u32[]{:S(2)}) collective-permute-start(f32[16,512]{1,0:T(8,128)S(1)} %small_sums.1.refs_1_), channel_id=1, source_target_pairs={{0,1},{1,0},{2,3},{3,2},{4,5},{5,4},{6,7},{7,6},{8,9},{9,8},{10,11... | collective-permute-start | bytes 98312 | tf_op jit(solution)/shard_map/ppermute | solution.py:1059
  (63 other events, 384.1 us)
Sparse Core Ops, SparseCore 0:
  186.0 83.1 all-gather.2

commit v4 on v3

--- a/solution.py
+++ b/solution.py
@@ -265,7 +265,7 @@
             pltpu.VMEM((hidden, width), BF16),
             pltpu.SemaphoreType.DMA((2 * hidden // cols,)),
         ],
-        vmem=60,
+        vmem=52,
         flops=9 * length * width * hidden,
     )
 
@@ -348,7 +348,7 @@
         [(lhs, specs[0]), (rhs, specs[1])] + ([(got, anywhere)] if own else []),
         outs,
         scratch,
-        vmem=24,
+        vmem=28,
         flops=2 * rows * width * lhs.shape[0],
     )
 
@@ -591,7 +591,7 @@
         ],
         [((n, width), F32, anywhere) for n in sizes] + [((2, width), F32, whole(2, width))],
         [pltpu.VMEM((2, rows, width), F32), pltpu.SemaphoreType.DMA((2, 2))],
-        vmem=60,
+        vmem=44,
         flops=6 * length * width * local,
     )
 
@@ -1085,10 +1085,10 @@
         tokens, gain, shift, w3, merge_weight, cotangent, cos, sin
     )
     out_f, dn_f, active, d_pre, inner_g = hidden_pass(
-        (outer_g,), normed, cotangent, up_weight, inner_row, down_weight
-    )
-
-    (down_s,) = down_grad(place, OTHER, (inner_g,), active, cotangent)
+        (), normed, cotangent, up_weight, inner_row, down_weight
+    )
+
+    (down_s,) = down_grad(place, OTHER, (), active, cotangent)
     down_got = exchange(down_s, "core")
     (up_s,) = up_grad(place, OTHER, (down_s,), normed_t, d_pre)
     up_got = exchange(up_s, "core")
@@ -1179,7 +1179,7 @@
             place, bit_slot(0, step), (turn, tail1), tail0, tail_got0, top=SMALL
         )
         tail_got0 = send_step(tail0, 0, step - 1)
-        sink = (back_got[1],) if step == 2 else ()
+        sink = (back_got[1],) if step == 1 else ()
         tail1 = join(place, bit_slot(1, step), (tail0, *sink), tail1, tail_got1)
         tail_got1 = send_step(tail1, 1, step - 1)
         turn = tail1

time: 320 us -> 332 us (1.038)
  starting transfers between devices: 57.5 us -> 84.6 us
  waiting for transfers between devices: 55 us -> 42.9 us
  Pallas kernels: 171 us -> 165 us
    ppermute x17, starting transfers between devices: 30.1 us -> 48.2 us  [exchange(): return lax.ppermute(x, axis, SWAP)]
    ppermute x17, waiting for transfers between devices: 16.3 us -> 6.59 us  [exchange(): return lax.ppermute(x, axis, SWAP)]
    ppermute x24, starting transfers between devices: 27.4 us -> 36.4 us  [send_step(): return lax.ppermute(x, RINGS, step_pairs(part, step))]
    ppermute x24, waiting for transfers between devices: 36.6 us -> 29.7 us  [send_step(): return lax.ppermute(x, RINGS, step_pairs(part, step))]
    pallas_call x44, Pallas kernels: 171 us -> 165 us  [launch(): pl.pallas_call(without, grid_spec=pltpu.PrefetchScalarGridSpec(num_scalar...]
    all_gather x1, waiting for transfers between devices: 2 us -> 6.56 us  [body(): gathered = lax.all_gather(feed_x, ('core', 'z', 'y'))]
    unnamed x112 -> x114, local copies, waits for them, and re-layouts: 17 us -> 16.8 us
  transfers between devices with their start and end apart: 42 -> 42, of which waited for: 19 -> 14; matrix products, arithmetic and copies ran while one was open for 0% -> 0% of each run, Pallas kernels for 40% -> 38%
where the time goes in v4:
time: 332 us; the launch traced here: 325 us
  Pallas kernels  165 us (50%)
  starting transfers between devices  84.6 us (25%)
  waiting for transfers between devices  42.9 us (13%)
  local copies, waits for them, and re-layouts  17.5 us (5%)
  between operations  15.1 us (5%)
    pallas_call x44, Pallas kernels, launch(): pl.pallas_call(without, grid_spec=pltpu.PrefetchScalarGridSpec(num_scalar...  165 us
    ppermute x17, starting transfers between devices, exchange(): return lax.ppermute(x, axis, SWAP)  48.2 us
    ppermute x24, starting transfers between devices, send_step(): return lax.ppermute(x, RINGS, step_pairs(part, step))  36.4 us
    ppermute x24, waiting for transfers between devices, send_step(): return lax.ppermute(x, RINGS, step_pairs(part, step))  29.7 us
    unnamed x114, local copies, waits for them, and re-layouts  16.8 us
  transfers between devices with their start and end apart: 42, of which 14 were waited for; matrix products, arithmetic and copies ran while one was open for 0% of the time, Pallas kernels for 38%

profile of v4, /device:TPU:1, one launch (start us, length us, event | category | flops | bytes accessed | tf_op | source)
XLA Modules:
  0.0 325.2 jit_solution(16639002451062878141)
XLA Ops:
  7.9 11.5 %project.1 = (bf16[1024,1024]{1,0:T(8,128)(2,1)}, bf16[1024,1024]{1,0:T(8,128)(2,1)}, bf16[1024,512]{1,0:T(8,128)(2,1)}, bf16[1024,512]{1,0:T(8,128)(2,1)}, bf16...) custom-call(bf16[1024,1024]{1,0:T(8,128)(2,1)} %refs_2_.13, f32[1,1024]{1,0:T(1,128)} %bitcast.36, ...), custom_call_target="tpu_custom_call" | custom-call | flops 4294967296 | bytes 17838080 | tf_op jit(solution)/shard_map/project/pallas_call | solution.py:57
  19.5 26.9 %hidden.1 = (f32[1024,1024]{1,0:T(8,128)}, f32[1024,1024]{1,0:T(8,128)}, bf16[1024,2048]{1,0:T(8,128)(2,1)}, bf16[1024,2048]{1,0:T(8,128)(2,1)}, f32[1,2048]{1,0:T(1,128)S(1)}) custom-call(bf16[1024,1024]{1,0:T(8,128)(2,1)} %get-tuple-element.94.refs_0_, bf16[1024,1024]{1,0:T(8,128)(2,1)} %refs_3_.5, bf16[1024,2048]{1,0:T(8,128)(2,1)} %refs_2_.7, ...), custom_call_target="tpu_custom_call" | custom-call | flops 19327352832 | bytes 29376512 | tf_op jit(solution)/shard_map/hidden/pallas_call | solution.py:57
  48.6 3.8 %grad.4.refs_1_ = f32[16,64,1024]{2,1,0:T(8,128)S(1)} custom-call(s32[77]{0:T(128)S(1)} %dynamic-slice_bitcast_fusion.refs_0_, bf16[1024,2048]{1,0:T(8,128)(2,1)S(1)} %copy-done.9, bf16[1024,1024]{1,0:T(8,128)(2,1)S(1)} %copy-done.1), custom_call_target="tpu_custom_call" | custom-call | flops 2147483648 | bytes 10485760 | tf_op jit(solution)/shard_map/grad/pallas_call | solution.py:57
  54.0 4.7 %grad.5.refs_0_ = f32[16,64,1024]{2,1,0:T(8,128)} custom-call(s32[77]{0:T(128)S(1)} %dynamic-slice_bitcast_fusion.refs_0_, f32[16,64,1024]{2,1,0:T(8,128)S(1)} %grad.4.refs_1_, bf16[1024,1024]{1,0:T(8,128)(2,1)S(1)} %copy-done.22, bf16[1024,2048]{1,0:T(8,128)(2,1)S(1)} %copy-done.7), custom_call_target="tpu_custom_call" | custom-call | flops 2147483648 | bytes 10485760 | tf_op jit(solution)/shard_map/grad/pallas_call | solution.py:57
  58.9 8.9 %attend.2 = (bf16[512,512]{1,0:T(8,128)(2,1)S(1)}, bf16[512,512]{1,0:T(8,128)(2,1)S(1)}, f32[512,512]{1,0:T(8,128)S(1)}, f32[512,512]{1,0:T(8,128)S(1)}) custom-call(f32[16,64,1024]{2,1,0:T(8,128)} %grad.5.refs_0_, bf16[1024,512]{1,0:T(8,128)(2,1)S(1)} %copy-done.43, bf16[1024,512]{1,0:T(8,128)(2,1)S(1)} %copy-done.47, bf16[1024,512]{1,0:T(8,128)(2,1)S(1)} %copy-done.44, ...), custom_call_target="tpu_custom_call" | custom-call | flops 4026531840 | bytes 8388608 | tf_op jit(solution)/shard_map/attend/pallas_call | solution.py:57
  70.2 2.9 collective-permute-start.2
  73.1 5.5 %grad.6 = (f32[8,64,1024]{2,1,0:T(8,128)S(1)}, f32[8,64,1024]{2,1,0:T(8,128)}) custom-call(s32[77]{0:T(128)S(1)} %dynamic-slice_bitcast_fusion.refs_0_, f32[512,1024]{1,0:T(8,128)S(1)} %forward.2.refs_1_.refs_2_, bf16[1024,2048]{1,0:T(8,128)(2,1)S(1)} %copy-done.10, bf16[1024,1024]{1,0:T(8,128)(2,1)S(1)} %copy-done.1, ...), custom_call_target="tpu_custom_call" | custom-call | flops 2147483648 | bytes 14680064 | tf_op jit(solution)/shard_map/grad/pallas_call | solution.py:57
  80.5 6.0 %grad.7 = (f32[8,64,1024]{2,1,0:T(8,128)S(1)}, f32[8,64,1024]{2,1,0:T(8,128)}) custom-call(s32[77]{0:T(128)S(1)} %dynamic-slice_bitcast_fusion.refs_0_, f32[512,1024]{1,0:T(8,128)} %bitcast.5.refs_1_, bf16[1024,1024]{1,0:T(8,128)(2,1)S(1)} %copy-done.23, bf16[1024,2048]{1,0:T(8,128)(2,1)S(1)} %copy-done.7, f32[16,64,1024]{2,1,0:T(8,128)} %collective-permute-done.1.refs_4_), custom_call_target="tpu_custom_call" | custom-call | flops 2147483648 | bytes 14680064 | tf_op jit(solution)/shard_map/grad/pallas_call | solution.py:57
  89.2 17.4 %attend.3 = (bf16[512,512]{1,0:T(8,128)(2,1)S(1)}, bf16[512,512]{1,0:T(8,128)(2,1)S(1)}, bf16[1024,512]{1,0:T(8,128)(2,1)S(1)}, bf16[1024,512]{1,0:T(8,128)(2,1)S(1)}) custom-call(f32[512,1024]{1,0:T(8,128)} %bitcast.6.refs_0_, bf16[1024,512]{1,0:T(8,128)(2,1)S(1)} %copy-done.43, bf16[1024,512]{1,0:T(8,128)(2,1)S(1)} %copy-done.48, ...), custom_call_target="tpu_custom_call" | custom-call | flops 8053063680 | bytes 10485760 | tf_op jit(solution)/shard_map/attend/pallas_call | solution.py:57
  106.6 2.6 forward.3.refs_1_.refs_3_
  109.7 8.1 %tail.1 = (f32[1024,512]{1,0:T(8,128)S(1)}, f32[1024,512]{1,0:T(8,128)S(1)}, f32[1024,512]{1,0:T(8,128)S(1)}, f32[1024,512]{1,0:T(8,128)S(1)}) custom-call(s32[77]{0:T(128)S(1)} %dynamic-slice_bitcast_fusion.refs_0_, f32[512,1024]{1,0:T(8,128)} %forward.3.refs_1_.refs_3_, bf16[1024,1024]{1,0:T(8,128)(2,1)S(1)} %copy-done.24, ...), custom_call_target="tpu_custom_call" | custom-call | flops 4294967296 | bytes 16777216 | tf_op jit(solution)/shard_map/tail/pallas_call | solution.py:57
  123.6 2.8 collective-permute-start.7
  134.4 7.4 %backward.1 = (f32[128,1024]{1,0:T(8,128)S(1)}, f32[256,1024]{1,0:T(8,128)S(1)}, f32[512,1024]{1,0:T(8,128)S(1)}, f32[128,1024]{1,0:T(8,128)S(1)}, f32[2,1024]{1,0:T(2,128)S(1)}) custom-call(f32[512,512]{1,0:T(8,128)S(1)} %get-tuple-element.122.refs_0_, bf16[512,512]{1,0:T(8,128)(2,1)S(1)} %get-tuple-element.102.refs_0_.refs_6_.refs_1_, ...), custom_call_target="tpu_custom_call" | custom-call | flops 3221225472 | bytes 16785408 | tf_op jit(solution)/shard_map/backward/pallas_call | solution.py:57
  141.8 2.6 halve.18
  144.5 2.6 collective-permute-start.11
  158.5 3.6 %collective-permute-done.11.refs_3_.refs_5_ = f32[128,1024]{1,0:T(8,128)S(1)} collective-permute-done((f32[128,1024]{1,0:T(8,128)S(1)}, f32[128,1024]{1,0:T(8,128)S(1)}, u32[]{:S(2)}, u32[]{:S(2)}) %collective-permute-start.11) | collective-permute-done | bytes 524320 | tf_op jit(solution)/shard_map/ppermute | solution.py:1055
  168.0 3.0 collective-permute-done.15.refs_3_.refs_5_
  174.4 2.8 collective-permute-start.18
  177.2 3.8 %collective-permute-done.18.refs_3_.refs_5_ = f32[128,512]{1,0:T(8,128)S(1)} collective-permute-done((f32[128,512]{1,0:T(8,128)S(1)}, f32[128,512]{1,0:T(8,128)S(1)}, u32[]{:S(2)}, u32[]{:S(2)}) %collective-permute-start.18) | collective-permute-done | bytes 262176 | tf_op jit(solution)/shard_map/ppermute | solution.py:1055
  188.4 3.2 collective-permute-done.21.refs_2_
  194.0 4.4 %collective-permute-done.24.refs_3_ = f32[144,512]{1,0:T(8,128)S(1)} collective-permute-done((f32[144,512]{1,0:T(8,128)S(1)}, f32[144,512]{1,0:T(8,128)S(1)}, u32[]{:S(2)}, u32[]{:S(2)}) %collective-permute-start.24) | collective-permute-done | bytes 294944 | tf_op jit(solution)/shard_map/ppermute | solution.py:1059
  202.5 4.9 %collective-permute-start.26 = (f32[64,512]{1,0:T(8,128)S(1)}, f32[64,512]{1,0:T(8,128)S(1)}, u32[]{:S(2)}, u32[]{:S(2)}) collective-permute-start(f32[64,512]{1,0:T(8,128)S(1)} %copy-done.32), channel_id=1, source_target_pairs={{0,16},{2,14},{4,20},{6,10},{8,24},{10,6},{12,28},{14,2},{16,0},{1... | collective-permute-start | bytes 393224 | tf_op jit(solution)/shard_map/ppermute | solution.py:1055
  213.2 8.5 %collective-permute-done.27.refs_4_ = f32[144,512]{1,0:T(8,128)S(1)} collective-permute-done((f32[144,512]{1,0:T(8,128)S(1)}, f32[144,512]{1,0:T(8,128)S(1)}, u32[]{:S(2)}, u32[]{:S(2)}) %collective-permute-start.27) | collective-permute-done | bytes 294944 | tf_op jit(solution)/shard_map/ppermute | solution.py:1055
  229.1 6.0 %finish_out.1 = (bf16[1024,1024]{1,0:T(8,128)(2,1)}, f32[8,128]{1,0:T(8,128)S(1)}) custom-call(f32[256,512]{1,0:T(8,128)S(1)} %join.9.refs_0_.refs_2_.refs_3_, bf16[1024,1024]{1,0:T(8,128)(2,1)S(1)} %copy-done, f32[512,1024]{1,0:T(8,128)S(1)} %copy-done.3, f32[512,1024]{1,0:T(8,128)} %forward.3.refs_1_.refs_3_, f32[512,1024]{1,0:T(8,128)S(1)} %copy-done.16, ...), custom_call_target="tpu_custom_call" | custom-call | bytes 12591104 | tf_op jit(solution)/shard_map/finish_out/pallas_call | solution.py:57
  235.8 27.8 %collective-permute-start.32 = (f32[528,512]{1,0:T(8,128)S(1)}, f32[528,512]{1,0:T(8,128)S(1)}, u32[]{:S(2)}, u32[]{:S(2)}) collective-permute-start(f32[528,512]{1,0:T(8,128)S(1)} %join.10.refs_1_.refs_2_), channel_id=1, source_target_pairs={{0,2},{2,0},{1,3},{3,1},{4,6},{6,4},{5,7},{7,5},{8,10},{10,8},{9,1... | collective-permute-start | bytes 3244040 | tf_op jit(solution)/shard_map/ppermute | solution.py:1059
  267.0 4.9 %finish_grad.3 = (bf16[1024,1024]{1,0:T(8,128)(2,1)}, f32[8,128]{1,0:T(8,128)}) custom-call(f32[512,512]{1,0:T(8,128)} %join.11.refs_0_.refs_3_, bf16[1024,1024]{1,0:T(8,128)(2,1)} %refs_2_.13, bf16[1024,1024]{1,0:T(8,128)(2,1)} %refs_3_.5, f32[128,1024]{1,0:T(8,128)} %gate.3.refs_3_, f32[256,1024]{1,0:T(8,128)} %get-tuple-element.156.refs_1_.refs_4_, ...), custom_call_target="tpu_custom_call" | custom-call | bytes 9445376 | tf_op jit(solution)/shard_map/finish_grad/pallas_call | solution.py:57
  271.9 6.6 %all-gather.3.cloned.1.call-done = f32[4096,1024]{1,0:T(8,128)} async-done(((f32[128,1024]{1,0:T(8,128)}), f32[4096,1024]{1,0:T(8,128)}) %all-gather.3.cloned.1.call-update) | async-done | bytes 16777232 | tf_op jit(solution)/shard_map/all_gather | solution.py:1162
  278.5 12.6 %spread.1 = (f32[1024,2048]{1,0:T(8,128)}, f32[2,1024,1024]{2,1,0:T(8,128)}, f32[8,128]{1,0:T(8,128)}) custom-call(f32[8,128]{1,0:T(8,128)} %get-tuple-element.160.refs_0_, f32[528,512]{1,0:T(8,128)} %copy-done.11, f32[512,512]{1,0:T(8,128)} %collective-permute-done.33.refs_2_.refs_5_, f32[32,128,1024]{2,1,0:T(8,128)} %bitcast.32), custom_call_target="tpu_custom_call" | custom-call | bytes 33558528 | tf_op jit(solution)/shard_map/spread/pallas_call | solution.py:57
  292.6 4.2 %collective-permute-start.39 = (f32[128,1024]{1,0:T(8,128)}, f32[128,1024]{1,0:T(8,128)S(1)}, u32[]{:S(2)}, u32[]{:S(2)}) collective-permute-start(f32[128,1024]{1,0:T(8,128)} %get-tuple-element.172.refs_4_), channel_id=1, source_target_pairs={{0,1},{1,0},{2,3},{3,2},{4,5},{5,4},{6,7},{7,6},{8,9},{9,8},{10,11... | collective-permute-start | bytes 1572872 | tf_op jit(solution)/shard_map/ppermute | solution.py:1059
  298.1 3.9 %place.2 = (f32[3,1024,512]{2,1,0:T(8,128)}, f32[512,1024]{1,0:T(8,128)}, f32[8,128]{1,0:T(8,128)S(1)}) custom-call(s32[77]{0:T(128)S(1)} %dynamic-slice_bitcast_fusion.refs_0_, f32[528,512]{1,0:T(8,128)S(1)} %copy-done.5, f32[528,512]{1,0:T(8,128)S(1)} %join.10.refs_1_.refs_2_, f32[512,512]{1,0:T(8,128)} %join.11.refs_0_.refs_3_, ...), custom_call_target="tpu_custom_call" | custom-call | bytes 12652544 | tf_op jit(solution)/shard_map/place/pallas_call | solution.py:57
  303.5 3.9 %place.3 = (f32[3,1024,512]{2,1,0:T(8,128)}, f32[512,1024]{1,0:T(8,128)}, f32[8,128]{1,0:T(8,128)S(1)}) custom-call(s32[77]{0:T(128)S(1)} %dynamic-slice_bitcast_fusion.refs_0_, f32[16,512]{1,0:T(8,128)S(1)} %small_sums.1.refs_1_, f32[3,1024,512]{2,1,0:T(8,128)} %get-tuple-element.165.refs_2_, ...), custom_call_target="tpu_custom_call", output_to_operand_aliasing={{0}: (2, {}), {1}: (3, {})} | custom-call | bytes 12652544 | tf_op jit(solution)/shard_map/place/pallas_call | solution.py:57
  308.0 5.1 %finish_grad.4 = (bf16[1024,1024]{1,0:T(8,128)(2,1)}, f32[8,128]{1,0:T(8,128)}) custom-call(f32[8,128]{1,0:T(8,128)} %copy-done.39, bf16[1024,1024]{1,0:T(8,128)(2,1)} %get-tuple-element.169.refs_1_, bf16[1024,1024]{1,0:T(8,128)(2,1)} %refs_2_.13, bf16[1024,1024]{1,0:T(8,128)(2,1)} %refs_3_.5, ...), custom_call_target="tpu_custom_call", output_to_operand_aliasing={{0}: (1, {})} | custom-call | bytes 10493952 | tf_op jit(solution)/shard_map/finish_grad/pallas_call | solution.py:57
  (216 shorter events, 87.2 us)
Async XLA Ops:
  7.2 271.3 %all-gather.3.cloned.1.call-start = ((), (), s32[]{:S(2)}) async-start(), calls=%async_computation | async-start | bytes 17301504 | tf_op jit(solution)/shard_map/all_gather | solution.py:1162
  52.4 20.6 %collective-permute-start = (f32[16,64,1024]{2,1,0:T(8,128)S(1)}, f32[16,64,1024]{2,1,0:T(8,128)S(1)}, u32[]{:S(2)}, u32[]{:S(2)}) collective-permute-start(f32[16,64,1024]{2,1,0:T(8,128)S(1)} %grad.4.refs_1_), channel_id=1, source_target_pairs={{0,2},{2,0},{1,3},{3,1},{4,6},{6,4},{5,7},{7,5},{8,10},{10,8},{9,1... | collective-permute-start | bytes 12582920 | tf_op jit(solution)/shard_map/ppermute | solution.py:1059
  58.7 21.7 %collective-permute-start.1 = (f32[16,64,1024]{2,1,0:T(8,128)}, f32[16,64,1024]{2,1,0:T(8,128)}, u32[]{:S(2)}, u32[]{:S(2)}) collective-permute-start(f32[16,64,1024]{2,1,0:T(8,128)} %grad.5.refs_0_), channel_id=1, source_target_pairs={{0,2},{2,0},{1,3},{3,1},{4,6},{6,4},{5,7},{7,5},{8,10},{10,8},{9,1... | collective-permute-start | bytes 12582920 | tf_op jit(solution)/shard_map/ppermute | solution.py:1059
  70.2 48.7 %collective-permute-start.2 = (f32[512,1024]{1,0:T(8,128)S(1)}, f32[512,1024]{1,0:T(8,128)S(1)}, u32[]{:S(2)}, u32[]{:S(2)}) collective-permute-start(f32[512,1024]{1,0:T(8,128)S(1)} %forward.2.refs_1_.refs_2_), channel_id=1, source_target_pairs={{0,1},{1,0},{2,3},{3,2},{4,5},{5,4},{6,7},{7,6},{8,9},{9,8},{10,11... | collective-permute-start | bytes 6291464 | tf_op jit(solution)/shard_map/ppermute | solution.py:1059
  78.6 42.7 %collective-permute-start.3 = (f32[512,1024]{1,0:T(8,128)}, f32[512,1024]{1,0:T(8,128)}, u32[]{:S(2)}, u32[]{:S(2)}) collective-permute-start(f32[512,1024]{1,0:T(8,128)} %bitcast.5.refs_1_), channel_id=1, source_target_pairs={{0,4},{2,18},{4,0},{6,22},{8,12},{10,26},{12,8},{14,30},{16,20},{1... | collective-permute-start | bytes 6291464 | tf_op jit(solution)/shard_map/ppermute | solution.py:1055
  86.5 40.0 %collective-permute-start.4 = (f32[512,1024]{1,0:T(8,128)}, f32[512,1024]{1,0:T(8,128)}, u32[]{:S(2)}, u32[]{:S(2)}) collective-permute-start(f32[512,1024]{1,0:T(8,128)} %bitcast.6.refs_0_), channel_id=1, source_target_pairs={{0,12},{2,50},{4,8},{6,54},{8,4},{10,58},{12,0},{14,62},{16,28},{1... | collective-permute-start | bytes 6291464 | tf_op jit(solution)/shard_map/ppermute | solution.py:1055
  117.8 11.0 %collective-permute-start.5 = (f32[1024,512]{1,0:T(8,128)S(1)}, f32[1024,512]{1,0:T(8,128)S(1)}, u32[]{:S(2)}, u32[]{:S(2)}) collective-permute-start(f32[1024,512]{1,0:T(8,128)S(1)} %get-tuple-element.113.refs_1_), channel_id=1, source_target_pairs={{0,2},{2,0},{1,3},{3,1},{4,6},{6,4},{5,7},{7,5},{8,10},{10,8},{9,1... | collective-permute-start | bytes 6291464 | tf_op jit(solution)/shard_map/ppermute | solution.py:1059
  118.7 12.6 %collective-permute-start.6 = (f32[1024,512]{1,0:T(8,128)S(1)}, f32[1024,512]{1,0:T(8,128)S(1)}, u32[]{:S(2)}, u32[]{:S(2)}) collective-permute-start(f32[1024,512]{1,0:T(8,128)S(1)} %get-tuple-element.121), channel_id=1, source_target_pairs={{0,2},{2,0},{1,3},{3,1},{4,6},{6,4},{5,7},{7,5},{8,10},{10,8},{9,1... | collective-permute-start | bytes 6291464 | tf_op jit(solution)/shard_map/ppermute | solution.py:1059
  118.8 47.9 %collective-permute-start.13 = (f32[512,1024]{1,0:T(8,128)}, f32[512,1024]{1,0:T(8,128)S(1)}, u32[]{:S(2)}, u32[]{:S(2)}) collective-permute-start(f32[512,1024]{1,0:T(8,128)} %forward.3.refs_1_.refs_3_), channel_id=1, source_target_pairs={{0,1},{1,0},{2,3},{3,2},{4,5},{5,4},{6,7},{7,6},{8,9},{9,8},{10,11... | collective-permute-start | bytes 6291464 | tf_op jit(solution)/shard_map/ppermute | solution.py:1059
  123.6 18.2 %collective-permute-start.7 = (f32[256,1024]{1,0:T(8,128)S(1)}, f32[256,1024]{1,0:T(8,128)}, u32[]{:S(2)}, u32[]{:S(2)}) collective-permute-start(f32[256,1024]{1,0:T(8,128)S(1)} %get-tuple-element.115.refs_1_), channel_id=1, source_target_pairs={{0,16},{2,14},{4,20},{6,10},{8,24},{10,6},{12,28},{14,2},{16,0},{1... | collective-permute-start | bytes 3145736 | tf_op jit(solution)/shard_map/ppermute | solution.py:1055
  128.7 20.7 %collective-permute-start.8 = (f32[256,1024]{1,0:T(8,128)S(1)}, f32[256,1024]{1,0:T(8,128)}, u32[]{:S(2)}, u32[]{:S(2)}) collective-permute-start(f32[256,1024]{1,0:T(8,128)S(1)} %get-tuple-element.117.refs_1_), channel_id=1, source_target_pairs={{0,48},{2,6},{4,52},{6,2},{8,56},{10,14},{12,60},{14,10},{16,32},{... | collective-permute-start | bytes 3145736 | tf_op jit(solution)/shard_map/ppermute | solution.py:1055
  129.6 24.2 %collective-permute-start.9 = (f32[512,512]{1,0:T(8,128)S(1)}, f32[512,512]{1,0:T(8,128)S(1)}, u32[]{:S(2)}, u32[]{:S(2)}) collective-permute-start(f32[512,512]{1,0:T(8,128)S(1)} %get-tuple-element.119.refs_1_), channel_id=1, source_target_pairs={{0,4},{2,18},{4,0},{6,22},{8,12},{10,26},{12,8},{14,30},{16,20},{1... | collective-permute-start | bytes 3145736 | tf_op jit(solution)/shard_map/ppermute | solution.py:1055
  132.1 24.4 %collective-permute-start.10 = (f32[512,512]{1,0:T(8,128)S(1)}, f32[512,512]{1,0:T(8,128)S(1)}, u32[]{:S(2)}, u32[]{:S(2)}) collective-permute-start(f32[512,512]{1,0:T(8,128)S(1)} %get-tuple-element.122.refs_0_), channel_id=1, source_target_pairs={{0,12},{2,50},{4,8},{6,54},{8,4},{10,58},{12,0},{14,62},{16,28},{1... | collective-permute-start | bytes 3145736 | tf_op jit(solution)/shard_map/ppermute | solution.py:1055
  144.5 17.5 %collective-permute-start.11 = (f32[128,1024]{1,0:T(8,128)S(1)}, f32[128,1024]{1,0:T(8,128)S(1)}, u32[]{:S(2)}, u32[]{:S(2)}) collective-permute-start(f32[128,1024]{1,0:T(8,128)S(1)} %get-tuple-element.126.refs_1_), channel_id=1, source_target_pairs={{0,12},{2,50},{4,8},{6,54},{8,4},{10,58},{12,0},{14,62},{16,28},{1... | collective-permute-start | bytes 1572872 | tf_op jit(solution)/shard_map/ppermute | solution.py:1055
  151.3 12.7 %collective-permute-start.12 = (f32[128,1024]{1,0:T(8,128)S(1)}, f32[128,1024]{1,0:T(8,128)S(1)}, u32[]{:S(2)}, u32[]{:S(2)}) collective-permute-start(f32[128,1024]{1,0:T(8,128)S(1)} %get-tuple-element.128.refs_1_), channel_id=1, source_target_pairs={{0,4},{2,18},{4,0},{6,22},{8,12},{10,26},{12,8},{14,30},{16,20},{1... | collective-permute-start | bytes 1572872 | tf_op jit(solution)/shard_map/ppermute | solution.py:1055
  154.5 12.2 %collective-permute-start.14 = (f32[256,512]{1,0:T(8,128)S(1)}, f32[256,512]{1,0:T(8,128)S(1)}, u32[]{:S(2)}, u32[]{:S(2)}) collective-permute-start(f32[256,512]{1,0:T(8,128)S(1)} %get-tuple-element.130.refs_1_), channel_id=1, source_target_pairs={{0,16},{2,14},{4,20},{6,10},{8,24},{10,6},{12,28},{14,2},{16,0},{1... | collective-permute-start | bytes 1572872 | tf_op jit(solution)/shard_map/ppermute | solution.py:1055
  157.1 14.0 %collective-permute-start.15 = (f32[256,512]{1,0:T(8,128)S(1)}, f32[256,512]{1,0:T(8,128)S(1)}, u32[]{:S(2)}, u32[]{:S(2)}) collective-permute-start(f32[256,512]{1,0:T(8,128)S(1)} %get-tuple-element.132.refs_1_), channel_id=1, source_target_pairs={{0,48},{2,6},{4,52},{6,2},{8,56},{10,14},{12,60},{14,10},{16,32},{... | collective-permute-start | bytes 1572872 | tf_op jit(solution)/shard_map/ppermute | solution.py:1055
  162.6 11.2 %collective-permute-start.16 = (f32[64,1024]{1,0:T(8,128)S(1)}, f32[64,1024]{1,0:T(8,128)S(1)}, u32[]{:S(2)}, u32[]{:S(2)}) collective-permute-start(f32[64,1024]{1,0:T(8,128)S(1)} %get-tuple-element.134.refs_1_), channel_id=1, source_target_pairs={{0,48},{2,6},{4,52},{6,2},{8,56},{10,14},{12,60},{14,10},{16,32},{... | collective-permute-start | bytes 786440 | tf_op jit(solution)/shard_map/ppermute | solution.py:1055
  184.2 9.8 %collective-permute-start.23 = (f32[128,1024]{1,0:T(8,128)}, f32[128,1024]{1,0:T(8,128)S(1)}, u32[]{:S(2)}, u32[]{:S(2)}) collective-permute-start(f32[128,1024]{1,0:T(8,128)} %gate.3.refs_3_), channel_id=1, source_target_pairs={{0,1},{1,0},{2,3},{3,2},{4,5},{5,4},{6,7},{7,6},{8,9},{9,8},{10,11... | collective-permute-start | bytes 1572872 | tf_op jit(solution)/shard_map/ppermute | solution.py:1059
  199.5 64.1 %collective-permute-start.30 = (f32[256,1024]{1,0:T(8,128)}, f32[256,1024]{1,0:T(8,128)S(1)}, u32[]{:S(2)}, u32[]{:S(2)}) collective-permute-start(f32[256,1024]{1,0:T(8,128)} %get-tuple-element.156.refs_1_.refs_4_), channel_id=1, source_target_pairs={{0,1},{1,0},{2,3},{3,2},{4,5},{5,4},{6,7},{7,6},{8,9},{9,8},{10,11... | collective-permute-start | bytes 3145736 | tf_op jit(solution)/shard_map/ppermute | solution.py:1059
  200.5 90.6 %collective-permute-start.34 = (f32[512,1024]{1,0:T(8,128)}, f32[512,1024]{1,0:T(8,128)}, u32[]{:S(2)}, u32[]{:S(2)}) collective-permute-start(f32[512,1024]{1,0:T(8,128)} %get-tuple-element.162.refs_4_), channel_id=1, source_target_pairs={{0,1},{1,0},{2,3},{3,2},{4,5},{5,4},{6,7},{7,6},{8,9},{9,8},{10,11... | collective-permute-start | bytes 6291464 | tf_op jit(solution)/shard_map/ppermute | solution.py:1059
  209.6 12.1 %collective-permute-start.27 = (f32[144,512]{1,0:T(8,128)S(1)}, f32[144,512]{1,0:T(8,128)S(1)}, u32[]{:S(2)}, u32[]{:S(2)}) collective-permute-start(f32[144,512]{1,0:T(8,128)S(1)} %join.6.refs_1_.refs_3_), channel_id=1, source_target_pairs={{0,12},{2,50},{4,8},{6,54},{8,4},{10,58},{12,0},{14,62},{16,28},{1... | collective-permute-start | bytes 884744 | tf_op jit(solution)/shard_map/ppermute | solution.py:1055
  213.1 11.7 %collective-permute-start.28 = (f32[128,512]{1,0:T(8,128)S(1)}, f32[128,512]{1,0:T(8,128)S(1)}, u32[]{:S(2)}, u32[]{:S(2)}) collective-permute-start(f32[128,512]{1,0:T(8,128)S(1)} %join.7.refs_1_.refs_2_), channel_id=1, source_target_pairs={{0,4},{2,18},{4,0},{6,22},{8,12},{10,26},{12,8},{14,30},{16,20},{1... | collective-permute-start | bytes 786440 | tf_op jit(solution)/shard_map/ppermute | solution.py:1055
  222.4 12.6 %collective-permute-start.29 = (f32[272,512]{1,0:T(8,128)S(1)}, f32[272,512]{1,0:T(8,128)S(1)}, u32[]{:S(2)}, u32[]{:S(2)}) collective-permute-start(f32[272,512]{1,0:T(8,128)S(1)} %join.8.refs_1_.refs_3_), channel_id=1, source_target_pairs={{0,16},{2,14},{4,20},{6,10},{8,24},{10,6},{12,28},{14,2},{16,0},{1... | collective-permute-start | bytes 1671176 | tf_op jit(solution)/shard_map/ppermute | solution.py:1055
  225.4 38.2 %collective-permute-start.31 = (f32[256,512]{1,0:T(8,128)S(1)}, f32[256,512]{1,0:T(8,128)S(1)}, u32[]{:S(2)}, u32[]{:S(2)}) collective-permute-start(f32[256,512]{1,0:T(8,128)S(1)} %join.9.refs_0_.refs_2_.refs_3_), channel_id=1, source_target_pairs={{0,48},{2,6},{4,52},{6,2},{8,56},{10,14},{12,60},{14,10},{16,32},{... | collective-permute-start | bytes 1572872 | tf_op jit(solution)/shard_map/ppermute | solution.py:1055
  235.8 36.1 %collective-permute-start.32 = (f32[528,512]{1,0:T(8,128)S(1)}, f32[528,512]{1,0:T(8,128)S(1)}, u32[]{:S(2)}, u32[]{:S(2)}) collective-permute-start(f32[528,512]{1,0:T(8,128)S(1)} %join.10.refs_1_.refs_2_), channel_id=1, source_target_pairs={{0,2},{2,0},{1,3},{3,1},{4,6},{6,4},{5,7},{7,5},{8,10},{10,8},{9,1... | collective-permute-start | bytes 3244040 | tf_op jit(solution)/shard_map/ppermute | solution.py:1059
  263.6 27.4 %collective-permute-start.35 = (f32[528,512]{1,0:T(8,128)S(1)}, f32[528,512]{1,0:T(8,128)S(1)}, u32[]{:S(2)}, u32[]{:S(2)}) collective-permute-start(f32[528,512]{1,0:T(8,128)S(1)} %join.10.refs_1_.refs_2_), channel_id=1, source_target_pairs={{0,4},{2,18},{4,0},{6,22},{8,12},{10,26},{12,8},{14,30},{16,20},{1... | collective-permute-start | bytes 3244040 | tf_op jit(solution)/shard_map/ppermute | solution.py:1055
  266.7 24.4 %collective-permute-start.36 = (f32[512,512]{1,0:T(8,128)}, f32[512,512]{1,0:T(8,128)}, u32[]{:S(2)}, u32[]{:S(2)}) collective-permute-start(f32[512,512]{1,0:T(8,128)} %join.11.refs_0_.refs_3_), channel_id=1, source_target_pairs={{0,12},{2,50},{4,8},{6,54},{8,4},{10,58},{12,0},{14,62},{16,28},{1... | collective-permute-start | bytes 3145736 | tf_op jit(solution)/shard_map/ppermute | solution.py:1055
  292.1 9.9 %collective-permute-start.37 = (f32[528,512]{1,0:T(8,128)}, f32[528,512]{1,0:T(8,128)S(1)}, u32[]{:S(2)}, u32[]{:S(2)}) collective-permute-start(f32[528,512]{1,0:T(8,128)} %get-tuple-element.163.refs_1_.refs_2_.refs_4_), channel_id=1, source_target_pairs={{0,2},{2,0},{1,3},{3,1},{4,6},{6,4},{5,7},{7,5},{8,10},{10,8},{9,1... | collective-permute-start | bytes 3244040 | tf_op jit(solution)/shard_map/ppermute | solution.py:1059
  292.4 11.1 %collective-permute-start.38 = (f32[512,512]{1,0:T(8,128)}, f32[512,512]{1,0:T(8,128)S(1)}, u32[]{:S(2)}, u32[]{:S(2)}) collective-permute-start(f32[512,512]{1,0:T(8,128)} %get-tuple-element.167.refs_5_), channel_id=1, source_target_pairs={{0,2},{2,0},{1,3},{3,1},{4,6},{6,4},{5,7},{7,5},{8,10},{10,8},{9,1... | collective-permute-start | bytes 3145736 | tf_op jit(solution)/shard_map/ppermute | solution.py:1059
  292.6 20.5 %collective-permute-start.39 = (f32[128,1024]{1,0:T(8,128)}, f32[128,1024]{1,0:T(8,128)S(1)}, u32[]{:S(2)}, u32[]{:S(2)}) collective-permute-start(f32[128,1024]{1,0:T(8,128)} %get-tuple-element.172.refs_4_), channel_id=1, source_target_pairs={{0,1},{1,0},{2,3},{3,2},{4,5},{5,4},{6,7},{7,6},{8,9},{9,8},{10,11... | collective-permute-start | bytes 1572872 | tf_op jit(solution)/shard_map/ppermute | solution.py:1059
  302.1 14.3 %collective-permute-start.40 = (f32[16,512]{1,0:T(8,128)S(1)}, f32[16,512]{1,0:T(8,128)S(1)}, u32[]{:S(2)}, u32[]{:S(2)}) collective-permute-start(f32[16,512]{1,0:T(8,128)S(1)} %small_sums.1.refs_1_), channel_id=1, source_target_pairs={{0,1},{1,0},{2,3},{3,2},{4,5},{5,4},{6,7},{7,6},{8,9},{9,8},{10,11... | collective-permute-start | bytes 98312 | tf_op jit(solution)/shard_map/ppermute | solution.py:1059
  (64 other events, 380.3 us)
Sparse Core Ops, SparseCore 0:
  184.3 94.1 all-gather.2
